TPU v7x, 32 devices: a whole 2x2x4 slice. The times are simulated.
32 devices in a mesh: dp: 8 (over y, x, core), mp: 4 (over z).
Axes of the slice: x: 2, y: 2, z: 4, core: 2. Of those that a mesh axis runs over, the one named last changes fastest.
Arguments:
- word_features: bfloat16 [10240, 768], P('dp'), may hold values from -6 to 6
- sentence_numbering: int32 [256, 40], P('dp'), may hold values from 0 to 1, as said below
- region_features: bfloat16 [256, 145, 1024], P('dp'), may hold values from -6 to 6
- picture_global_feature: bfloat16 [256, 1024], P('dp'), may hold values from -6 to 6
- matched_picture: int32 [256, 2], P('dp'), may hold values from 0 to 255
- sharpness_array: float32 [1], replicated, may hold values from 0.02 to 0.04
- incoming_adjoint: bfloat16 [10240, 768], P('dp'), may hold values from -6 to 6
- intra_asking_map: bfloat16 [768, 768], P(None, 'mp'), may hold values from -0.21875 to 0.21875
- intra_lookup_map: bfloat16 [768, 768], P(None, 'mp'), may hold values from -0.21875 to 0.21875
- intra_content_map: bfloat16 [768, 768], P(None, 'mp'), may hold values from -0.21875 to 0.21875
- intra_attend_exit_map: bfloat16 [768, 768], P('mp'), may hold values from -0.4375 to 0.4375
- visual_asking_map: bfloat16 [768, 768], P(None, 'mp'), may hold values from -0.21875 to 0.21875
- visual_lookup_map: bfloat16 [1024, 768], P(None, 'mp'), may hold values from -0.1875 to 0.1875
- visual_content_map: bfloat16 [1024, 768], P(None, 'mp'), may hold values from -0.1875 to 0.1875
- visual_attend_exit_map: bfloat16 [768, 768], P('mp'), may hold values from -0.75 to 0.75
- mlp_widening_factor: bfloat16 [768, 3072], P(None, 'mp'), may hold values from -0.21875 to 0.21875
- mlp_narrowing_factor: bfloat16 [3072, 768], P('mp'), may hold values from -0.109375 to 0.109375
- initial_standardize_scale: float32 [768], replicated, may hold values from 0.5 to 1.5
- initial_standardize_offset: float32 [768], replicated, may hold values from -3 to 3
- middle_standardize_scale: float32 [768], replicated, may hold values from 0.5 to 1.5
- middle_standardize_offset: float32 [768], replicated, may hold values from -3 to 3
- final_standardize_scale: float32 [768], replicated, may hold values from 0.5 to 1.5
- final_standardize_offset: float32 [768], replicated, may hold values from -3 to 3
- sentence_mapping_factor: bfloat16 [768, 256], replicated, may hold values from -0.21875 to 0.21875
- picture_mapping_factor: bfloat16 [1024, 256], replicated, may hold values from -0.1875 to 0.1875
Outputs:
- per_sentence_contrast_cost: float32 [256, 2], P('dp')
- block_exit_features: bfloat16 [10240, 768], P('dp')
- adjoint_word_features: float32 [10240, 768], P('dp')
- adjoint_region_features: bfloat16 [256, 145, 1024], P('dp')
- adjoint_picture_global: float32 [256, 1024], P('dp')
- grad_temperature: float32 [1], replicated
- grad_self_query: float32 [768, 768], P(None, 'mp')
- grad_self_key: float32 [768, 768], P(None, 'mp')
- grad_self_value: float32 [768, 768], P(None, 'mp')
- grad_self_out: float32 [768, 768], P('mp')
- grad_cross_query: float32 [768, 768], P(None, 'mp')
- grad_cross_key: float32 [1024, 768], P(None, 'mp')
- grad_cross_value: float32 [1024, 768], P(None, 'mp')
- grad_cross_out: float32 [768, 768], P('mp')
- grad_inner_up: float32 [768, 3072], P(None, 'mp')
- grad_inner_down: float32 [3072, 768], P('mp')
- grad_first_gain: float32 [768], replicated
- grad_first_shift: float32 [768], replicated
- grad_second_gain: float32 [768], replicated
- grad_second_shift: float32 [768], replicated
- grad_third_gain: float32 [768], replicated
- grad_third_shift: float32 [768], replicated
- grad_text_weight: float32 [768, 256], replicated
- grad_image_weight: float32 [1024, 256], replicated
Inputs may be any that keep to these rules, and one draw needn't show every extreme that they name: `sentence_numbering`: each row holds two captions: segments is 0 on the first one and 1 on the second one, each caption at least one token long.
All inputs are finite; a program needn't handle non-finite values.
Results may differ from a plain program's by a relative error of at most 0.025.
Values may be sent and summed in bfloat16 or wider, within the bound.
A program may use at most 192 MiB of HBM per device.

v0:
```python
from functools import partial

import jax
import jax.numpy as jnp
from jax import lax
from jax.sharding import PartitionSpec as P

HEAD = 64


LN_EPS = 1e-06
NORM_EPS = 1e-06
BIG_NEG = -1000000000.0


def layer_norm(inputs, norm_gain, norm_shift):
    center = inputs - jnp.mean(inputs, axis=-1, keepdims=True)
    spread = jnp.mean(center * center, axis=-1, keepdims=True)
    return center * lax.rsqrt(spread + LN_EPS) * norm_gain + norm_shift


def unit_rows(inputs):
    return inputs * lax.rsqrt(jnp.sum(inputs * inputs, axis=-1, keepdims=True) + NORM_EPS)


def project(left, right):
    return jnp.dot(left, right, preferred_element_type=jnp.float32)


def project_left(left, right):
    return jnp.einsum("tc,td->cd", left, right, preferred_element_type=jnp.float32)


def project_right(left, right):
    return jnp.einsum("tc,dc->td", left, right, preferred_element_type=jnp.float32)


def head_scores(queries, key_heads, mask_bias):
    plain_affinity = jnp.einsum(
        "gqhd,gkhd->ghqk", queries, key_heads, preferred_element_type=jnp.float32
    )
    return plain_affinity * 0.125 + mask_bias


def attend_forward(queries, key_heads, value_heads, mask_bias):
    scores = head_scores(queries, key_heads, mask_bias)
    row_top = jnp.max(scores, axis=-1, keepdims=True)
    shifted = jnp.exp(scores - row_top)
    row_total = jnp.sum(shifted, axis=-1, keepdims=True)
    weights = (shifted / row_total).astype(jnp.bfloat16)
    context = jnp.einsum(
        "ghqk,gkhd->gqhd", weights, value_heads, preferred_element_type=jnp.float32
    )
    return (context.astype(jnp.bfloat16), row_top + jnp.log(row_total))


def attend_backward(queries, key_heads, value_heads, mask_bias, log_total, grad_context):
    scores = head_scores(queries, key_heads, mask_bias)
    probs = jnp.exp(scores - log_total)
    weights = probs.astype(jnp.bfloat16)
    grad_weights = jnp.einsum(
        "gqhd,gkhd->ghqk", grad_context, value_heads, preferred_element_type=jnp.float32
    )
    grad_values = jnp.einsum(
        "ghqk,gqhd->gkhd", weights, grad_context, preferred_element_type=jnp.float32
    )
    grad_scores = probs * (grad_weights - jnp.sum(grad_weights * probs, axis=-1, keepdims=True))
    adjoint_plain = (grad_scores * 0.125).astype(jnp.bfloat16)
    grad_queries = jnp.einsum(
        "ghqk,gkhd->gqhd", adjoint_plain, key_heads, preferred_element_type=jnp.float32
    )
    grad_keys = jnp.einsum(
        "ghqk,gqhd->gkhd", adjoint_plain, queries, preferred_element_type=jnp.float32
    )
    return (
        grad_queries.astype(jnp.bfloat16),
        grad_keys.astype(jnp.bfloat16),
        grad_values.astype(jnp.bfloat16),
    )


def body(
    word_features,
    sentence_numbering,
    region_features,
    picture_global_feature,
    matched_picture,
    sharpness_array,
    incoming_adjoint,
    intra_asking_map,
    intra_lookup_map,
    intra_content_map,
    intra_attend_exit_map,
    visual_asking_map,
    visual_lookup_map,
    visual_content_map,
    visual_attend_exit_map,
    mlp_widening_factor,
    mlp_narrowing_factor,
    initial_standardize_scale,
    initial_standardize_offset,
    middle_standardize_scale,
    middle_standardize_offset,
    final_standardize_scale,
    final_standardize_offset,
    sentence_mapping_factor,
    picture_mapping_factor,
):
    rows_here, length = sentence_numbering.shape
    model_width = word_features.shape[1]
    heads_here = intra_asking_map.shape[1] // HEAD
    patch_count = region_features.shape[1]
    vision = region_features.shape[2]
    local_width = heads_here * HEAD

    def split_heads(tensor, how_many):
        return tensor.reshape(rows_here, how_many, heads_here, HEAD)

    def merge_heads(tensor):
        return tensor.reshape(-1, local_width)

    same_doc = sentence_numbering[:, :, None] == sentence_numbering[:, None, :]
    self_bias = jnp.where(same_doc, 0.0, BIG_NEG).astype(jnp.float32)[:, None, :, :]
    queries = split_heads(project(word_features, intra_asking_map).astype(jnp.bfloat16), length)
    key_heads = split_heads(project(word_features, intra_lookup_map).astype(jnp.bfloat16), length)
    value_heads = split_heads(
        project(word_features, intra_content_map).astype(jnp.bfloat16), length
    )
    context, self_lse = attend_forward(queries, key_heads, value_heads, self_bias)
    context_flat = merge_heads(context)
    attn_out = lax.psum(project(context_flat, intra_attend_exit_map), "mp")
    first_in = word_features.astype(jnp.float32) + attn_out
    hidden_one = layer_norm(first_in, initial_standardize_scale, initial_standardize_offset)
    hidden_one_low = hidden_one.astype(jnp.bfloat16)
    cross_q = split_heads(project(hidden_one_low, visual_asking_map).astype(jnp.bfloat16), length)
    flat_patches = region_features.reshape(rows_here * patch_count, vision)
    cross_k = split_heads(
        project(flat_patches, visual_lookup_map).astype(jnp.bfloat16), patch_count
    )
    cross_v = split_heads(
        project(flat_patches, visual_content_map).astype(jnp.bfloat16), patch_count
    )
    cross_ctx, cross_lse = attend_forward(cross_q, cross_k, cross_v, 0.0)
    cross_flat = merge_heads(cross_ctx)
    cross_add = lax.psum(project(cross_flat, visual_attend_exit_map), "mp")
    second_in = hidden_one + cross_add
    hidden_two = layer_norm(second_in, middle_standardize_scale, middle_standardize_offset)
    hidden_two_low = hidden_two.astype(jnp.bfloat16)
    inner_pre = project(hidden_two_low, mlp_widening_factor)
    activated = jax.nn.gelu(inner_pre, approximate=False).astype(jnp.bfloat16)
    inner_add = lax.psum(
        project(activated, mlp_narrowing_factor).astype(jnp.bfloat16), "mp"
    ).astype(jnp.float32)
    third_in = hidden_two + inner_add
    block_exit_features = layer_norm(third_in, final_standardize_scale, final_standardize_offset)
    position = jnp.arange(length, dtype=jnp.int32)
    split_at = length - jnp.sum(sentence_numbering, axis=1)
    starts = jnp.stack([jnp.zeros_like(split_at), split_at], axis=1)
    leader_mask = (position[None, None, :] == starts[:, :, None]).astype(jnp.float32)
    out_rows = block_exit_features.reshape(rows_here, length, model_width)
    leading = jnp.sum(leader_mask[:, :, :, None] * out_rows[:, None, :, :], axis=2).reshape(
        rows_here * 2, model_width
    )
    leading_low = leading.astype(jnp.bfloat16)
    text_raw = project(leading_low, sentence_mapping_factor)
    text_low = unit_rows(text_raw).astype(jnp.bfloat16)
    image_raw = project(picture_global_feature, picture_mapping_factor)
    image_low = unit_rows(image_raw).astype(jnp.bfloat16)
    sharpness_number = sharpness_array[0]
    targets = matched_picture.reshape(-1)
    caption_count = targets.shape[0]

    def score_piece(shard_piece):
        plain_portion = jnp.einsum(
            "se,ie->si", text_low, shard_piece, preferred_element_type=jnp.float32
        )
        affinity_portion = plain_portion / sharpness_number
        columns = jnp.arange(shard_piece.shape[0], dtype=jnp.int32)
        target_hit = (columns[None, :] == targets[:, None]).astype(jnp.float32)
        return (affinity_portion, target_hit)

    row_top = jnp.full((caption_count,), -1e30, jnp.float32)
    affinity_portion, target_hit = score_piece(lax.all_gather(image_low, "dp", axis=0, tiled=True))
    new_top = jnp.maximum(row_top, jnp.max(affinity_portion, axis=1))
    row_total = jnp.sum(jnp.exp(affinity_portion - new_top[:, None]), axis=1)
    chosen = jnp.sum(target_hit * affinity_portion, axis=1)
    row_top, row_total, chosen = (new_top, row_total, chosen)
    log_flat = row_top + jnp.log(row_total)
    per_sentence_contrast_cost = log_flat - chosen
    shard_piece = lax.all_gather(image_low, "dp", axis=0, tiled=True)
    sharpness_running = jnp.zeros((), jnp.float32)
    affinity_portion, target_hit = score_piece(shard_piece)
    adjoint_affinity = jnp.exp(affinity_portion - log_flat[:, None]) - target_hit
    adjoint_plain = (adjoint_affinity / sharpness_number).astype(jnp.bfloat16)
    grad_acc = jnp.einsum(
        "si,ie->se", adjoint_plain, shard_piece, preferred_element_type=jnp.float32
    )
    sharpness_addend = (
        sharpness_running - jnp.sum(adjoint_affinity * affinity_portion) / sharpness_number
    )
    my_first = lax.axis_index("dp") * rows_here
    my_columns = my_first + jnp.arange(rows_here, dtype=jnp.int32)
    text_piece = lax.all_gather(text_low.astype(jnp.float32), "dp", axis=0, tiled=True)
    lse_piece = lax.all_gather(log_flat, "dp", axis=0, tiled=True)
    target_piece = lax.all_gather(targets, "dp", axis=0, tiled=True)
    text_piece_low = text_piece.astype(jnp.bfloat16)
    plain_portion = jnp.einsum(
        "se,ie->si", text_piece_low, image_low, preferred_element_type=jnp.float32
    )
    affinity_portion = plain_portion / sharpness_number
    target_hit = (my_columns[None, :] == target_piece[:, None]).astype(jnp.float32)
    adjoint_affinity = jnp.exp(affinity_portion - lse_piece[:, None]) - target_hit
    adjoint_plain = (adjoint_affinity / sharpness_number).astype(jnp.bfloat16)
    adjoint_picture_features = jnp.einsum(
        "si,se->ie", adjoint_plain, text_piece_low, preferred_element_type=jnp.float32
    )
    unused, text_pull = jax.vjp(unit_rows, text_raw)
    grad_text_raw = text_pull(grad_acc)[0].astype(jnp.bfloat16)
    grad_text_weight = project_left(leading_low, grad_text_raw)
    grad_leading = project_right(grad_text_raw, sentence_mapping_factor)
    unused, image_pull = jax.vjp(unit_rows, image_raw)
    grad_image_raw = image_pull(adjoint_picture_features)[0].astype(jnp.bfloat16)
    grad_image_weight = project_left(picture_global_feature, grad_image_raw)
    adjoint_picture_global = project_right(grad_image_raw, picture_mapping_factor)
    placed = jnp.sum(
        leader_mask[:, :, :, None] * grad_leading.reshape(rows_here, 2, 1, model_width), axis=1
    )
    grad_out = incoming_adjoint.astype(jnp.float32) + placed.reshape(
        rows_here * length, model_width
    )
    unused, third_pull = jax.vjp(
        layer_norm, third_in, final_standardize_scale, final_standardize_offset
    )
    grad_third, grad_gain_three, grad_shift_three = third_pull(grad_out)
    grad_inner_add = grad_third.astype(jnp.bfloat16)
    grad_down = project_left(activated, grad_inner_add)
    grad_activated = project_right(grad_inner_add, mlp_narrowing_factor)
    unused, gelu_pull = jax.vjp(partial(jax.nn.gelu, approximate=False), inner_pre)
    grad_inner = gelu_pull(grad_activated)[0].astype(jnp.bfloat16)
    grad_up = project_left(hidden_two_low, grad_inner)
    grad_hidden_two = (
        lax.psum(project_right(grad_inner, mlp_widening_factor).astype(jnp.bfloat16), "mp").astype(
            jnp.float32
        )
        + grad_third
    )
    unused, second_pull = jax.vjp(
        layer_norm, second_in, middle_standardize_scale, middle_standardize_offset
    )
    grad_second, grad_gain_two, grad_shift_two = second_pull(grad_hidden_two)
    grad_cross_add = grad_second.astype(jnp.bfloat16)
    grad_cross_out = project_left(cross_flat, grad_cross_add)
    grad_cross_ctx = project_right(grad_cross_add, visual_attend_exit_map).astype(jnp.bfloat16)
    grad_cq, grad_ck, grad_cv = attend_backward(
        cross_q, cross_k, cross_v, 0.0, cross_lse, split_heads(grad_cross_ctx, length)
    )
    grad_cq_flat = merge_heads(grad_cq)
    grad_ck_flat = merge_heads(grad_ck)
    grad_cv_flat = merge_heads(grad_cv)
    grad_cross_query = project_left(hidden_one_low, grad_cq_flat)
    grad_cross_key = project_left(flat_patches, grad_ck_flat)
    grad_cross_value = project_left(flat_patches, grad_cv_flat)
    part_hidden = project_right(grad_cq_flat, visual_asking_map)
    part_patch = project_right(grad_ck_flat, visual_lookup_map) + project_right(
        grad_cv_flat, visual_content_map
    )
    sum_hidden, sum_patch = (
        lax.psum(part_hidden.astype(jnp.bfloat16), "mp").astype(jnp.float32),
        lax.psum(part_patch.astype(jnp.bfloat16), "mp").astype(jnp.float32),
    )
    adjoint_region_features = sum_patch.astype(jnp.bfloat16).reshape(rows_here, patch_count, vision)
    grad_hidden_one = sum_hidden + grad_second
    sharpness_addend = sharpness_addend.reshape(1)
    unused, first_pull = jax.vjp(
        layer_norm, first_in, initial_standardize_scale, initial_standardize_offset
    )
    grad_first, grad_gain_one, grad_shift_one = first_pull(grad_hidden_one)
    grad_attn = grad_first.astype(jnp.bfloat16)
    grad_self_out = project_left(context_flat, grad_attn)
    grad_context = project_right(grad_attn, intra_attend_exit_map).astype(jnp.bfloat16)
    grad_sq, grad_sk, grad_sv = attend_backward(
        queries, key_heads, value_heads, self_bias, self_lse, split_heads(grad_context, length)
    )
    grad_sq_flat = merge_heads(grad_sq)
    grad_sk_flat = merge_heads(grad_sk)
    grad_sv_flat = merge_heads(grad_sv)
    grad_self_query = project_left(word_features, grad_sq_flat)
    grad_self_key = project_left(word_features, grad_sk_flat)
    grad_self_value = project_left(word_features, grad_sv_flat)
    part_tokens = (
        project_right(grad_sq_flat, intra_asking_map)
        + project_right(grad_sk_flat, intra_lookup_map)
        + project_right(grad_sv_flat, intra_content_map)
    )
    adjoint_word_features = (
        lax.psum(part_tokens.astype(jnp.bfloat16), "mp").astype(jnp.float32) + grad_first
    )
    (
        grad_self_query,
        grad_self_key,
        grad_self_value,
        grad_self_out,
        grad_gain_one,
        grad_shift_one,
        grad_cross_query,
        grad_cross_key,
        grad_cross_value,
        grad_cross_out,
        grad_up,
        grad_down,
        grad_gain_two,
        grad_shift_two,
        grad_gain_three,
        grad_shift_three,
        grad_text_weight,
        grad_image_weight,
        sharpness_addend,
    ) = (
        lax.psum(grad_self_query.astype(jnp.bfloat16), "dp").astype(jnp.float32),
        lax.psum(grad_self_key.astype(jnp.bfloat16), "dp").astype(jnp.float32),
        lax.psum(grad_self_value.astype(jnp.bfloat16), "dp").astype(jnp.float32),
        lax.psum(grad_self_out.astype(jnp.bfloat16), "dp").astype(jnp.float32),
        lax.psum(grad_gain_one.astype(jnp.bfloat16), "dp").astype(jnp.float32),
        lax.psum(grad_shift_one.astype(jnp.bfloat16), "dp").astype(jnp.float32),
        lax.psum(grad_cross_query.astype(jnp.bfloat16), "dp").astype(jnp.float32),
        lax.psum(grad_cross_key.astype(jnp.bfloat16), "dp").astype(jnp.float32),
        lax.psum(grad_cross_value.astype(jnp.bfloat16), "dp").astype(jnp.float32),
        lax.psum(grad_cross_out.astype(jnp.bfloat16), "dp").astype(jnp.float32),
        lax.psum(grad_up.astype(jnp.bfloat16), "dp").astype(jnp.float32),
        lax.psum(grad_down.astype(jnp.bfloat16), "dp").astype(jnp.float32),
        lax.psum(grad_gain_two.astype(jnp.bfloat16), "dp").astype(jnp.float32),
        lax.psum(grad_shift_two.astype(jnp.bfloat16), "dp").astype(jnp.float32),
        lax.psum(grad_gain_three.astype(jnp.bfloat16), "dp").astype(jnp.float32),
        lax.psum(grad_shift_three.astype(jnp.bfloat16), "dp").astype(jnp.float32),
        lax.psum(grad_text_weight.astype(jnp.bfloat16), "dp").astype(jnp.float32),
        lax.psum(grad_image_weight.astype(jnp.bfloat16), "dp").astype(jnp.float32),
        lax.psum(sharpness_addend.astype(jnp.bfloat16), "dp").astype(jnp.float32),
    )
    return (
        per_sentence_contrast_cost.reshape(rows_here, 2),
        block_exit_features.astype(jnp.bfloat16),
        adjoint_word_features,
        adjoint_region_features,
        adjoint_picture_global,
        sharpness_addend,
        grad_self_query,
        grad_self_key,
        grad_self_value,
        grad_self_out,
        grad_cross_query,
        grad_cross_key,
        grad_cross_value,
        grad_cross_out,
        grad_up,
        grad_down,
        grad_gain_one,
        grad_shift_one,
        grad_gain_two,
        grad_shift_two,
        grad_gain_three,
        grad_shift_three,
        grad_text_weight,
        grad_image_weight,
    )


def solution(mesh):
    in_specs = (
        P("dp", None),
        P("dp", None),
        P("dp", None, None),
        P("dp", None),
        P("dp", None),
        P(),
        P("dp", None),
        P(None, "mp"),
        P(None, "mp"),
        P(None, "mp"),
        P("mp", None),
        P(None, "mp"),
        P(None, "mp"),
        P(None, "mp"),
        P("mp", None),
        P(None, "mp"),
        P("mp", None),
        P(),
        P(),
        P(),
        P(),
        P(),
        P(),
        P(),
        P(),
    )
    out_specs = (
        P("dp", None),
        P("dp", None),
        P("dp", None),
        P("dp", None, None),
        P("dp", None),
        P(),
        P(None, "mp"),
        P(None, "mp"),
        P(None, "mp"),
        P("mp", None),
        P(None, "mp"),
        P(None, "mp"),
        P(None, "mp"),
        P("mp", None),
        P(None, "mp"),
        P("mp", None),
        P(),
        P(),
        P(),
        P(),
        P(),
        P(),
        P(),
        P(),
    )
    return jax.shard_map(body, mesh=mesh, in_specs=in_specs, out_specs=out_specs, check_vma=False)
```

profile of v0, /device:TPU:0, one launch (start us, length us, event | category | flops | bytes accessed | tf_op | source)
XLA Modules:
  0.0 1358.0 jit_solution(7584425714380018013)
XLA Ops:
  51.5 12.9 copy.119
  64.4 9.1 reshape.304
  73.6 8.3 convolution_convert_fusion
  81.9 11.1 reshape.307
  93.0 8.2 convolution_convert_fusion.1
  101.2 11.2 reshape.305
  112.4 88.3 %all-reduce.14.cloned.1.call-done = f32[1280,768]{1,0:T(8,128)} async-done(((f32[1280,768]{1,0:T(8,128)}), f32[1280,768]{1,0:T(8,128)}) %all-reduce.14.cloned.1.call-update) | async-done | bytes 3932176 | tf_op jit(solution)/shard_map/psum | solution.py:131
  212.4 6.1 multiply_reduce_fusion.12
  230.7 145.6 %all-reduce.16.cloned.1.call-done = f32[1280,768]{1,0:T(8,128)} async-done(((f32[1280,768]{1,0:T(8,128)}), f32[1280,768]{1,0:T(8,128)}) %all-reduce.16.cloned.1.call-update) | async-done | bytes 3932176 | tf_op jit(solution)/shard_map/psum | solution.py:145
  382.2 10.9 multiply_convert_fusion.1
  400.3 8.6 all-reduce.2
  409.8 9.5 all_gather.13
  421.3 57.3 %all-reduce.18.cloned.1.call-done = bf16[1280,768]{1,0:T(8,128)(2,1)} async-done(((bf16[1280,768]{1,0:T(8,128)(2,1)}), bf16[1280,768]{1,0:T(8,128)(2,1)}) %all-reduce.18.cloned.1.call-update) | async-done | bytes 1966096 | tf_op jit(solution)/shard_map/psum | solution.py:151
  514.9 9.4 all_gather.14
  524.3 14.2 %all-reduce.1 = f32[512]{0:T(512)S(1)} all-reduce(f32[512]{0:T(512)S(1)} %copy-done.117), channel_id=1, replica_groups=mesh['dp'=8,'mp'=4] {'dp'}, use_global_device_ids=true, to_apply=%add.1 | all-reduce | flops 512 | bytes 4096
  548.7 47.2 %all-reduce.20.cloned.1.call-done = bf16[1280,768]{1,0:T(8,128)(2,1)} async-done(((bf16[1280,768]{1,0:T(8,128)(2,1)}), bf16[1280,768]{1,0:T(8,128)(2,1)}) %all-reduce.20.cloned.1.call-update) | async-done | bytes 1966096 | tf_op jit(solution)/shard_map/psum | solution.py:242
  612.3 7.7 fusion.16
  622.9 28.6 %fusion.69 = bf16[32,40,3,64]{3,1,2,0:T(8,128)(2,1)S(1)} fusion(f32[32,3,40,145]{3,2,1,0:T(8,128)} %fusion.16, f32[32,3,40,145]{3,2,1,0:T(8,128)} %copy-done.11, f32[32,3,40]{2,1,0:T(4,128)S(1)} %copy-done.80, bf16[32,145,3,64]{1,0,3,2:T(8,128)(2,1)} %reshape.307), kind=kOutput, calls=%fused_computation.109 | convolution fusion | flops 76531344 | bytes 6743040 | tf_op jit(solution)/shard_map/ghqk,gkhd->gqhd/dot_general | solution.py:69
  651.5 29.8 %convert_bitcast_fusion.1 = bf16[32,145,3,64]{1,3,2,0:T(8,128)(2,1)} fusion(bf16[32,40,3,64]{3,1,2,0:T(8,128)(2,1)S(1)} %copy-done.36, f32[32,3,40,145]{3,2,1,0:T(8,128)} %fusion.16, f32[32,3,40,145]{3,2,1,0:T(8,128)} %copy-done.11, f32[32,3,40]{2,1,0:T(4,128)S(1)} %copy-done.80), kind=kOutput, calls=%fused_computation.66 | convolution fusion | flops 77176464 | bytes 6743040 | tf_op jit(solution)/shard_map/ghqk,gqhd->gkhd/dot_general | solution.py:72
  691.3 6.6 reshape.317
  703.3 5.6 reshape.316
  713.1 6.7 fusion.88
  719.8 6.6 fusion.87
  726.4 39.2 %all-reduce.22.cloned.1.call-done = bf16[1280,768]{1,0:T(8,128)(2,1)} async-done(((bf16[1280,768]{1,0:T(8,128)(2,1)}), bf16[1280,768]{1,0:T(8,128)(2,1)}) %all-reduce.22.cloned.1.call-update) | async-done | bytes 1966096 | tf_op jit(solution)/shard_map/psum | solution.py:268
  793.3 5.5 fusion.79
  822.9 8.9 fusion.158
  831.8 11.3 add_convert_fusion
  843.1 9.0 reshape.318
  860.1 25.0 %all-reduce.3 = (bf16[1]{0:T(256)(128)(2,1)}, bf16[768]{0:T(1024)(128)(2,1)S(1)}, bf16[768]{0:T(1024)(128)(2,1)S(1)}, bf16[768]{0:T(1024)(128)(2,1)S(1)}, bf16[7...) all-reduce(bf16[1]{0:T(256)(128)(2,1)} %bitcast.13, ...), channel_id=1, replica_groups=mesh['dp'=8,'mp'=4] {'dp'}, use_global_device_ids=true, to_apply=%region_36.37 | all-reduce | flops 4609 | bytes 18436 | tf_op jit(solution)/shard_map/psum | solution.py:337
  889.4 33.3 %all-reduce.24.cloned.1.call-done = (bf16[1024,256]{0,1:T(8,128)(2,1)}, bf16[768,192]{0,1:T(8,128)(2,1)}, bf16[768,192]{0,1:T(8,128)(2,1)}, bf16[768,192]{0,1:T(...) async-done(((bf16[1024,256]{0,1:T(8,128)(2,1)}, ...) | async-done | bytes 5832720 | tf_op jit(solution)/shard_map/psum | solution.py:336
  936.5 395.3 %all-reduce.26.cloned.1.call-done = (bf16[1280,768]{1,0:T(8,128)(2,1)}, bf16[32,145,1024]{2,1,0:T(8,128)(2,1)}) async-done(((bf16[1280,768]{1,0:T(8,128)(2,1)}, bf16[32,145,1024]{2,1,0:T(8,128)(2,1)}), (bf16[1280,768]{1,0:T(8,128)(2,1)}, bf16[32,145,1024]{2,1,0:T(8,128)(2,1)})) %all-reduce.26.cloned.1.call-update) | async-done | bytes 11468816 | tf_op jit(solution)/shard_map/psum | solution.py:296
  1331.8 13.1 copy.146
  (436 shorter events, 247.7 us)
Async XLA Ops:
  7.2 375.0 %copy-start = (bf16[768,768]{1,0:T(8,128)(2,1)S(1)}, bf16[768,768]{1,0:T(8,128)(2,1)}, u32[]{:S(2)}) copy-start(bf16[768,768]{1,0:T(8,128)(2,1)} %param.40) | copy-start | bytes 3538948
  7.2 193.6 %all-reduce.14.cloned.1.call-start = ((), (), s32[]{:S(2)}) async-start(), calls=%async_computation | async-start | bytes 7864320 | tf_op jit(solution)/shard_map/psum | solution.py:131
  51.4 324.9 %all-reduce.16.cloned.1.call-start = ((), (), s32[]{:S(2)}) async-start(), calls=%async_computation.1 | async-start | bytes 7864320 | tf_op jit(solution)/shard_map/psum | solution.py:145
  204.1 172.2 %copy-start.93 = (f32[1280]{0:T(1024)}, f32[1280]{0:T(1024)S(1)}, u32[]{:S(2)}) copy-start(f32[1280]{0:T(1024)S(1)} %fusion.122) | copy-start | bytes 15364
  230.6 248.0 %all-reduce.18.cloned.1.call-start = ((), (), s32[]{:S(2)}) async-start(), calls=%async_computation.2 | async-start | bytes 3932160 | tf_op jit(solution)/shard_map/psum | solution.py:151
  381.1 97.5 %copy-start.91 = (f32[1280]{0:T(1024)}, f32[1280]{0:T(1024)S(1)}, u32[]{:S(2)}) copy-start(f32[1280]{0:T(1024)S(1)} %fusion.123) | copy-start | bytes 15364
  394.5 25.5 %copy-start.52 = (f32[32,3,40]{2,1,0:T(4,128)S(1)}, f32[32,3,40]{2,1,0:T(4,128)}, u32[]{:S(2)}) copy-start(f32[32,3,40]{2,1,0:T(4,128)} %copy-done.51) | copy-start | bytes 46084
  394.5 25.5 %copy-start.84 = (f32[32,3,40]{2,1,0:T(4,128)S(1)}, f32[32,3,40]{2,1,0:T(4,128)}, u32[]{:S(2)}) copy-start(f32[32,3,40]{2,1,0:T(4,128)} %copy-done.83) | copy-start | bytes 46084
  394.5 26.1 %copy-start.82 = (f32[32,3,40]{2,1,0:T(4,128)S(1)}, f32[32,3,40]{2,1,0:T(4,128)}, u32[]{:S(2)}) copy-start(f32[32,3,40]{2,1,0:T(4,128)} %copy-done.81) | copy-start | bytes 46084
  397.5 198.4 %all-reduce.20.cloned.1.call-start = ((), (), s32[]{:S(2)}) async-start(), calls=%async_computation.3 | async-start | bytes 3932160 | tf_op jit(solution)/shard_map/psum | solution.py:242
  409.1 73.0 %copy-start.73 = (f32[32,256]{1,0:T(8,128)}, f32[32,256]{1,0:T(8,128)S(1)}, u32[]{:S(2)}) copy-start(f32[32,256]{1,0:T(8,128)S(1)} %get-tuple-element.149) | copy-start | bytes 98308
  409.7 72.4 %copy-start.124 = (f32[32]{0:T(128)}, f32[32]{0:T(128)S(1)}, u32[]{:S(2)}) copy-start(f32[32]{0:T(128)S(1)} %add_rsqrt_fusion) | copy-start | bytes 388
  420.0 65.0 %copy-start.61 = (f32[32,2,40]{2,1,0:T(2,128)}, f32[32,2,40]{2,1,0:T(2,128)S(1)}, u32[]{:S(2)}) copy-start(f32[32,2,40]{2,1,0:T(2,128)S(1)} %compare_convert_fusion) | copy-start | bytes 30724
  511.7 26.8 %copy-start.74 = (f32[32,256]{1,0:T(8,128)S(1)}, f32[32,256]{1,0:T(8,128)}, u32[]{:S(2)}) copy-start(f32[32,256]{1,0:T(8,128)} %copy-done.73) | copy-start | bytes 98308
  511.7 26.8 %copy-start.123 = (s32[512]{0:T(512)S(1)}, s32[512]{0:T(512)}, u32[]{:S(2)}) copy-start(s32[512]{0:T(512)} %all-reduce.2) | copy-start | bytes 6148
  511.7 26.8 %copy-start.125 = (f32[32]{0:T(128)S(1)}, f32[32]{0:T(128)}, u32[]{:S(2)}) copy-start(f32[32]{0:T(128)} %copy-done.124) | copy-start | bytes 388
  511.7 26.8 %copy-start.132 = (s32[32]{0:T(128)S(1)}, s32[32]{0:T(128)}, u32[]{:S(2)}) copy-start(s32[32]{0:T(128)} %iota_add_fusion) | copy-start | bytes 388
  511.7 27.2 %copy-start.128 = (f32[32]{0:T(128)S(1)}, f32[32]{0:T(128)}, u32[]{:S(2)}) copy-start(f32[32]{0:T(128)} %copy-done.127) | copy-start | bytes 388
  511.7 27.3 %copy-start.50 = (bf16[64,768]{1,0:T(8,128)(2,1)S(1)}, bf16[64,768]{1,0:T(8,128)(2,1)}, u32[]{:S(2)}) copy-start(bf16[64,768]{1,0:T(8,128)(2,1)} %convert_element_type.348) | copy-start | bytes 294916
  511.7 27.3 %copy-start.72 = (bf16[64,256]{1,0:T(8,128)(2,1)S(1)}, bf16[64,256]{1,0:T(8,128)(2,1)}, u32[]{:S(2)}) copy-start(bf16[64,256]{1,0:T(8,128)(2,1)} %copy-done.71) | copy-start | bytes 98308
  511.7 28.3 %copy-start.88 = (bf16[32,1024]{1,0:T(8,128)(2,1)S(1)}, bf16[32,1024]{1,0:T(8,128)(2,1)}, u32[]{:S(2)}) copy-start(bf16[32,1024]{1,0:T(8,128)(2,1)} %param.28) | copy-start | bytes 196612
  514.8 26.4 %copy-start.42 = (bf16[1280,768]{1,0:T(8,128)(2,1)S(1)}, bf16[1280,768]{1,0:T(8,128)(2,1)}, u32[]{:S(2)}) copy-start(bf16[1280,768]{1,0:T(8,128)(2,1)} %copy-done.41) | copy-start | bytes 5898244
  514.8 250.8 %all-reduce.22.cloned.1.call-start = ((), (), s32[]{:S(2)}) async-start(), calls=%async_computation.4 | async-start | bytes 3932160 | tf_op jit(solution)/shard_map/psum | solution.py:268
  545.7 50.2 %copy-start.92 = (f32[1280]{0:T(1024)S(1)}, f32[1280]{0:T(1024)}, u32[]{:S(2)}) copy-start(f32[1280]{0:T(1024)} %copy-done.91) | copy-start | bytes 15364
  545.7 50.2 %copy-start.107 = (f32[768]{0:T(1024)S(1)}, f32[768]{0:T(1024)}, u32[]{:S(2)}) copy-start(f32[768]{0:T(1024)} %param.44) | copy-start | bytes 9220
  548.7 52.2 %copy-start.103 = (f32[1280]{0:T(1024)S(1)}, f32[1280]{0:T(1024)}, u32[]{:S(2)}) copy-start(f32[1280]{0:T(1024)} %copy-done.102) | copy-start | bytes 15364
  622.8 28.6 %copy-start.36 = (bf16[32,40,3,64]{3,1,2,0:T(8,128)(2,1)S(1)}, bf16[32,40,3,64]{3,1,2,0:T(8,128)(2,1)}, u32[]{:S(2)}) copy-start(bf16[32,40,3,64]{3,1,2,0:T(8,128)(2,1)} %copy.121) | copy-start | bytes 1474564
  684.5 238.2 %all-reduce.24.cloned.1.call-start = ((), (), s32[]{:S(2)}) async-start(), calls=%async_computation.5 | async-start | bytes 11665408 | tf_op jit(solution)/shard_map/psum | solution.py:336
  719.8 45.8 %copy-start.94 = (f32[1280]{0:T(1024)S(1)}, f32[1280]{0:T(1024)}, u32[]{:S(2)}) copy-start(f32[1280]{0:T(1024)} %copy-done.93) | copy-start | bytes 15364
  719.8 45.8 %copy-start.109 = (f32[768]{0:T(1024)S(1)}, f32[768]{0:T(1024)}, u32[]{:S(2)}) copy-start(f32[768]{0:T(1024)} %param.42) | copy-start | bytes 9220
  726.4 44.3 %copy-start.101 = (f32[1280]{0:T(1024)S(1)}, f32[1280]{0:T(1024)}, u32[]{:S(2)}) copy-start(f32[1280]{0:T(1024)} %copy-done.100) | copy-start | bytes 15364
  821.4 510.4 %all-reduce.26.cloned.1.call-start = ((), (), s32[]{:S(2)}) async-start(), calls=%async_computation.6 | async-start | bytes 23855104 | tf_op jit(solution)/shard_map/psum | solution.py:296
  (113 other events, 537.9 us)
Sparse Core Ops, SparseCore 0:
  51.6 149.1 all-reduce.13
  230.8 145.5 all-reduce.15
  397.6 80.9 all-reduce.17
  514.9 80.9 all-reduce.19
  684.6 80.9 all-reduce.21
  821.5 101.1 all-reduce.23
  925.9 405.8 all-reduce.25
where the time goes:
time: 1370 us; the launch traced here: 1360 us
  waiting for transfers between devices  806 us (59%)
  matrix products  217 us (16%)
  local copies, waits for them, and re-layouts  180 us (13%)
  other arithmetic  67.8 us (5%)
  blocking collectives  66.7 us (5%)
  between operations  19.8 us (1%)
    psum x1, waiting for transfers between devices, body(): lax.psum(part_tokens.astype(jnp.bfloat16), 'mp').astype(jnp.float32)  395 us
    psum x1, waiting for transfers between devices, body(): cross_add = lax.psum(project(cross_flat, visual_attend_exit_map), 'mp')  146 us
    psum x1, waiting for transfers between devices, body(): attn_out = lax.psum(project(context_flat, intra_attend_exit_map), 'mp')  88.3 us
    reshape x14, local copies, waits for them, and re-layouts, split_heads(): return tensor.reshape(rows_here, how_many, heads_here, HEAD)  62.3 us
    psum x1, waiting for transfers between devices, body(): lax.psum(project(activated, mlp_narrowing_factor).astype(jnp.bfloat16), '...  57.3 us
    unnamed x286, local copies, waits for them, and re-layouts  48.6 us
    psum x1, waiting for transfers between devices, body(): lax.psum(project_right(grad_inner, mlp_widening_factor).astype(jnp.bfloat...  47.2 us
    dot_general x12, matrix products, project(): return jnp.dot(left, right, preferred_element_type=jnp.float32)  45.5 us
  transfers between devices with their start and end apart: 7, of which 7 were waited for; matrix products, arithmetic and copies ran while one was open for 12% of the time, Pallas kernels for 0%

commit v1 on v0

v1 whole, which is shorter than its diff:
```python
from functools import partial

import jax
import jax.numpy as jnp
from jax import lax
from jax.experimental import pallas as pl
from jax.experimental.pallas import tpu as pltpu
from jax.sharding import PartitionSpec as P

HEAD = 64
GROUP = 4 * HEAD
LN_EPS = 1e-06
NORM_EPS = 1e-06
BIG_NEG = -1000000000.0
F32 = jnp.float32
BF16 = jnp.bfloat16
VMEM_LIMIT = 60 * 2**20


def dot_nn(left, right):
    return lax.dot_general(left, right, (((1,), (0,)), ((), ())), preferred_element_type=F32)


def dot_nt(left, right):
    return lax.dot_general(left, right, (((1,), (1,)), ((), ())), preferred_element_type=F32)


def dot_tn(left, right):
    return lax.dot_general(left, right, (((0,), (0,)), ((), ())), preferred_element_type=F32)


def normalize(inputs):
    center = inputs - jnp.mean(inputs, axis=-1, keepdims=True)
    rstd = lax.rsqrt(jnp.mean(center * center, axis=-1, keepdims=True) + LN_EPS)
    return center * rstd, rstd


def norm_pull(grad, xhat, rstd, gain):
    scaled = grad * gain
    first = jnp.mean(scaled, axis=-1, keepdims=True)
    second = jnp.mean(scaled * xhat, axis=-1, keepdims=True)
    grad_in = rstd * (scaled - first - xhat * second)
    return grad_in, jnp.sum(grad * xhat, axis=0, keepdims=True), jnp.sum(grad, axis=0, keepdims=True)


def unit_pull(raw, grad):
    scale = lax.rsqrt(jnp.sum(raw * raw, axis=-1, keepdims=True) + NORM_EPS)
    inner = jnp.sum(grad * raw, axis=-1, keepdims=True)
    return scale * grad - raw * (scale * scale * scale * inner)


def spread_heads(tensor):
    count = tensor.shape[0]
    left = lax.broadcasted_iota(jnp.int32, (count, 2 * HEAD), 1) < HEAD
    low, high = tensor[:, : 2 * HEAD], tensor[:, 2 * HEAD :]
    zero = jnp.zeros_like(low)
    blank = jnp.zeros((2 * count, 2 * HEAD), tensor.dtype)
    near = jnp.concatenate([jnp.where(left, low, zero), jnp.where(left, zero, low), blank], axis=0)
    far = jnp.concatenate([blank, jnp.where(left, high, zero), jnp.where(left, zero, high)], axis=0)
    return jnp.concatenate([near, far], axis=1).astype(BF16)


def collect_heads(stacked, count):
    left = lax.broadcasted_iota(jnp.int32, (count, 2 * HEAD), 1) < HEAD
    low = jnp.where(left, stacked[:count, : 2 * HEAD], stacked[count : 2 * count, : 2 * HEAD])
    high = jnp.where(
        left, stacked[2 * count : 3 * count, 2 * HEAD :], stacked[3 * count :, 2 * HEAD :]
    )
    return jnp.concatenate([low, high], axis=1)


def attend_probs(query_blocks, keys, keep):
    scores = dot_nt(keys, query_blocks)
    scores = jnp.where(keep, scores, BIG_NEG)
    top = jnp.max(scores, axis=0, keepdims=True)
    shifted = jnp.exp(scores - top)
    total = jnp.sum(shifted, axis=0, keepdims=True)
    return shifted * (1.0 / total)


def attend_forward(query, keys, values, keep):
    probs = attend_probs(spread_heads(query), keys, keep).astype(BF16)
    return collect_heads(dot_tn(probs, values), query.shape[0])


def attend_backward(query, keys, values, keep, grad_context):
    query_blocks = spread_heads(query)
    grad_blocks = spread_heads(grad_context)
    probs = attend_probs(query_blocks, keys, keep)
    grad_probs = dot_nt(values, grad_blocks)
    inner = jnp.sum(grad_probs * probs, axis=0, keepdims=True)
    grad_scores = (probs * (grad_probs - inner)).astype(BF16)
    grad_values = dot_nn(probs.astype(BF16), grad_blocks)
    grad_keys = dot_nn(grad_scores, query_blocks)
    grad_query = collect_heads(dot_tn(grad_scores, keys), query.shape[0]) * 0.125
    return grad_query, grad_keys, grad_values


def row_keep(bound, length):
    key = lax.broadcasted_iota(jnp.int32, (length, 4 * length), 0)
    query = lax.broadcasted_iota(jnp.int32, (length, 4 * length), 1) % length
    return (key >= bound) == (query >= bound)


def own_part(tensor, which, width):
    out = tensor[:, :width]
    for index in range(1, tensor.shape[1] // width):
        out = jnp.where(which == index, tensor[:, index * width : (index + 1) * width], out)
    return out


def self_forward_kernel(
    length, bound_ref, tok_ref, wqkv_ref, wout_ref, gain_ref, shift_ref, wcq_ref,
    qkv_ref, ctx_ref, xhat_ref, rstd_ref, cq_ref,
):
    width = tok_ref.shape[1]
    rows = tok_ref.shape[0] // length
    step = pl.program_id(0)
    tok = tok_ref[...]
    for part in range(3):
        proj = dot_nt(tok, wqkv_ref[part * width : (part + 1) * width, :])
        if part == 0:
            proj = proj * 0.125
        qkv_ref[:, part * width : (part + 1) * width] = proj.astype(BF16)

    def pair(index, carry):
        span = pl.ds(pl.multiple_of(index * 2 * length, 16), 2 * length)
        keeps = [row_keep(bound_ref[step * rows + 2 * index + j], length) for j in range(2)]
        for group in range(width // GROUP):
            q, k, v = (
                qkv_ref[span, part * width + group * GROUP : part * width + (group + 1) * GROUP].astype(F32)
                for part in range(3)
            )
            out = []
            for j in range(2):
                at = slice(j * length, (j + 1) * length)
                out.append(attend_forward(q[at], k[at].astype(BF16), v[at].astype(BF16), keeps[j]))
            ctx_ref[span, group * GROUP : (group + 1) * GROUP] = jnp.concatenate(out, axis=0).astype(BF16)
        return carry

    lax.fori_loop(0, rows // 2, pair, 0)
    attn = dot_nn(ctx_ref[...], wout_ref[...])
    xhat, rstd = normalize(tok.astype(F32) + attn)
    xhat_ref[...] = xhat
    rstd_ref[...] = rstd
    hidden = (xhat * gain_ref[...] + shift_ref[...]).astype(BF16)
    cq_ref[...] = (dot_nt(hidden, wcq_ref[...]) * 0.125).astype(BF16)


def cross_forward_kernel(
    patch_count, length, region_ref, wkv_ref, cq_ref, xhat1_ref, gain1_ref, shift1_ref, wout_ref,
    kv_ref, ctx_ref, xhat_ref, rstd_ref, flat_ref,
):
    images = region_ref.shape[1]
    vision = region_ref.shape[2]
    width = cq_ref.shape[1]
    padded = kv_ref.shape[1]
    whole = patch_count // 8 * 8
    flat = region_ref[...].reshape(patch_count * images, vision)

    def chunk(index, carry):
        at = pl.ds(pl.multiple_of(index * GROUP, GROUP), GROUP)
        proj = dot_nt(flat, wkv_ref[at, :])
        row = lax.broadcasted_iota(jnp.int32, (padded - whole, 128), 0)
        for half in range(GROUP // 128):
            flat_ref[half] = proj[:, half * 128 : (half + 1) * 128]
        for half in range(GROUP // 128):
            lanes = pl.ds(pl.multiple_of(index * GROUP + half * 128, 128), 128)
            for image in range(images):
                main = flat_ref[half, pl.ds(image, whole, stride=images), :]
                kv_ref[image, 0:whole, lanes] = main.astype(BF16)
                last = flat_ref[half, pl.ds(whole * images + image, 1), :]
                kv_ref[image, whole:padded, lanes] = jnp.where(row == 0, last, 0.0).astype(BF16)
        return carry

    lax.fori_loop(0, 2 * width // GROUP, chunk, 0)
    keep = lax.broadcasted_iota(jnp.int32, (padded, 4 * length), 0) < patch_count

    def pair(index, carry):
        span = pl.ds(pl.multiple_of(index * 2 * length, 16), 2 * length)
        for group in range(width // GROUP):
            lanes = slice(group * GROUP, (group + 1) * GROUP)
            q = cq_ref[span, lanes].astype(F32)
            out = []
            for j in range(2):
                image = 2 * index + j
                keys = kv_ref[image, :, lanes]
                values = kv_ref[image, :, width + group * GROUP : width + (group + 1) * GROUP]
                out.append(attend_forward(q[j * length : (j + 1) * length], keys, values, keep))
            ctx_ref[span, lanes] = jnp.concatenate(out, axis=0).astype(BF16)
        return carry

    lax.fori_loop(0, images // 2, pair, 0)
    hidden1 = xhat1_ref[...] * gain1_ref[...] + shift1_ref[...]
    xhat, rstd = normalize(hidden1 + dot_nn(ctx_ref[...], wout_ref[...]))
    xhat_ref[...] = xhat
    rstd_ref[...] = rstd


def gelu_parts(inputs):
    cdf = 0.5 * (1.0 + lax.erf(inputs * 0.7071067811865476))
    density = jnp.exp(inputs * inputs * -0.5) * 0.3989422804014327
    return inputs * cdf, cdf + inputs * density


def feed_forward_kernel(
    length, bound_ref, which_ref, temp_ref, xhat2_ref, rstd2_ref, gain2_ref, shift2_ref, gain3_ref, shift3_ref,
    wup_ref, wdown_ref, adj_ref, target_ref, images_ref, wtext_ref,
    out_ref, loss_ref, pack_ref, dr2_ref, dup_ref, ddown_ref, dgain2_ref, dshift2_ref, dgain3_ref, dshift3_ref,
    dtext_ref, dtemp_ref,
    act_ref, slope_ref, final_ref, grad_ref, lead_ref, up_acc, down_acc, text_acc,
):
    step = pl.program_id(0)
    steps = pl.num_programs(0)
    tokens, width = xhat2_ref.shape
    hidden_units = wup_ref.shape[0]
    rows = tokens // length
    chunk = min(768, hidden_units)

    @pl.when(step == 0)
    def _():
        for ref in (dgain2_ref, dshift2_ref, dgain3_ref, dshift3_ref, dtemp_ref, up_acc, down_acc, text_acc):
            ref[...] = jnp.zeros_like(ref)

    xhat2 = xhat2_ref[...]
    hidden2 = xhat2 * gain2_ref[...] + shift2_ref[...]
    low = hidden2.astype(BF16)
    final_ref[...] = hidden2

    def forward(index, carry):
        at = pl.ds(pl.multiple_of(index * chunk, chunk), chunk)
        act, slope = gelu_parts(dot_nt(low, wup_ref[at, :]))
        act = act.astype(BF16)
        act_ref[:, at] = act
        slope_ref[:, at] = slope
        final_ref[...] += dot_nn(act, wdown_ref[at, :])
        return carry

    lax.fori_loop(0, hidden_units // chunk, forward, 0)
    xhat3, rstd3 = normalize(final_ref[...])
    final = xhat3 * gain3_ref[...] + shift3_ref[...]
    out_ref[...] = final.astype(BF16)
    final_ref[...] = final
    grad_ref[...] = adj_ref[...].astype(F32)

    for row in range(rows):
        lead_ref[pl.ds(2 * row, 1), :] = final_ref[pl.ds(row * length, 1), :]
        second = row * length + bound_ref[step * rows + row]
        lead_ref[pl.ds(2 * row + 1, 1), :] = final_ref[pl.ds(second, 1), :]
    lead = lead_ref[...].astype(BF16)
    raw = dot_nn(lead, wtext_ref[...])
    text = raw * lax.rsqrt(jnp.sum(raw * raw, axis=-1, keepdims=True) + NORM_EPS)
    text_low = text.astype(BF16)
    temp = temp_ref[0]
    logits = dot_nt(text_low, images_ref[...]) / temp
    top = jnp.max(logits, axis=1, keepdims=True)
    lse = top + jnp.log(jnp.sum(jnp.exp(logits - top), axis=1, keepdims=True))
    target = target_ref[...]
    hit = lax.broadcasted_iota(jnp.int32, logits.shape, 1) == target
    loss_ref[...] = lse - jnp.sum(jnp.where(hit, logits, 0.0), axis=1, keepdims=True)
    dlogits = jnp.exp(logits - lse) - hit.astype(F32)
    dtemp_ref[...] += -jnp.sum(jnp.sum(dlogits * logits, axis=1, keepdims=True), axis=0, keepdims=True) / temp
    embed = raw.shape[1]
    lane = lax.broadcasted_iota(jnp.int32, (2 * rows, 128), 1)
    pack_ref[:, :embed] = text_low.astype(F32)
    pack_ref[:, embed:] = jnp.where(lane == 0, lse, jnp.where(lane == 1, target.astype(F32), 0.0))
    dtext = dot_nn((dlogits / temp).astype(BF16), images_ref[...])
    draw = unit_pull(raw, dtext).astype(BF16)
    text_acc[...] += dot_tn(lead, draw)
    lead_ref[...] = dot_nt(draw, wtext_ref[...])
    for row in range(rows):
        first = pl.ds(row * length, 1)
        grad_ref[first, :] += lead_ref[pl.ds(2 * row, 1), :]
        second = pl.ds(row * length + bound_ref[step * rows + row], 1)
        grad_ref[second, :] += lead_ref[pl.ds(2 * row + 1, 1), :]

    dr3, dgain3, dshift3 = norm_pull(grad_ref[...], xhat3, rstd3, gain3_ref[...])
    dgain3_ref[...] += dgain3
    dshift3_ref[...] += dshift3
    grad_ref[...] = dr3
    dfinal = dr3.astype(BF16)
    own = hidden_units // 4
    own_at = pl.ds(pl.multiple_of(which_ref[0] * own, own), own)
    down_acc[...] += dot_tn(act_ref[:, own_at], dfinal)

    def backward(index, carry):
        at = pl.ds(pl.multiple_of(index * chunk, chunk), chunk)
        dact = dot_nt(dfinal, wdown_ref[at, :])
        dinner = (dact * slope_ref[:, at]).astype(BF16)
        act_ref[:, at] = dinner
        grad_ref[...] += dot_nn(dinner, wup_ref[at, :])
        return carry

    lax.fori_loop(0, hidden_units // chunk, backward, 0)
    up_acc[...] += dot_tn(low, act_ref[:, own_at])
    dr2, dgain2, dshift2 = norm_pull(grad_ref[...], xhat2, rstd2_ref[...], gain2_ref[...])
    dgain2_ref[...] += dgain2
    dshift2_ref[...] += dshift2
    dr2_ref[...] = dr2

    @pl.when(step == steps - 1)
    def _():
        dup_ref[...] = up_acc[...].astype(BF16)
        ddown_ref[...] = down_acc[...].astype(BF16)
        dtext_ref[...] = text_acc[...].astype(BF16)


def cross_backward_kernel(
    patch_count, length, which_ref, region_ref, kv_ref, cq_ref, ctx_ref, xhat1_ref, rstd1_ref, gain1_ref, shift1_ref,
    dr2_ref, wkv_ref, wout_ref, wcq_ref,
    dregion_ref, dr1_ref, dkv_ref, dcq_ref, dout_ref, dgain_ref, dshift_ref,
    dctx_ref, dq_ref, flat_ref, stage_ref, kv_acc, cq_acc, out_acc, sem,
):
    step = pl.program_id(0)
    steps = pl.num_programs(0)
    images = region_ref.shape[1]
    vision = region_ref.shape[2]
    width = cq_ref.shape[1]
    padded = kv_ref.shape[1]
    own = width // 4
    which = which_ref[0]

    @pl.when(step == 0)
    def _():
        for ref in (dgain_ref, dshift_ref, kv_acc, cq_acc, out_acc):
            ref[...] = jnp.zeros_like(ref)

    dr2 = dr2_ref[...]
    dx = dr2.astype(BF16)
    dctx_ref[...] = dot_nt(dx, wout_ref[...]).astype(BF16)
    out_acc[...] += dot_tn(own_part(ctx_ref[...].astype(F32), which, own).astype(BF16), dx)
    keep = lax.broadcasted_iota(jnp.int32, (padded, 4 * length), 0) < patch_count
    stored = flat_ref.shape[1] // images

    def pair(index, carry):
        span = pl.ds(pl.multiple_of(index * 2 * length, 16), 2 * length)
        for group in range(width // GROUP):
            lanes = slice(group * GROUP, (group + 1) * GROUP)
            value_lanes = slice(width + group * GROUP, width + (group + 1) * GROUP)
            q = cq_ref[span, lanes].astype(F32)
            d = dctx_ref[span, lanes].astype(F32)
            out = []
            for j in range(2):
                image = 2 * index + j
                at = slice(j * length, (j + 1) * length)
                dq, dk, dv = attend_backward(
                    q[at], kv_ref[image, :, lanes], kv_ref[image, :, value_lanes], keep, d[at]
                )
                out.append(dq)
                spot = pl.ds(image, stored, stride=images)
                for half in range(2):
                    near = slice(half * 128, half * 128 + 128)
                    flat_ref[(2 * group + half), spot, :] = dk[:stored, near]
                    flat_ref[(width // 128 + 2 * group + half), spot, :] = dv[:stored, near]
            dq_ref[span, lanes] = jnp.concatenate(out, axis=0).astype(BF16)
        return carry

    lax.fori_loop(0, images // 2, pair, 0)

    pieces = 5
    patches = patch_count // pieces
    tall = patches * images
    base = step * images

    def send(index):
        slot = index % 2
        return pltpu.make_async_copy(
            stage_ref.at[slot],
            dregion_ref.at[pl.ds(index * patches, patches), pl.ds(pl.multiple_of(base, 16), images), :],
            sem.at[slot],
        )

    for index in range(pieces):
        rows = slice(index * tall, (index + 1) * tall)
        low = jnp.concatenate([flat_ref[c, rows, :].astype(BF16) for c in range(2 * width // 128)], axis=1)
        grad = dot_nn(low, wkv_ref[...])
        if index >= 2:
            send(index - 2).wait()
        stage_ref[index % 2] = grad.astype(BF16).reshape(patches, images, vision)
        send(index).start()
        region = region_ref[index * patches : (index + 1) * patches].reshape(tall, vision)
        for part in range(2):
            mine = own_part(low[:, part * width : (part + 1) * width].astype(F32), which, own).astype(BF16)
            kv_acc[part * own : (part + 1) * own, :] += dot_tn(mine, region)
    send(pieces - 2).wait()
    send(pieces - 1).wait()

    xhat1 = xhat1_ref[...]
    hidden1 = (xhat1 * gain1_ref[...] + shift1_ref[...]).astype(BF16)
    dq = dq_ref[...]
    cq_acc[...] += dot_tn(own_part(dq.astype(F32), which, own).astype(BF16), hidden1)
    dh1 = dr2 + dot_nn(dq, wcq_ref[...])
    dr1, dgain, dshift = norm_pull(dh1, xhat1, rstd1_ref[...], gain1_ref[...])
    dr1_ref[...] = dr1
    dgain_ref[...] += dgain
    dshift_ref[...] += dshift

    @pl.when(step == steps - 1)
    def _():
        dkv_ref[...] = kv_acc[...].astype(BF16)
        dcq_ref[...] = cq_acc[...].astype(BF16)
        dout_ref[...] = out_acc[...].astype(BF16)


def self_backward_kernel(
    length, bound_ref, which_ref, tok_ref, qkv_ref, ctx_ref, dr1_ref, wqkv_ref, wout_ref,
    dtok_ref, dqkv_ref, dout_ref, dctx_ref, grads_ref, qkv_acc, out_acc,
):
    step = pl.program_id(0)
    steps = pl.num_programs(0)
    tokens, width = tok_ref.shape
    rows = tokens // length
    own = width // 4
    which = which_ref[0]

    @pl.when(step == 0)
    def _():
        for ref in (qkv_acc, out_acc):
            ref[...] = jnp.zeros_like(ref)

    dr1 = dr1_ref[...]
    da = dr1.astype(BF16)
    dctx_ref[...] = dot_nt(da, wout_ref[...]).astype(BF16)
    out_acc[...] += dot_tn(own_part(ctx_ref[...].astype(F32), which, own).astype(BF16), da)

    def pair(index, carry):
        span = pl.ds(pl.multiple_of(index * 2 * length, 16), 2 * length)
        keeps = [row_keep(bound_ref[step * rows + 2 * index + j], length) for j in range(2)]
        for group in range(width // GROUP):
            q, k, v = (
                qkv_ref[span, part * width + group * GROUP : part * width + (group + 1) * GROUP].astype(F32)
                for part in range(3)
            )
            d = dctx_ref[span, group * GROUP : (group + 1) * GROUP].astype(F32)
            outs = []
            for j in range(2):
                at = slice(j * length, (j + 1) * length)
                outs.append(attend_backward(q[at], k[at].astype(BF16), v[at].astype(BF16), keeps[j], d[at]))
            for part in range(3):
                both = jnp.concatenate([outs[0][part], outs[1][part]], axis=0).astype(BF16)
                grads_ref[span, part * width + group * GROUP : part * width + (group + 1) * GROUP] = both
        return carry

    lax.fori_loop(0, rows // 2, pair, 0)
    tok = tok_ref[...]
    dtok_ref[...] = dr1 + dot_nn(grads_ref[...], wqkv_ref[...])
    for part in range(3):
        mine = own_part(grads_ref[:, part * width : (part + 1) * width].astype(F32), which, own).astype(BF16)
        qkv_acc[part * own : (part + 1) * own, :] += dot_tn(mine, tok)

    @pl.when(step == steps - 1)
    def _():
        dqkv_ref[...] = qkv_acc[...].astype(BF16)
        dout_ref[...] = out_acc[...].astype(BF16)


def image_backward_kernel(
    first_ref, temp_ref, picture_ref, weight_ref, pack_ref, dpicture_ref, dweight_ref
):
    raw = dot_nn(picture_ref[...], weight_ref[...])
    own = (raw * lax.rsqrt(jnp.sum(raw * raw, axis=-1, keepdims=True) + NORM_EPS)).astype(BF16)
    embed = raw.shape[1]
    temp = temp_ref[0]
    text = pack_ref[:, :embed].astype(BF16)
    lse = pack_ref[:, embed : embed + 1]
    target = pack_ref[:, embed + 1 : embed + 2].astype(jnp.int32)
    logits = dot_nt(text, own) / temp
    hit = lax.broadcasted_iota(jnp.int32, logits.shape, 1) + first_ref[0] == target
    dlogits = jnp.exp(logits - lse) - hit.astype(F32)
    dimage = dot_tn((dlogits / temp).astype(BF16), text)
    draw = unit_pull(raw, dimage).astype(BF16)
    dpicture_ref[...] = dot_nt(draw, weight_ref[...])
    dweight_ref[...] = dot_tn(picture_ref[...], draw).astype(BF16)


def full(shape):
    return pl.BlockSpec(shape, lambda i: (0,) * len(shape), pipeline_mode=pl.Buffered(1))


def fixed(shape):
    return pl.BlockSpec(shape, lambda i: (0,) * len(shape))


def rows_of(count, width):
    return pl.BlockSpec((count, width), lambda i: (i, 0))


def rows_once(count, width):
    return pl.BlockSpec((count, width), lambda i: (i, 0), pipeline_mode=pl.Buffered(1))


SMEM = pl.BlockSpec(memory_space=pltpu.SMEM)


def shape_of(shape, kind):
    return jax.ShapeDtypeStruct(shape, kind)


def call(kernel, steps, ins, outs, args, scratch=(), flops=0, moved=0):
    specs, shapes = zip(*outs, strict=True)
    return pl.pallas_call(
        kernel,
        grid=(steps,),
        in_specs=list(ins),
        out_specs=list(specs),
        out_shape=list(shapes),
        scratch_shapes=list(scratch),
        compiler_params=pltpu.CompilerParams(
            vmem_limit_bytes=VMEM_LIMIT, dimension_semantics=("arbitrary",)
        ),
        cost_estimate=pl.CostEstimate(flops=flops, bytes_accessed=moved, transcendentals=0),
    )(*args)


def gather_weight(shard, pieces):
    index = lax.axis_index("dp")
    count = shard.shape[0] // pieces
    piece = lax.dynamic_slice_in_dim(shard, index * count, count, 0)
    return lax.all_gather(piece, ("mp", "dp"), axis=0, tiled=True)


def body(
    dp_size,
    word_features,
    sentence_numbering,
    region_features,
    picture_global_feature,
    matched_picture,
    sharpness_array,
    incoming_adjoint,
    intra_asking_map,
    intra_lookup_map,
    intra_content_map,
    intra_attend_exit_map,
    visual_asking_map,
    visual_lookup_map,
    visual_content_map,
    visual_attend_exit_map,
    mlp_widening_factor,
    mlp_narrowing_factor,
    initial_standardize_scale,
    initial_standardize_offset,
    middle_standardize_scale,
    middle_standardize_offset,
    final_standardize_scale,
    final_standardize_offset,
    sentence_mapping_factor,
    picture_mapping_factor,
):
    rows, length = sentence_numbering.shape
    tokens, width = word_features.shape
    patch_count, vision = region_features.shape[1:]
    padded = -(-patch_count // 16) * 16
    images = 16
    embed = sentence_mapping_factor.shape[1]
    hidden_units = mlp_widening_factor.shape[1] * 4
    own = width // 4
    which = lax.axis_index("mp").astype(jnp.int32).reshape(1)
    bound = (length - jnp.sum(sentence_numbering, axis=1)).astype(jnp.int32)
    target = matched_picture.reshape(-1, 1)
    gain1, shift1, gain2, shift2, gain3, shift3 = (
        v.reshape(1, width)
        for v in (
            initial_standardize_scale, initial_standardize_offset, middle_standardize_scale,
            middle_standardize_offset, final_standardize_scale, final_standardize_offset,
        )
    )

    def gather_all(shards):
        sizes = [s.shape[0] for s in shards]
        return [gather_weight(s, dp_size) for s in shards]

    wq, wk, wv, wo = gather_all(
        [intra_asking_map.T, intra_lookup_map.T, intra_content_map.T, intra_attend_exit_map]
    )
    wqkv = jnp.concatenate([wq, wk, wv], axis=0)
    wcq, wco = gather_all([visual_asking_map.T, visual_attend_exit_map])
    wkv = jnp.concatenate(gather_all([visual_lookup_map.T, visual_content_map.T]), axis=0)
    wup, wdown = gather_all([mlp_widening_factor.T, mlp_narrowing_factor])

    image_raw = dot_nn(picture_global_feature, picture_mapping_factor)
    image_scale = lax.rsqrt(jnp.sum(image_raw * image_raw, axis=-1, keepdims=True) + NORM_EPS)
    image_all = lax.all_gather((image_raw * image_scale).astype(BF16), "dp", axis=0, tiled=True)

    token_rows = 8
    block = token_rows * length
    steps = rows // token_rows
    vec = full((1, width))
    square = full((width, width))

    qkv, ctx1, xhat1, rstd1, cq = call(
        partial(self_forward_kernel, length),
        steps,
        [SMEM, rows_of(block, width), full((3 * width, width)), square, vec, vec, square],
        [
            (rows_of(block, 3 * width), shape_of((tokens, 3 * width), BF16)),
            (rows_of(block, width), shape_of((tokens, width), BF16)),
            (rows_of(block, width), shape_of((tokens, width), F32)),
            (rows_of(block, 1), shape_of((tokens, 1), F32)),
            (rows_of(block, width), shape_of((tokens, width), BF16)),
        ],
        (bound, word_features, wqkv, wo, gain1, shift1, wcq),
        flops=10 * tokens * width * width,
        moved=20 * tokens * width,
    )

    region = jnp.transpose(region_features, (1, 0, 2))
    block2 = images * length
    region_spec = pl.BlockSpec((patch_count, images, vision), lambda i: (0, i, 0))
    kv_spec = pl.BlockSpec((images, padded, 2 * width), lambda i: (i, 0, 0))
    kv, ctx2, xhat2, rstd2 = call(
        partial(cross_forward_kernel, patch_count, length),
        rows // images,
        [
            region_spec, full((2 * width, vision)), rows_of(block2, width), rows_of(block2, width), vec, vec,
            square,
        ],
        [
            (kv_spec, shape_of((rows, padded, 2 * width), BF16)),
            (rows_of(block2, width), shape_of((tokens, width), BF16)),
            (rows_of(block2, width), shape_of((tokens, width), F32)),
            (rows_of(block2, 1), shape_of((tokens, 1), F32)),
        ],
        (region, wkv, cq, xhat1, gain1, shift1, wco),
        scratch=[pltpu.VMEM((GROUP // 128, patch_count * images, 128), F32)],
        flops=4 * rows * patch_count * width * vision,
        moved=2 * rows * padded * (vision + 2 * width),
    )

    captions = 2 * token_rows
    ff_own = hidden_units // 4
    (
        block_exit, loss, pack, dr2, dup, ddown, dgain2, dshift2, dgain3, dshift3, dtext, dtemp,
    ) = call(
        partial(feed_forward_kernel, length),
        steps,
        [
            SMEM, SMEM, SMEM, rows_of(block, width), rows_of(block, 1), vec, vec, vec, vec,
            full((hidden_units, width)), full((hidden_units, width)), rows_of(block, width), rows_of(captions, 1),
            full(image_all.shape), full((width, embed)),
        ],
        [
            (rows_of(block, width), shape_of((tokens, width), BF16)),
            (rows_of(captions, 1), shape_of((2 * rows, 1), F32)),
            (rows_of(captions, embed + 128), shape_of((2 * rows, embed + 128), F32)),
            (rows_of(block, width), shape_of((tokens, width), F32)),
            (fixed((width, ff_own)), shape_of((width, ff_own), BF16)),
            (fixed((ff_own, width)), shape_of((ff_own, width), BF16)),
            (fixed((1, width)), shape_of((1, width), F32)),
            (fixed((1, width)), shape_of((1, width), F32)),
            (fixed((1, width)), shape_of((1, width), F32)),
            (fixed((1, width)), shape_of((1, width), F32)),
            (fixed((width, embed)), shape_of((width, embed), BF16)),
            (fixed((1, 1)), shape_of((1, 1), F32)),
        ],
        (
            bound, which, sharpness_array, xhat2, rstd2, gain2, shift2, gain3, shift3, wup, wdown, incoming_adjoint, target, image_all,
            sentence_mapping_factor,
        ),
        scratch=[
            pltpu.VMEM((block, hidden_units), BF16),
            pltpu.VMEM((block, hidden_units), F32),
            pltpu.VMEM((block, width), F32),
            pltpu.VMEM((block, width), F32),
            pltpu.VMEM((captions, width), F32),
            pltpu.VMEM((width, ff_own), F32),
            pltpu.VMEM((ff_own, width), F32),
            pltpu.VMEM((width, embed), F32),
        ],
        flops=10 * tokens * width * hidden_units,
        moved=20 * tokens * width,
    )

    pack_all = lax.all_gather(pack, "dp", axis=0, tiled=True)
    dp_sum = lambda grad: lax.psum(grad, "dp")
    dup, ddown, dtext = dp_sum((dup, ddown, dtext))

    first = (lax.axis_index("dp") * rows).astype(jnp.int32).reshape(1)
    dpicture, dimage = call(
        image_backward_kernel,
        1,
        [SMEM, SMEM, full(picture_global_feature.shape), full(picture_mapping_factor.shape), full(pack_all.shape)],
        [
            (fixed((rows, vision)), shape_of((rows, vision), F32)),
            (fixed((vision, embed)), shape_of((vision, embed), BF16)),
        ],
        (first, sharpness_array, picture_global_feature, picture_mapping_factor, pack_all),
    )

    dregion, dr1, dkv, dcq, dco, dgain1, dshift1 = call(
        partial(cross_backward_kernel, patch_count, length),
        rows // images,
        [
            SMEM,
            pl.BlockSpec((patch_count, images, vision), lambda i: (0, i, 0), pipeline_mode=pl.Buffered(1)),
            pl.BlockSpec((images, padded, 2 * width), lambda i: (i, 0, 0), pipeline_mode=pl.Buffered(1)),
            rows_of(block2, width), rows_of(block2, width), rows_once(block2, width), rows_of(block2, 1), vec, vec,
            rows_once(block2, width), full((2 * width, vision)), square, square,
        ],
        [
            (pl.BlockSpec(memory_space=pl.ANY), shape_of((patch_count, rows, vision), BF16)),
            (rows_of(block2, width), shape_of((tokens, width), F32)),
            (fixed((2 * own, vision)), shape_of((2 * own, vision), BF16)),
            (fixed((own, width)), shape_of((own, width), BF16)),
            (fixed((own, width)), shape_of((own, width), BF16)),
            (fixed((1, width)), shape_of((1, width), F32)),
            (fixed((1, width)), shape_of((1, width), F32)),
        ],
        (which, region, kv, cq, ctx2, xhat1, rstd1, gain1, shift1, dr2, wkv, wco, wcq),
        scratch=[
            pltpu.VMEM((block2, width), BF16),
            pltpu.VMEM((block2, width), BF16),
            pltpu.VMEM((2 * width // 128, -(-patch_count // 8) * 8 * images, 128), F32),
            pltpu.VMEM((2, patch_count // 5, images, vision), BF16),
            pltpu.VMEM((2 * own, vision), F32),
            pltpu.VMEM((own, width), F32),
            pltpu.VMEM((own, width), F32),
            pltpu.SemaphoreType.DMA((2,)),
        ],
        flops=6 * rows * patch_count * width * vision,
        moved=2 * rows * padded * 2 * (vision + width),
    )
    dkv, dcq, dco, dimage = dp_sum((dkv, dcq, dco, dimage))

    dtok, dqkv, dso = call(
        partial(self_backward_kernel, length),
        steps,
        [
            SMEM, SMEM, rows_of(block, width), rows_of(block, 3 * width), rows_of(block, width), rows_of(block, width),
            full((3 * width, width)), square,
        ],
        [
            (rows_of(block, width), shape_of((tokens, width), F32)),
            (fixed((3 * own, width)), shape_of((3 * own, width), BF16)),
            (fixed((own, width)), shape_of((own, width), BF16)),
        ],
        (bound, which, word_features, qkv, ctx1, dr1, wqkv, wo),
        scratch=[
            pltpu.VMEM((block, width), BF16),
            pltpu.VMEM((block, 3 * width), BF16),
            pltpu.VMEM((3 * own, width), F32),
            pltpu.VMEM((own, width), F32),
        ],
        flops=10 * tokens * width * width,
        moved=20 * tokens * width,
    )
    dqkv, dso = dp_sum((dqkv, dso))
    small = jnp.concatenate(
        [dgain1, dshift1, dgain2, dshift2, dgain3, dshift3, jnp.broadcast_to(dtemp, (1, width))], axis=0
    )
    small = lax.psum(small, "dp")

    return (
        loss.reshape(rows, 2),
        block_exit,
        dtok,
        jnp.transpose(dregion, (1, 0, 2)),
        dpicture,
        small[6, :1],
        dqkv[:own].astype(F32).T,
        dqkv[own : 2 * own].astype(F32).T,
        dqkv[2 * own :].astype(F32).T,
        dso.astype(F32),
        dcq.astype(F32).T,
        dkv[:own].astype(F32).T,
        dkv[own:].astype(F32).T,
        dco.astype(F32),
        dup.astype(F32),
        ddown.astype(F32),
        small[0],
        small[1],
        small[2],
        small[3],
        small[4],
        small[5],
        dtext.astype(F32),
        dimage.astype(F32),
    )


def solution(mesh):
    rows = P("dp", None)
    by_column = P(None, "mp")
    by_row = P("mp", None)
    in_specs = (
        rows, rows, P("dp", None, None), rows, rows, P(), rows,
        by_column, by_column, by_column, by_row, by_column, by_column, by_column, by_row, by_column, by_row,
        P(), P(), P(), P(), P(), P(), P(), P(),
    )
    out_specs = (
        rows, rows, rows, P("dp", None, None), rows, P(),
        by_column, by_column, by_column, by_row, by_column, by_column, by_column, by_row, by_column, by_row,
        P(), P(), P(), P(), P(), P(), P(), P(),
    )
    return jax.shard_map(
        partial(body, mesh.shape["dp"]), mesh=mesh, in_specs=in_specs, out_specs=out_specs, check_vma=False
    )
```

time: 1370 us -> 936 us (0.68)
  Pallas kernels: 0 us -> 288 us
  waiting for transfers between devices: 806 us -> 529 us
  matrix products: 217 us -> 0.3 us
  local copies, waits for them, and re-layouts: 180 us -> 34.1 us
  other arithmetic: 67.8 us -> 12.3 us
  blocking collectives: 66.7 us -> 48.4 us
    psum x7 -> x1, waiting for transfers between devices: 806 us -> 72.2 us  [body(): dp_sum = lambda grad: lax.psum(grad, 'dp')]
    all_gather x0 -> x10, waiting for transfers between devices: none -> 457 us  [gather_weight(): return lax.all_gather(piece, ('mp', 'dp'), axis=0, tiled=True)]
    pallas_call x0 -> x6, Pallas kernels: none -> 288 us  [call(): pl.pallas_call(kernel, grid=(steps,), in_specs=list(ins), out_specs=list(...]
    dot_general x51 -> x1, matrix products: 217 us -> 0.3 us  [dot_nn(): lax.dot_general(left, right, (((1,), (0,)), ((), ())), preferred_element_...]
    reshape x24 -> x8, local copies, waits for them, and re-layouts: 107 us -> 4.28 us  [the longest x6 3.48 us: body(): v.reshape(1, width)]
    reduce_sum x19 -> x1, other arithmetic: 39.3 us -> 0.11 us  [body(): bound = (length - jnp.sum(sentence_numbering, axis=1)).astype(jnp.int32)]
    unnamed x286 -> x60, local copies, waits for them, and re-layouts: 48.6 us -> 9.79 us
    convert_element_type x9 -> x0, local copies, waits for them, and re-layouts: 23.3 us -> none  [the longest x2 8.16 us: attend_backward(): grad_keys.astype(jnp.bfloat16)]
  transfers between devices with their start and end apart: 7 -> 11, of which waited for: 7 -> 11; matrix products, arithmetic and copies ran while one was open for 12% -> 4% of each run, Pallas kernels for 0% -> 9%
where the time goes in v1:
time: 936 us; the launch traced here: 928 us
  waiting for transfers between devices  529 us (57%)
  Pallas kernels  288 us (31%)
  blocking collectives  48.4 us (5%)
  local copies, waits for them, and re-layouts  34.1 us (4%)
  between operations  15.3 us (2%)
  other arithmetic  12.3 us (1%)
    all_gather x10, waiting for transfers between devices, gather_weight(): return lax.all_gather(piece, ('mp', 'dp'), axis=0, tiled=True)  457 us
    pallas_call x6, Pallas kernels, call(): pl.pallas_call(kernel, grid=(steps,), in_specs=list(ins), out_specs=list(...  288 us
    psum x1, waiting for transfers between devices, body(): dp_sum = lambda grad: lax.psum(grad, 'dp')  72.2 us
    psum x1, blocking collectives, body(): small = lax.psum(small, 'dp')  25 us
  transfers between devices with their start and end apart: 11, of which 11 were waited for; matrix products, arithmetic and copies ran while one was open for 4% of the time, Pallas kernels for 9%

profile of v1, /device:TPU:0, one launch (start us, length us, event | category | flops | bytes accessed | tf_op | source)
XLA Modules:
  0.0 927.8 jit_solution(2001982170525852263)
XLA Ops:
  7.4 1.5 dynamic-slice_bitcast_fusion.5
  14.8 1.4 dynamic-slice_bitcast_fusion.1
  16.3 1.4 dynamic-slice_bitcast_fusion
  20.3 1.6 constant_dynamic-slice_fusion
  27.4 11.7 %all_gather.46.images_ref = bf16[256,256]{1,0:T(8,128)(2,1)} all-gather(bf16[32,256]{1,0:T(8,128)(2,1)S(1)} %multiply_convert_fusion), channel_id=1, replica_groups=mesh['dp'=8,'mp'=4] {'dp'}, dimensions={0}, use_global_device_ids=true | all-gather | bytes 147456 | tf_op jit(solution)/shard_map/all_gather | solution.py:583
  39.6 28.8 %all-gather.15.cloned.1.call-done = bf16[768,768]{1,0:T(8,128)(2,1)} async-done(((bf16[24,768]{1,0:T(8,128)(2,1)}), bf16[768,768]{1,0:T(8,128)(2,1)}) %all-gather.15.cloned.1.call-update) | async-done | bytes 1179664 | tf_op jit(solution)/shard_map/all_gather | solution.py:519
  68.4 2.4 constant_dynamic-update-slice_fusion.4
  70.8 54.1 %all-gather.17.cloned.1.call-done = bf16[768,768]{1,0:T(8,128)(2,1)} async-done(((bf16[24,768]{1,0:T(8,128)(2,1)}), bf16[768,768]{1,0:T(8,128)(2,1)}) %all-gather.17.cloned.1.call-update) | async-done | bytes 1179664 | tf_op jit(solution)/shard_map/all_gather | solution.py:519
  124.9 2.4 constant_dynamic-update-slice_fusion.3
  127.3 54.1 %all-gather.19.cloned.1.call-done = bf16[768,768]{1,0:T(8,128)(2,1)} async-done(((bf16[24,768]{1,0:T(8,128)(2,1)}), bf16[768,768]{1,0:T(8,128)(2,1)}) %all-gather.19.cloned.1.call-update) | async-done | bytes 1179664 | tf_op jit(solution)/shard_map/all_gather | solution.py:519
  181.3 2.4 constant_dynamic-update-slice_fusion.2.wqkv_ref
  183.7 53.9 %all-gather.21.cloned.1.call-done.wout_ref = bf16[768,768]{1,0:T(8,128)(2,1)} async-done(((bf16[24,768]{1,0:T(8,128)(2,1)}), bf16[768,768]{1,0:T(8,128)(2,1)}) %all-gather.21.cloned.1.call-update) | async-done | bytes 1179664 | tf_op jit(solution)/shard_map/all_gather | solution.py:519
  237.7 56.3 %all-gather.23.cloned.1.call-done.wcq_ref = bf16[768,768]{1,0:T(8,128)(2,1)} async-done(((bf16[24,768]{1,0:T(8,128)(2,1)}), bf16[768,768]{1,0:T(8,128)(2,1)}) %all-gather.23.cloned.1.call-update) | async-done | bytes 1179664 | tf_op jit(solution)/shard_map/all_gather | solution.py:519
  294.0 35.8 %shard_map.424 = (bf16[1280,2304]{1,0:T(8,128)(2,1)}, bf16[1280,768]{1,0:T(8,128)(2,1)}, f32[1280,768]{1,0:T(8,128)}, f32[1280,1]{1,0:T(8,128)}, bf16[1280,768]{1,0:T(8,128)(2,1)}) custom-call(s32[32]{0:T(128)} %broadcast_subtract_fusion.bound_ref, bf16[1280,768]{1,0:T(8,128)(2,1)} %tok_ref.3, ...), custom_call_target="tpu_custom_call" | custom-call | flops 7549747200 | bytes 19660800 | tf_op jit(solution)/shard_map/pallas_call | solution.py:501
  329.8 21.6 %all-gather.11.cloned.1.call-done = bf16[768,1024]{1,0:T(8,128)(2,1)} async-done(((bf16[24,1024]{1,0:T(8,128)(2,1)}), bf16[768,1024]{1,0:T(8,128)(2,1)}) %all-gather.11.cloned.1.call-update) | async-done | bytes 1572880 | tf_op jit(solution)/shard_map/all_gather | solution.py:519
  351.4 2.7 constant_dynamic-update-slice_fusion.1
  354.1 54.6 %all-gather.13.cloned.1.call-done = bf16[768,1024]{1,0:T(8,128)(2,1)} async-done(((bf16[24,1024]{1,0:T(8,128)(2,1)}), bf16[768,1024]{1,0:T(8,128)(2,1)}) %all-gather.13.cloned.1.call-update) | async-done | bytes 1572880 | tf_op jit(solution)/shard_map/all_gather | solution.py:519
  408.7 2.7 constant_dynamic-update-slice_fusion.wkv_ref
  411.5 53.7 %all-gather.25.cloned.1.call-done.wout_ref = bf16[768,768]{1,0:T(8,128)(2,1)} async-done(((bf16[24,768]{1,0:T(8,128)(2,1)}), bf16[768,768]{1,0:T(8,128)(2,1)}) %all-gather.25.cloned.1.call-update) | async-done | bytes 1179664 | tf_op jit(solution)/shard_map/all_gather | solution.py:519
  465.2 52.3 %shard_map.425 = (bf16[32,160,1536]{2,1,0:T(8,128)(2,1)}, bf16[1280,768]{1,0:T(8,128)(2,1)}, f32[1280,768]{1,0:T(8,128)}, f32[1280,1]{1,0:T(8,128)}) custom-call(bf16[145,32,1024]{2,1,0:T(8,128)(2,1)} %bitcast.34, bf16[1536,1024]{1,0:T(8,128)(2,1)} %constant_dynamic-update-slice_fusion.wkv_ref, bf16[1280,768]{1,0:T(8,128)(2,1)} %get-tuple-element.57.cq_ref, ...), custom_call_target="tpu_custom_call" | custom-call | flops 14596177920 | bytes 26214400 | tf_op jit(solution)/shard_map/pallas_call | solution.py:501
  517.4 13.9 %all-gather.27.cloned.1.call-done.wup_ref = bf16[3072,768]{1,0:T(8,128)(2,1)} async-done(((bf16[96,768]{1,0:T(8,128)(2,1)}), bf16[3072,768]{1,0:T(8,128)(2,1)}) %all-gather.27.cloned.1.call-update) | async-done | bytes 4718608 | tf_op jit(solution)/shard_map/all_gather | solution.py:519
  531.4 65.9 %all-gather.29.cloned.1.call-done.wdown_ref = bf16[3072,768]{1,0:T(8,128)(2,1)} async-done(((bf16[96,768]{1,0:T(8,128)(2,1)}), bf16[3072,768]{1,0:T(8,128)(2,1)}) %all-gather.29.cloned.1.call-update) | async-done | bytes 4718608 | tf_op jit(solution)/shard_map/all_gather | solution.py:519
  597.2 62.5 %shard_map.426 = (bf16[1280,768]{1,0:T(8,128)(2,1)}, f32[64,1]{1,0:T(8,128)}, f32[64,384]{1,0:T(8,128)}, f32[1280,768]{1,0:T(8,128)}, bf16[768,768]{1,0:T(8,128)...) custom-call(s32[32]{0:T(128)} %broadcast_subtract_fusion.bound_ref, ...), custom_call_target="tpu_custom_call" | custom-call | flops 30198988800 | bytes 19660800 | tf_op jit(solution)/shard_map/pallas_call | solution.py:501
  659.7 11.6 %all_gather.47.pack_ref = f32[512,384]{1,0:T(8,128)} all-gather(f32[64,384]{1,0:T(8,128)} %get-tuple-element.72), channel_id=1, replica_groups=mesh['dp'=8,'mp'=4] {'dp'}, dimensions={0}, use_global_device_ids=true | all-gather | bytes 884736 | tf_op jit(solution)/shard_map/all_gather | solution.py:674
  671.3 3.3 shard_map.429
  674.6 91.3 %shard_map.427 = (bf16[145,32,1024]{2,1,0:T(8,128)(2,1)}, f32[1280,768]{1,0:T(8,128)}, bf16[384,1024]{1,0:T(8,128)(2,1)}, bf16[192,768]{1,0:T(8,128)(2,1)}, bf16...) custom-call(s32[1]{0:T(128)} %bitcast.which_ref, bf16[145,32,1024]{2,1,0:T(8,128)(2,1)} %bitcast.35, ...), custom_call_target="tpu_custom_call" | custom-call | flops 21894266880 | bytes 36700160 | tf_op jit(solution)/shard_map/pallas_call | solution.py:501
  765.9 42.5 %shard_map.428 = (f32[1280,768]{1,0:T(8,128)}, bf16[576,768]{1,0:T(8,128)(2,1)}, bf16[192,768]{1,0:T(8,128)(2,1)}) custom-call(s32[32]{0:T(128)} %broadcast_subtract_fusion.bound_ref, s32[1]{0:T(128)} %bitcast.which_ref, bf16[1280,768]{1,0:T(8,128)(2,1)} %tok_ref.3, bf16[1280,2304]{1,0:T(8,128)(2,1)} %get-tuple-element.63.qkv_ref, ...), custom_call_target="tpu_custom_call" | custom-call | flops 7549747200 | bytes 19660800 | tf_op jit(solution)/shard_map/pallas_call | solution.py:501
  810.8 25.0 %psum.70 = f32[7,768]{1,0:T(8,128)S(1)} all-reduce(f32[7,768]{1,0:T(8,128)S(1)} %concatenate.11), channel_id=1, replica_groups=mesh['dp'=8,'mp'=4] {'dp'}, use_global_device_ids=true, to_apply=%region_2.0 | all-reduce | flops 5376 | bytes 43008 | tf_op jit(solution)/shard_map/psum | solution.py:751
  837.0 72.2 %all-reduce.3.cloned.1.call-done = (bf16[576,768]{1,0:T(8,128)(2,1)}, bf16[192,768]{1,0:T(8,128)(2,1)}, bf16[768,192]{0,1:T(8,128)(2,1)}, bf16[384,1024]{1,0:T(8...) async-done(((bf16[576,768]{1,0:T(8,128)(2,1)}, ...) | async-done | bytes 5832720 | tf_op jit(solution)/shard_map/psum | solution.py:675
  909.2 2.5 convert_bitcast_fusion.2
  915.6 1.6 convert_element_type.30
  917.2 1.6 convert_element_type.31
  (109 shorter events, 23.2 us)
Async XLA Ops:
  7.2 12.1 %copy-start = (bf16[768,768]{1,0:T(8,128)(2,1)S(1)}, bf16[768,768]{1,0:T(8,128)(2,1)}, u32[]{:S(2)}) copy-start(bf16[768,768]{1,0:T(8,128)(2,1)} %param.40) | copy-start | bytes 3538948
  7.2 14.8 %copy-start.13 = (s32[32,40]{1,0:T(8,128)S(1)}, s32[32,40]{1,0:T(8,128)}, u32[]{:S(2)}) copy-start(s32[32,40]{1,0:T(8,128)} %param.26) | copy-start | bytes 15364
  7.2 15.5 %copy-start.14 = (f32[768]{0:T(1024)S(1)}, f32[768]{0:T(1024)}, u32[]{:S(2)}) copy-start(f32[768]{0:T(1024)} %param.42) | copy-start | bytes 9220
  7.2 16.1 %copy-start.15 = (f32[768]{0:T(1024)S(1)}, f32[768]{0:T(1024)}, u32[]{:S(2)}) copy-start(f32[768]{0:T(1024)} %param.43) | copy-start | bytes 9220
  7.2 16.7 %copy-start.16 = (f32[768]{0:T(1024)S(1)}, f32[768]{0:T(1024)}, u32[]{:S(2)}) copy-start(f32[768]{0:T(1024)} %param.44) | copy-start | bytes 9220
  7.3 17.3 %copy-start.17 = (f32[768]{0:T(1024)S(1)}, f32[768]{0:T(1024)}, u32[]{:S(2)}) copy-start(f32[768]{0:T(1024)} %param.45) | copy-start | bytes 9220
  7.3 17.8 %copy-start.18 = (f32[768]{0:T(1024)S(1)}, f32[768]{0:T(1024)}, u32[]{:S(2)}) copy-start(f32[768]{0:T(1024)} %param.46) | copy-start | bytes 9220
  7.3 18.4 %copy-start.19 = (f32[768]{0:T(1024)S(1)}, f32[768]{0:T(1024)}, u32[]{:S(2)}) copy-start(f32[768]{0:T(1024)} %param.47) | copy-start | bytes 9220
  7.3 19.0 %copy-start.26 = (s32[32,2]{0,1:T(2,128)S(1)}, s32[32,2]{0,1:T(2,128)}, u32[]{:S(2)}) copy-start(s32[32,2]{0,1:T(2,128)} %param.29) | copy-start | bytes 772
  7.3 19.7 %copy-start.11 = (bf16[32,1024]{1,0:T(8,128)(2,1)S(1)}, bf16[32,1024]{1,0:T(8,128)(2,1)}, u32[]{:S(2)}) copy-start(bf16[32,1024]{1,0:T(8,128)(2,1)} %picture_ref.1) | copy-start | bytes 196612
  7.3 19.7 %copy-start.2 = (bf16[1024,256]{1,0:T(8,128)(2,1)S(1)}, bf16[1024,256]{1,0:T(8,128)(2,1)}, u32[]{:S(2)}) copy-start(bf16[1024,256]{1,0:T(8,128)(2,1)} %weight_ref.1) | copy-start | bytes 1572868
  7.3 61.1 %all-gather.15.cloned.1.call-start = ((), (), s32[]{:S(2)}) async-start(), calls=%async_computation.2 | async-start | bytes 1216512 | tf_op jit(solution)/shard_map/all_gather | solution.py:519
  8.9 116.0 %all-gather.17.cloned.1.call-start = ((), (), s32[]{:S(2)}) async-start(), calls=%async_computation.3 | async-start | bytes 1216512 | tf_op jit(solution)/shard_map/all_gather | solution.py:519
  10.4 171.0 %all-gather.19.cloned.1.call-start = ((), (), s32[]{:S(2)}) async-start(), calls=%async_computation.4 | async-start | bytes 1216512 | tf_op jit(solution)/shard_map/all_gather | solution.py:519
  11.8 225.9 %all-gather.21.cloned.1.call-start = ((), (), s32[]{:S(2)}) async-start(), calls=%async_computation.5 | async-start | bytes 1216512 | tf_op jit(solution)/shard_map/all_gather | solution.py:519
  13.3 280.7 %all-gather.23.cloned.1.call-start = ((), (), s32[]{:S(2)}) async-start(), calls=%async_computation.6 | async-start | bytes 1216512 | tf_op jit(solution)/shard_map/all_gather | solution.py:519
  14.8 336.7 %all-gather.11.cloned.1.call-start = ((), (), s32[]{:S(2)}) async-start(), calls=%async_computation | async-start | bytes 1622016 | tf_op jit(solution)/shard_map/all_gather | solution.py:519
  16.3 392.5 %all-gather.13.cloned.1.call-start = ((), (), s32[]{:S(2)}) async-start(), calls=%async_computation.1 | async-start | bytes 1622016 | tf_op jit(solution)/shard_map/all_gather | solution.py:519
  17.8 447.4 %all-gather.25.cloned.1.call-start = ((), (), s32[]{:S(2)}) async-start(), calls=%async_computation.7 | async-start | bytes 1216512 | tf_op jit(solution)/shard_map/all_gather | solution.py:519
  19.2 512.1 %all-gather.27.cloned.1.call-start = ((), (), s32[]{:S(2)}) async-start(), calls=%async_computation.8 | async-start | bytes 4866048 | tf_op jit(solution)/shard_map/all_gather | solution.py:519
  20.3 577.0 %all-gather.29.cloned.1.call-start = ((), (), s32[]{:S(2)}) async-start(), calls=%async_computation.9 | async-start | bytes 4866048 | tf_op jit(solution)/shard_map/all_gather | solution.py:519
  21.9 887.3 %all-reduce.3.cloned.1.call-start = ((), (), s32[]{:S(2)}) async-start(), calls=%async_computation.10 | async-start | bytes 11665408 | tf_op jit(solution)/shard_map/psum | solution.py:675
  808.4 2.3 copy-start.20
  808.4 2.3 copy-start.21
  909.2 2.5 copy-start.10
  909.2 3.4 copy-start.9
  909.2 4.2 copy-start.5
  911.7 3.0 copy-start.8
  911.7 3.9 copy-start.4
  914.8 2.4 copy-start.3
  917.2 3.6 copy-start.1
  917.2 2.5 copy-start.6
  (6 other events, 11.6 us)
Sparse Core Ops, SparseCore 0:
  11.6 56.7 all-gather.14
  71.9 52.9 all-gather.16
  128.3 52.9 all-gather.18
  184.7 52.9 all-gather.20
  241.0 52.9 all-gather.22
  297.3 54.1 all-gather.10
  354.9 53.8 all-gather.12
  412.2 52.9 all-gather.24
  468.6 62.6 all-gather.26
  534.7 62.4 all-gather.28
  808.6 100.5 all-reduce.2

commit v2 on v1

v2 whole, which is shorter than its diff:
```python
from functools import partial

import jax
import jax.numpy as jnp
from jax import lax
from jax.experimental import pallas as pl
from jax.experimental.pallas import tpu as pltpu
from jax.sharding import PartitionSpec as P

HEAD = 64
GROUP = 4 * HEAD
LN_EPS = 1e-06
NORM_EPS = 1e-06
BIG_NEG = -1000000000.0
F32 = jnp.float32
BF16 = jnp.bfloat16
VMEM_LIMIT = 60 * 2**20


def dot_nn(left, right):
    return lax.dot_general(left, right, (((1,), (0,)), ((), ())), preferred_element_type=F32)


def dot_nt(left, right):
    return lax.dot_general(left, right, (((1,), (1,)), ((), ())), preferred_element_type=F32)


def dot_tn(left, right):
    return lax.dot_general(left, right, (((0,), (0,)), ((), ())), preferred_element_type=F32)


def normalize(inputs):
    center = inputs - jnp.mean(inputs, axis=-1, keepdims=True)
    rstd = lax.rsqrt(jnp.mean(center * center, axis=-1, keepdims=True) + LN_EPS)
    return center * rstd, rstd


def norm_pull(grad, xhat, rstd, gain):
    scaled = grad * gain
    first = jnp.mean(scaled, axis=-1, keepdims=True)
    second = jnp.mean(scaled * xhat, axis=-1, keepdims=True)
    grad_in = rstd * (scaled - first - xhat * second)
    return grad_in, jnp.sum(grad * xhat, axis=0, keepdims=True), jnp.sum(grad, axis=0, keepdims=True)


def unit_pull(raw, grad):
    scale = lax.rsqrt(jnp.sum(raw * raw, axis=-1, keepdims=True) + NORM_EPS)
    inner = jnp.sum(grad * raw, axis=-1, keepdims=True)
    return scale * grad - raw * (scale * scale * scale * inner)


MESH = pl.DeviceIdType.MESH
DMA = pltpu.SemaphoreType.DMA


class Gather:
    def __init__(self, shards, outs, refs):
        count = len(outs)
        self.ins, self.outs, self.shards, sems = refs[:count], outs, shards, refs[count:]
        self.local, self.up, self.down, self.across, self.below, self.above, self.near, self.out, self.back = sems
        self.dp, self.z = lax.axis_index("dp"), lax.axis_index("mp")
        dp, z = self.dp, self.z
        self.core, self.x, self.y = dp % 2, dp // 2 % 2, dp // 4
        self.depth = outs[0].shape[1]
        self.color = (self.x + self.y) % 2
        east, north = 2 - 4 * self.x, 4 - 8 * self.y
        self.peers = [(dp + east, z), (dp + north, z), (dp + east + north, z)]
        self.twin = (dp + 1 - 2 * self.core, z)

    @staticmethod
    def semaphores(count, depth):
        grid = (count, depth)
        return [DMA((count,)), DMA(grid), DMA(grid), DMA((3, *grid)), DMA(grid), DMA(grid), DMA((3, *grid)), DMA(grid), DMA(grid)]

    def enter(self, everyone=0):
        barrier = pltpu.get_barrier_semaphore()
        peers = [*self.peers, self.twin]
        if everyone:
            peers = [((self.dp + k) % everyone, self.z) for k in range(1, everyone)]
        for peer in peers:
            pl.semaphore_signal(barrier, inc=1, device_id=peer, device_id_type=MESH)
        for step in (-1, 1):

            @pl.when(self.inside(self.z + step))
            def _(step=step):
                pl.semaphore_signal(barrier, inc=1, device_id=(self.dp, self.z + step), device_id_type=MESH)

        ends = (self.z > 0).astype(jnp.int32) + (self.z < self.depth - 1).astype(jnp.int32)
        pl.semaphore_wait(barrier, len(peers) + ends)

    def inside(self, z):
        return (z >= 0) & (z < self.depth)

    def part(self, index, source, first, size, core=None):
        mats = self.ins[index].shape[0] // 2
        core = self.core if core is None else core
        return self.outs[index].at[pl.ds(core * mats, mats), source, pl.ds(pl.multiple_of(first, 16), size), :]

    def copy(self, src, dst, send, recv, to):
        return pltpu.make_async_remote_copy(
            src_ref=src, dst_ref=dst, send_sem=send, recv_sem=recv, device_id=to, device_id_type=MESH
        )

    def span(self, index):
        tall = self.ins[index].shape[1]
        return self.color * (tall // 2) + self.y * (tall // 6), tall // 3

    def hop(self, index, source, step):
        spot = self.part(index, source, *self.span(index))
        send, recv = (self.up, self.below) if step > 0 else (self.down, self.above)
        return self.copy(spot, spot, send.at[index, source], recv.at[index, source], (self.dp, self.z + step))

    def first_hop(self, index, step):
        first, size = self.span(index)
        mats = self.ins[index].shape[0] // 2
        src = self.ins[index].at[pl.ds(self.core * mats, mats), pl.ds(pl.multiple_of(first, 16), size), :]
        send, recv = (self.up, self.below) if step > 0 else (self.down, self.above)
        spot = self.part(index, self.z, first, size)
        return self.copy(src, spot, send.at[index, self.z], recv.at[index, self.z], (self.dp, self.z + step))

    def side(self, index, source, which, inward=False):
        tall = self.ins[index].shape[1]
        color, y = self.color, self.y
        if inward:
            color, y = (1 - color, y) if which == 0 else (1 - color, 1 - y) if which == 1 else (color, 1 - y)
        pace, size = ((tall // 4, tall // 4), (tall // 4, tall // 4), (tall // 3, tall // 6))[which]
        spot = self.part(index, source, color * (tall // 2) + y * pace, size)
        sems = self.across.at[which, index, source], self.near.at[which, index, source]
        return self.copy(spot, spot, *sems, self.peers[which])

    def pass_on(self, index, source, inward=False):
        core = 1 - self.core if inward else self.core
        spot = self.part(index, source, 0, self.ins[index].shape[1], core)
        return self.copy(spot, spot, self.out.at[index, source], self.back.at[index, source], self.twin)

    def keep(self, index):
        return pltpu.make_async_copy(self.ins[index], self.outs[index].at[:, self.z], self.local.at[index])

    def start(self, everyone=0):
        count = 0
        for stack in self.ins:
            for index in range(stack.shape[0]):
                stack[index] = self.shards[count][...]
                count += 1
        self.enter(everyone)
        for index in range(len(self.ins)):
            for step in (1, -1):

                @pl.when(self.inside(self.z + step))
                def _(index=index, step=step):
                    self.first_hop(index, step).start()

            self.keep(index).start()

    def each(self, distance, what):
        for index in range(len(self.ins)):
            for step in (1, -1):
                source = self.z - step * distance

                @pl.when(self.inside(source))
                def _(index=index, step=step, source=source):
                    what(index, step, source)

    def pull(self, distance):
        def what(index, step, source):
            self.hop(index, source, step).wait_recv()

            @pl.when(self.inside(self.z + step))
            def _():
                self.hop(index, source, step).start()

            for which in range(3):
                self.side(index, source, which).start()

        self.each(distance, what)

    def pair(self, distance):
        def what(index, step, source):
            for which in range(3):
                self.side(index, source, which, inward=True).wait_recv()
            self.pass_on(index, source).start()

        self.each(distance, what)

    def finish(self):
        def what(index, step, source):
            self.pass_on(index, source, inward=True).wait_recv()
            self.pass_on(index, source).wait_send()
            for which in range(3):
                self.side(index, source, which).wait_send()

            @pl.when(self.inside(self.z + step))
            def _():
                self.hop(index, source, step).wait_send()

        for distance in range(1, self.depth):
            self.each(distance, what)
        for index in range(len(self.ins)):
            for step in (1, -1):

                @pl.when(self.inside(self.z + step))
                def _(index=index, step=step):
                    self.first_hop(index, step).wait_send()

            self.keep(index).wait()


class Reduce:
    def __init__(self, src, done, half, part, quarter, twin_sems, plane_sems):
        self.src, self.done, self.half, self.part, self.quarter = src, done, half, part, quarter
        self.twin_sems, self.plane_sems = twin_sems, plane_sems
        dp, z = lax.axis_index("dp"), lax.axis_index("mp")
        self.core, self.chip = dp % 2, dp // 2
        x, y = self.chip % 2, self.chip // 2
        east, north = 2 - 4 * x, 4 - 8 * y
        self.shifts = (east, north, east + north)
        self.peers = [(dp + shift, z) for shift in self.shifts]
        self.twin = (dp + 1 - 2 * self.core, z)
        self.tall = src.shape[0]

    @staticmethod
    def scratch(shape):
        rows, columns = shape
        sizes = ((rows, columns), (rows // 2, columns), (rows // 2, columns), (3, rows // 8, columns))
        return [*(pltpu.VMEM(size, BF16) for size in sizes), DMA((4,)), DMA((4, 3))]

    def enter(self):
        barrier = pltpu.get_barrier_semaphore()
        for peer in [*self.peers, self.twin]:
            pl.semaphore_signal(barrier, inc=1, device_id=peer, device_id_type=MESH)
        pl.semaphore_wait(barrier, 4)

    def copy(self, src, dst, send, recv, to):
        return pltpu.make_async_remote_copy(
            src_ref=src, dst_ref=dst, send_sem=send, recv_sem=recv, device_id=to, device_id_type=MESH
        )

    def mine(self, core):
        return pl.ds(pl.multiple_of(core * (self.tall // 2), 16), self.tall // 2)

    def slot(self, chip, core=None):
        first = chip * (self.tall // 8)
        if core is not None:
            first = first + core * (self.tall // 2)
        return pl.ds(pl.multiple_of(first, 16), self.tall // 8)

    def to_twin(self):
        sems = self.twin_sems.at[0], self.twin_sems.at[1]
        return self.copy(self.src.at[self.mine(1 - self.core)], self.half, *sems, self.twin)

    def scatter(self, which):
        chip = self.chip + self.shifts[which] // 2
        sems = self.plane_sems.at[0, which], self.plane_sems.at[1, which]
        return self.copy(self.part.at[self.slot(chip)], self.quarter.at[which], *sems, self.peers[which])

    def spread(self, which, chip):
        spot = self.done.at[self.slot(chip, self.core)]
        sems = self.plane_sems.at[2, which], self.plane_sems.at[3, which]
        return self.copy(spot, spot, *sems, self.peers[which])

    def back(self, core):
        spot = self.done.at[self.mine(core)]
        return self.copy(spot, spot, self.twin_sems.at[2], self.twin_sems.at[3], self.twin)

    def stage(self, number):
        if number == 1:
            self.to_twin().start()
        elif number == 2:
            self.to_twin().wait_recv()
            total = self.src[self.mine(self.core), :].astype(F32) + self.half[...].astype(F32)
            self.part[...] = total.astype(BF16)
            for which in range(3):
                self.scatter(which).start()
        elif number == 3:
            total = self.part[self.slot(self.chip), :].astype(F32)
            for which in range(3):
                self.scatter(which).wait_recv()
                total = total + self.quarter[which].astype(F32)
            self.done[self.slot(self.chip, self.core), :] = total.astype(BF16)
            for which in range(3):
                self.spread(which, self.chip).start()
        elif number == 4:
            for which in range(3):
                self.spread(which, self.chip + self.shifts[which] // 2).wait_recv()
            self.back(self.core).start()
        else:
            self.back(1 - self.core).wait_recv()
            self.to_twin().wait_send()
            for which in range(3):
                self.scatter(which).wait_send()
                self.spread(which, self.chip).wait_send()
            self.back(self.core).wait_send()


def spread_heads(tensor):
    count = tensor.shape[0]
    left = lax.broadcasted_iota(jnp.int32, (count, 2 * HEAD), 1) < HEAD
    low, high = tensor[:, : 2 * HEAD], tensor[:, 2 * HEAD :]
    zero = jnp.zeros_like(low)
    blank = jnp.zeros((2 * count, 2 * HEAD), tensor.dtype)
    near = jnp.concatenate([jnp.where(left, low, zero), jnp.where(left, zero, low), blank], axis=0)
    far = jnp.concatenate([blank, jnp.where(left, high, zero), jnp.where(left, zero, high)], axis=0)
    return jnp.concatenate([near, far], axis=1).astype(BF16)


def collect_heads(stacked, count):
    left = lax.broadcasted_iota(jnp.int32, (count, 2 * HEAD), 1) < HEAD
    low = jnp.where(left, stacked[:count, : 2 * HEAD], stacked[count : 2 * count, : 2 * HEAD])
    high = jnp.where(
        left, stacked[2 * count : 3 * count, 2 * HEAD :], stacked[3 * count :, 2 * HEAD :]
    )
    return jnp.concatenate([low, high], axis=1)


def attend_probs(query_blocks, keys, keep):
    scores = dot_nt(keys, query_blocks)
    scores = jnp.where(keep, scores, BIG_NEG)
    top = jnp.max(scores, axis=0, keepdims=True)
    shifted = jnp.exp(scores - top)
    total = jnp.sum(shifted, axis=0, keepdims=True)
    return shifted * (1.0 / total)


def attend_forward(query, keys, values, keep):
    probs = attend_probs(spread_heads(query), keys, keep).astype(BF16)
    return collect_heads(dot_tn(probs, values), query.shape[0])


def split_heads(tensor):
    left = lax.broadcasted_iota(jnp.int32, tensor.shape, 1) < HEAD
    zero = jnp.zeros_like(tensor)
    return jnp.concatenate([jnp.where(left, tensor, zero), jnp.where(left, zero, tensor)], axis=0).astype(BF16)


def attend_short(query, keys, values, keep):
    count = query.shape[0]
    left = lax.broadcasted_iota(jnp.int32, (count, 2 * HEAD), 1) < HEAD
    out = []
    for half in range(2):
        at = slice(half * 2 * HEAD, (half + 1) * 2 * HEAD)
        probs = attend_probs(split_heads(query[:, at]), keys[:, at], keep[:, : 2 * count])
        stacked = dot_nn(jnp.transpose(probs.astype(BF16)), values[:, at])
        out.append(jnp.where(left, stacked[:count], stacked[count:]))
    return jnp.concatenate(out, axis=1)


def attend_backward(query, keys, values, keep, grad_context):
    query_blocks = spread_heads(query)
    grad_blocks = spread_heads(grad_context)
    probs = attend_probs(query_blocks, keys, keep)
    grad_probs = dot_nt(values, grad_blocks)
    inner = jnp.sum(grad_probs * probs, axis=0, keepdims=True)
    grad_scores = (probs * (grad_probs - inner)).astype(BF16)
    grad_values = dot_nn(probs.astype(BF16), grad_blocks)
    grad_keys = dot_nn(grad_scores, query_blocks)
    grad_query = collect_heads(dot_tn(grad_scores, keys), query.shape[0]) * 0.125
    return grad_query, grad_keys, grad_values


def row_keep(bound, length):
    key = lax.broadcasted_iota(jnp.int32, (length, 4 * length), 0)
    query = lax.broadcasted_iota(jnp.int32, (length, 4 * length), 1) % length
    return (key >= bound) == (query >= bound)


def window(which, width):
    return pl.ds(pl.multiple_of(which * 3 // 2 * (width // 2), width // 2), width)


def own_rows(acc, which, own):
    odd = which % 2 == 1
    return jnp.where(odd, acc[acc.shape[0] - own :], acc[:own])


def prep_kernel(gathers, count, *refs):
    region_ref, picture_ref, weight_ref = refs[:3]
    shards, refs = refs[3 : 3 + count], refs[3 + count :]
    moved_ref, embed_ref = refs[:2]
    whole, refs = refs[2 : 2 + gathers], refs[2 + gathers :]
    flat_ref = refs[0]
    patch_count, images, lanes = region_ref.shape
    padded = moved_ref.shape[1]
    full_tiles = patch_count // 8 * 8
    step = pl.program_id(0)
    steps = pl.num_programs(0)
    gather = Gather(shards, whole, refs[1:]) if gathers else None

    @pl.when(step == 0)
    def _():
        if gather:
            gather.start()
        raw = dot_nn(picture_ref[...], weight_ref[...])
        scale = lax.rsqrt(jnp.sum(raw * raw, axis=-1, keepdims=True) + NORM_EPS)
        embed_ref[...] = (raw * scale).astype(BF16)

    flat_ref[...] = region_ref[...].reshape(patch_count * images, lanes).astype(F32)
    row = lax.broadcasted_iota(jnp.int32, (padded - full_tiles, lanes), 0)
    for image in range(images):
        main = flat_ref[pl.ds(image, full_tiles, stride=images), :]
        moved_ref[image, 0:full_tiles, :] = main.astype(BF16)
        last = flat_ref[pl.ds(full_tiles * images + image, 1), :]
        moved_ref[image, full_tiles:padded, :] = jnp.where(row == 0, last, 0.0).astype(BF16)

    if gather:

        for late, distance in ((6, 1), (4, 2), (2, 3)):

            @pl.when(step == steps - late)
            def _(distance=distance):
                gather.pull(distance)

        @pl.when(step == steps - 3)
        def _():
            gather.pair(1)

        @pl.when(step == steps - 1)
        def _():
            gather.pair(2)
            gather.pair(3)
            gather.finish()


def self_forward_kernel(length, gathers, count, *refs):
    bound_ref, tok_ref, wqkv_ref, wout_ref, embed_ref = refs[:5]
    shards, refs = refs[5 : 5 + count], refs[5 + count :]
    qkv_ref, ctx_ref, xhat_ref, rstd_ref = refs[:4]
    whole, refs = refs[4 : 4 + gathers], refs[4 + gathers :]
    width = tok_ref.shape[1]
    rows = tok_ref.shape[0] // length
    step = pl.program_id(0)
    steps = pl.num_programs(0)
    if gathers:
        images_ref, embed_local, embed_send, embed_recv = refs[:4]
        gather = Gather(shards, whole, refs[4:])
        dp, z = lax.axis_index("dp"), lax.axis_index("mp")
        dp_size = images_ref.shape[0] // embed_ref.shape[0]
        held = embed_ref.shape[0]

        def embed_copy(k, owner, to):
            spot = images_ref.at[pl.ds(pl.multiple_of(owner * held, 16), held), :]
            return pltpu.make_async_remote_copy(
                src_ref=embed_ref, dst_ref=spot, send_sem=embed_send.at[k], recv_sem=embed_recv.at[k],
                device_id=(to, z), device_id_type=MESH,
            )

        def embed_own():
            spot = images_ref.at[pl.ds(pl.multiple_of(dp * held, 16), held), :]
            return pltpu.make_async_copy(embed_ref, spot, embed_local)

        @pl.when(step == 0)
        def _():
            gather.start(everyone=dp_size)
            embed_own().start()
            for k in range(1, dp_size):
                embed_copy(k, dp, (dp + k) % dp_size).start()

        for distance in range(1, 4):

            @pl.when(step == distance)
            def _(distance=distance):
                gather.pull(distance)
                if distance > 1:
                    gather.pair(distance - 1)

    tok = tok_ref[...]
    for part in range(3):
        proj = dot_nt(tok, wqkv_ref[part * width : (part + 1) * width, :])
        if part == 0:
            proj = proj * 0.125
        qkv_ref[:, part * width : (part + 1) * width] = proj.astype(BF16)

    def pair(index, carry):
        span = pl.ds(pl.multiple_of(index * 2 * length, 16), 2 * length)
        keeps = [row_keep(bound_ref[step * rows + 2 * index + j], length) for j in range(2)]
        for group in range(width // GROUP):
            q, k, v = (
                qkv_ref[span, part * width + group * GROUP : part * width + (group + 1) * GROUP].astype(F32)
                for part in range(3)
            )
            out = []
            for j in range(2):
                at = slice(j * length, (j + 1) * length)
                out.append(attend_short(q[at], k[at].astype(BF16), v[at].astype(BF16), keeps[j]))
            ctx_ref[span, group * GROUP : (group + 1) * GROUP] = jnp.concatenate(out, axis=0).astype(BF16)
        return carry

    lax.fori_loop(0, rows // 2, pair, 0, unroll=2)
    attn = dot_nn(ctx_ref[...], wout_ref[...])
    xhat, rstd = normalize(tok.astype(F32) + attn)
    xhat_ref[...] = xhat
    rstd_ref[...] = rstd

    if gathers:

        @pl.when(step == steps - 1)
        def _():
            gather.pair(3)
            for k in range(1, dp_size):
                embed_copy(k, (dp + dp_size - k) % dp_size, (dp + k) % dp_size).wait_recv()
                embed_copy(k, dp, (dp + k) % dp_size).wait_send()
            embed_own().wait()
            gather.finish()


def cross_forward_kernel(patch_count, length, gathers, count, *refs):
    region_ref, wkv_ref, xhat1_ref, norm_ref, wcq_ref, wout_ref = refs[:6]
    shards, refs = refs[6 : 6 + count], refs[6 + count :]
    kv_ref, cq_ref, ctx_ref, xhat_ref, rstd_ref = refs[:5]
    whole, refs = refs[5 : 5 + gathers], refs[5 + gathers :]
    images, padded, vision = region_ref.shape
    width = cq_ref.shape[1]
    step = pl.program_id(0)
    steps = pl.num_programs(0)
    gather = Gather(shards, whole, refs) if gathers else None
    if gathers:

        @pl.when(step == 0)
        def _():
            gather.start()

        for distance in range(1, 4):

            @pl.when(step == distance)
            def _(distance=distance):
                gather.pull(distance)
                if distance > 1:
                    gather.pair(distance - 1)

    hidden1 = xhat1_ref[...] * norm_ref[0:1] + norm_ref[1:2]
    cq_ref[...] = (dot_nt(hidden1.astype(BF16), wcq_ref[...]) * 0.125).astype(BF16)
    flat = region_ref[...].reshape(images * padded, vision)

    def chunk(index, carry):
        at = pl.ds(pl.multiple_of(index * 512, 512), 512)
        proj = dot_nt(flat, wkv_ref[at, :])
        kv_ref[:, :, at] = proj.astype(BF16).reshape(images, padded, 512)
        return carry

    lax.fori_loop(0, 2 * width // 512, chunk, 0, unroll=True)
    keep = lax.broadcasted_iota(jnp.int32, (padded, 4 * length), 0) < patch_count

    def pair(index, carry):
        span = pl.ds(pl.multiple_of(index * 2 * length, 16), 2 * length)
        for group in range(width // GROUP):
            lanes = slice(group * GROUP, (group + 1) * GROUP)
            q = cq_ref[span, lanes].astype(F32)
            out = []
            for j in range(2):
                image = 2 * index + j
                keys = kv_ref[image, :, lanes]
                values = kv_ref[image, :, width + group * GROUP : width + (group + 1) * GROUP]
                out.append(attend_forward(q[j * length : (j + 1) * length], keys, values, keep))
            ctx_ref[span, lanes] = jnp.concatenate(out, axis=0).astype(BF16)
        return carry

    lax.fori_loop(0, images // 2, pair, 0, unroll=4)
    xhat, rstd = normalize(hidden1 + dot_nn(ctx_ref[...], wout_ref[...]))
    xhat_ref[...] = xhat
    rstd_ref[...] = rstd

    if gathers:

        @pl.when(step == steps - 1)
        def _():
            gather.pair(3)
            gather.finish()


def gelu_parts(inputs):
    cdf = 0.5 * (1.0 + lax.erf(inputs * 0.7071067811865476))
    density = jnp.exp(inputs * inputs * -0.5) * 0.3989422804014327
    return inputs * cdf, cdf + inputs * density


def feed_forward_kernel(
    length, bound_ref, which_ref, temp_ref, xhat2_ref, rstd2_ref, norm_ref,
    wup_ref, wdown_ref, adj_ref, target_ref, images_ref, wtext_ref,
    out_ref, loss_ref, pack_ref, dr2_ref, dup_ref, ddown_ref, dgain2_ref, dshift2_ref, dgain3_ref, dshift3_ref,
    dtext_ref, dtemp_ref,
    act_ref, slope_ref, final_ref, grad_ref, lead_ref, up_acc, down_acc, text_acc,
):
    step = pl.program_id(0)
    steps = pl.num_programs(0)
    tokens, width = xhat2_ref.shape
    hidden_units = wup_ref.shape[0]
    rows = tokens // length
    chunk = min(768, hidden_units)

    @pl.when(step == 0)
    def _():
        for ref in (dgain2_ref, dshift2_ref, dgain3_ref, dshift3_ref, dtemp_ref, up_acc, down_acc, text_acc):
            ref[...] = jnp.zeros_like(ref)

    xhat2 = xhat2_ref[...]
    hidden2 = xhat2 * norm_ref[2:3] + norm_ref[3:4]
    low = hidden2.astype(BF16)
    final_ref[...] = hidden2

    def forward(index, carry):
        at = pl.ds(pl.multiple_of(index * chunk, chunk), chunk)
        act, slope = gelu_parts(dot_nt(low, wup_ref[at, :]))
        act = act.astype(BF16)
        act_ref[:, at] = act
        slope_ref[:, at] = slope
        final_ref[...] += dot_nn(act, wdown_ref[at, :])
        return carry

    lax.fori_loop(0, hidden_units // chunk, forward, 0, unroll=True)
    xhat3, rstd3 = normalize(final_ref[...])
    final = xhat3 * norm_ref[4:5] + norm_ref[5:6]
    out_ref[...] = final.astype(BF16)
    final_ref[...] = final
    grad_ref[...] = adj_ref[...].astype(F32)

    for row in range(rows):
        lead_ref[pl.ds(2 * row, 1), :] = final_ref[pl.ds(row * length, 1), :]
        second = row * length + bound_ref[step * rows + row]
        lead_ref[pl.ds(2 * row + 1, 1), :] = final_ref[pl.ds(second, 1), :]
    lead = lead_ref[...].astype(BF16)
    raw = dot_nn(lead, wtext_ref[...])
    text = raw * lax.rsqrt(jnp.sum(raw * raw, axis=-1, keepdims=True) + NORM_EPS)
    text_low = text.astype(BF16)
    temp = temp_ref[0]
    logits = dot_nt(text_low, images_ref[...]) / temp
    top = jnp.max(logits, axis=1, keepdims=True)
    lse = top + jnp.log(jnp.sum(jnp.exp(logits - top), axis=1, keepdims=True))
    target = target_ref[...]
    hit = lax.broadcasted_iota(jnp.int32, logits.shape, 1) == target
    loss_ref[...] = lse - jnp.sum(jnp.where(hit, logits, 0.0), axis=1, keepdims=True)
    dlogits = jnp.exp(logits - lse) - hit.astype(F32)
    dtemp_ref[...] += -jnp.sum(jnp.sum(dlogits * logits, axis=1, keepdims=True), axis=0, keepdims=True) / temp
    embed = raw.shape[1]
    lane = lax.broadcasted_iota(jnp.int32, (2 * rows, 128), 1)
    pack_ref[:, :embed] = text_low.astype(F32)
    pack_ref[:, embed:] = jnp.where(lane == 0, lse, jnp.where(lane == 1, target.astype(F32), 0.0))
    dtext = dot_nn((dlogits / temp).astype(BF16), images_ref[...])
    draw = unit_pull(raw, dtext).astype(BF16)
    text_acc[...] += dot_tn(lead, draw)
    lead_ref[...] = dot_nt(draw, wtext_ref[...])
    for row in range(rows):
        first = pl.ds(row * length, 1)
        grad_ref[first, :] += lead_ref[pl.ds(2 * row, 1), :]
        second = pl.ds(row * length + bound_ref[step * rows + row], 1)
        grad_ref[second, :] += lead_ref[pl.ds(2 * row + 1, 1), :]

    dr3, dgain3, dshift3 = norm_pull(grad_ref[...], xhat3, rstd3, norm_ref[4:5])
    dgain3_ref[...] += dgain3
    dshift3_ref[...] += dshift3
    grad_ref[...] = dr3
    dfinal = dr3.astype(BF16)
    own = hidden_units // 4
    own_at = pl.ds(pl.multiple_of(which_ref[0] * own, own), own)
    down_acc[...] += dot_tn(act_ref[:, own_at], dfinal)

    def backward(index, carry):
        at = pl.ds(pl.multiple_of(index * chunk, chunk), chunk)
        dact = dot_nt(dfinal, wdown_ref[at, :])
        dinner = (dact * slope_ref[:, at]).astype(BF16)
        act_ref[:, at] = dinner
        grad_ref[...] += dot_nn(dinner, wup_ref[at, :])
        return carry

    lax.fori_loop(0, hidden_units // chunk, backward, 0, unroll=True)
    up_acc[...] += dot_tn(low, act_ref[:, own_at])
    dr2, dgain2, dshift2 = norm_pull(grad_ref[...], xhat2, rstd2_ref[...], norm_ref[2:3])
    dgain2_ref[...] += dgain2
    dshift2_ref[...] += dshift2
    dr2_ref[...] = dr2

    @pl.when(step == steps - 1)
    def _():
        dup_ref[...] = up_acc[...].astype(BF16)
        ddown_ref[...] = down_acc[...].astype(BF16)
        dtext_ref[...] = text_acc[...].astype(BF16)


def cross_backward_kernel(
    patch_count, length, which_ref, region_ref, kv_ref, cq_ref, ctx_ref, xhat1_ref, rstd1_ref, norm_ref,
    dr2_ref, wkv_ref, wout_ref, wcq_ref,
    dregion_ref, dr1_ref, dkv_ref, dqo_ref, dgain_ref, dshift_ref,
    dctx_ref, dq_ref, grads_ref, flat_ref, stage_ref, kv_acc, cq_acc, out_acc, sem,
):
    step = pl.program_id(0)
    steps = pl.num_programs(0)
    images, padded, vision = region_ref.shape
    width = cq_ref.shape[1]
    own = width // 4
    which = which_ref[0]
    mine = window(which, GROUP)
    wide = stage_ref.shape[2]
    parts = wide // images
    stored = flat_ref.shape[1] // wide

    @pl.when(step == 0)
    def _():
        for ref in (dgain_ref, dshift_ref, kv_acc, cq_acc, out_acc):
            ref[...] = jnp.zeros_like(ref)

    dr2 = dr2_ref[...]
    dx = dr2.astype(BF16)
    dctx_ref[...] = dot_nt(dx, wout_ref[...]).astype(BF16)
    out_acc[...] += dot_tn(ctx_ref[:, mine], dx)
    keep = lax.broadcasted_iota(jnp.int32, (padded, 4 * length), 0) < patch_count

    def pair(index, carry):
        span = pl.ds(pl.multiple_of(index * 2 * length, 16), 2 * length)
        for group in range(width // GROUP):
            lanes = slice(group * GROUP, (group + 1) * GROUP)
            value_lanes = slice(width + group * GROUP, width + (group + 1) * GROUP)
            q = cq_ref[span, lanes].astype(F32)
            d = dctx_ref[span, lanes].astype(F32)
            out = []
            for j in range(2):
                image = 2 * index + j
                at = slice(j * length, (j + 1) * length)
                dq, dk, dv = attend_backward(
                    q[at], kv_ref[image, :, lanes], kv_ref[image, :, value_lanes], keep, d[at]
                )
                out.append(dq)
                grads_ref[image, :, lanes] = dk.astype(BF16)
                grads_ref[image, :, value_lanes] = dv.astype(BF16)
            dq_ref[span, lanes] = jnp.concatenate(out, axis=0).astype(BF16)
        return carry

    lax.fori_loop(0, images // 2, pair, 0, unroll=4)

    some = 4
    for index in range(images // some):
        grads = grads_ref[index * some : (index + 1) * some].reshape(some * padded, 2 * width)
        dregion = dot_nn(grads, wkv_ref[...])
        for image in range(some):
            spot = pl.ds(step % parts * images + index * some + image, stored, stride=wide)
            for lane in range(vision // 128):
                flat_ref[lane, spot, :] = dregion[
                    image * padded : image * padded + stored, lane * 128 : (lane + 1) * 128
                ]
    region = region_ref[...].reshape(images * padded, vision)
    for part in range(2):
        at = window(which, GROUP)
        grads = grads_ref[:, :, pl.ds(pl.multiple_of(which * 3 // 2 * 128 + part * width, 128), GROUP)]
        kv_acc[part] += dot_tn(grads.reshape(images * padded, GROUP), region)

    pieces = 5
    patches = patch_count // pieces
    tall = patches * wide

    def send(index):
        slot = index % 2
        base = pl.multiple_of(step // parts * wide, 16)
        return pltpu.make_async_copy(
            stage_ref.at[slot],
            dregion_ref.at[pl.ds(index * patches, patches), pl.ds(base, wide), :],
            sem.at[slot],
        )

    @pl.when(step % parts == parts - 1)
    def _():
        for index in range(pieces):
            rows = slice(index * tall, (index + 1) * tall)
            low = jnp.concatenate([flat_ref[c, rows, :].astype(BF16) for c in range(vision // 128)], axis=1)
            if index >= 2:
                send(index - 2).wait()
            stage_ref[index % 2] = low.reshape(patches, wide, vision)
            send(index).start()
        send(pieces - 2).wait()
        send(pieces - 1).wait()

    xhat1 = xhat1_ref[...]
    hidden1 = (xhat1 * norm_ref[0:1] + norm_ref[1:2]).astype(BF16)
    cq_acc[...] += dot_tn(dq_ref[:, mine], hidden1)
    dh1 = dr2 + dot_nn(dq_ref[...], wcq_ref[...])
    dr1, dgain, dshift = norm_pull(dh1, xhat1, rstd1_ref[...], norm_ref[0:1])
    dr1_ref[...] = dr1
    dgain_ref[...] += dgain
    dshift_ref[...] += dshift

    @pl.when(step == steps - 1)
    def _():
        for part in range(2):
            dkv_ref[part * own : (part + 1) * own, :] = own_rows(kv_acc[part], which, own).astype(BF16)
        dqo_ref[:own, :] = own_rows(cq_acc[...], which, own).astype(BF16)
        dqo_ref[own:, :] = own_rows(out_acc[...], which, own).astype(BF16)


def self_backward_kernel(length, sums, *refs):
    bound_ref, tok_ref, qkv_ref, ctx_ref, dr1_ref, wqkv_ref, wout_ref = refs[:7]
    refs = refs[7:]
    if sums:
        dkv_ref, dqo_ref, temp_ref, pack_ref, picture_ref, wimage_ref = refs[:6]
        vectors, refs = refs[6:13], refs[13:]
    dtok_ref, last_ref = refs[:2]
    refs = refs[2:]
    if sums:
        outs, dpicture_ref, refs = refs[:4], refs[4], refs[5:]
    dctx_ref, grads_ref, qkv_acc, out_acc, last = refs[:5]
    refs = refs[5:]
    step = pl.program_id(0)
    steps = pl.num_programs(0)
    tokens, width = tok_ref.shape
    rows = tokens // length
    own = width // 4
    which = lax.axis_index("mp")
    if sums:
        packs, dimage, small, pack_sent, pack_came = refs[:5]
        refs = refs[5:]
        spots = (dkv_ref, dqo_ref, small, dimage, last.at[: 2 * own], last.at[2 * own :])
        kv_sum, qo_sum, small_sum, image_sum, *finals = (
            Reduce(spot, *refs[6 * i : 6 * i + 6]) for i, spot in enumerate(spots)
        )
        dp, z = lax.axis_index("dp"), lax.axis_index("mp")
        dp_size = packs.shape[0]

        def pack_copy(k, owner):
            return pltpu.make_async_remote_copy(
                src_ref=pack_ref, dst_ref=packs.at[owner], send_sem=pack_sent.at[k], recv_sem=pack_came.at[k],
                device_id=((dp + k) % dp_size, z), device_id_type=MESH,
            )

        @pl.when(step == 0)
        def _():
            small[...] = jnp.zeros(small.shape, BF16)
            lines = [ref[...] for ref in vectors[:6]] + [jnp.broadcast_to(vectors[6][...], (1, width))]
            lines = [*lines, jnp.zeros((16 - len(lines), width), F32)]
            small[0:16, :] = jnp.concatenate(lines, axis=0).astype(BF16)
            barrier = pltpu.get_barrier_semaphore()
            for k in range(1, dp_size):
                pl.semaphore_signal(barrier, inc=1, device_id=((dp + k) % dp_size, z), device_id_type=MESH)
            pl.semaphore_wait(barrier, dp_size - 1)
            for k in range(1, dp_size):
                pack_copy(k, dp).start()
            packs[dp] = pack_ref[...]
            for reduce in (kv_sum, qo_sum, small_sum):
                reduce.stage(1)

        @pl.when(step == 1)
        def _():
            for reduce in (kv_sum, qo_sum, small_sum):
                reduce.stage(2)
            for k in range(1, dp_size):
                pack_copy(k, (dp + dp_size - k) % dp_size).wait_recv()
                pack_copy(k, dp).wait_send()
            everyone = packs[...].reshape(-1, packs.shape[2])
            first = dp * picture_ref.shape[0]
            dpicture, dweight = image_backward(first, temp_ref[0], picture_ref[...], wimage_ref[...], everyone)
            dpicture_ref[...] = dpicture
            dimage[...] = dweight.astype(BF16)
            image_sum.stage(1)

        for number in (3, 4):

            @pl.when(step == number - 1)
            def _(number=number):
                for reduce in (kv_sum, qo_sum, small_sum):
                    reduce.stage(number)
                image_sum.stage(number - 1)

    @pl.when(step == 0)
    def _():
        for ref in (qkv_acc, out_acc):
            ref[...] = jnp.zeros_like(ref)

    dr1 = dr1_ref[...]
    da = dr1.astype(BF16)
    dctx_ref[...] = dot_nt(da, wout_ref[...]).astype(BF16)
    out_acc[...] += dot_tn(ctx_ref[:, window(which, GROUP)], da)

    def pair(index, carry):
        span = pl.ds(pl.multiple_of(index * 2 * length, 16), 2 * length)
        keeps = [row_keep(bound_ref[step * rows + 2 * index + j], length) for j in range(2)]
        for group in range(width // GROUP):
            q, k, v = (
                qkv_ref[span, part * width + group * GROUP : part * width + (group + 1) * GROUP].astype(F32)
                for part in range(3)
            )
            d = dctx_ref[span, group * GROUP : (group + 1) * GROUP].astype(F32)
            outs = []
            for j in range(2):
                at = slice(j * length, (j + 1) * length)
                outs.append(attend_backward(q[at], k[at].astype(BF16), v[at].astype(BF16), keeps[j], d[at]))
            for part in range(3):
                both = jnp.concatenate([outs[0][part], outs[1][part]], axis=0).astype(BF16)
                grads_ref[span, part * width + group * GROUP : part * width + (group + 1) * GROUP] = both
        return carry

    lax.fori_loop(0, rows // 2, pair, 0, unroll=4)
    tok = tok_ref[...]
    for part in range(3):
        mine = grads_ref[:, pl.ds(pl.multiple_of(which * 3 // 2 * 128 + part * width, 128), GROUP)]
        qkv_acc[part] += dot_tn(mine, tok)

    @pl.when(step == steps - 1)
    def _():
        for part in range(3):
            last[part * own : (part + 1) * own, :] = own_rows(qkv_acc[part], which, own).astype(BF16)
        last[3 * own : 4 * own, :] = own_rows(out_acc[...], which, own).astype(BF16)
        if sums:
            for reduce in finals:
                reduce.stage(1)

    dtok_ref[...] = dr1 + dot_nn(grads_ref[...], wqkv_ref[...])

    @pl.when(step == steps - 1)
    def _():
        if sums:
            image_sum.stage(4)
            for number in range(2, 6):
                for reduce in finals:
                    reduce.stage(number)
            for reduce in (kv_sum, qo_sum, small_sum, image_sum):
                reduce.stage(5)
            for reduce, out in zip((kv_sum, qo_sum, small_sum, image_sum), outs, strict=True):
                out[...] = reduce.done[...]
            last_ref[: 2 * own, :] = finals[0].done[...]
            last_ref[2 * own :, :] = finals[1].done[...]
        else:
            last_ref[...] = last[...]


def image_backward(first, temp, picture, weight, pack):
    raw = dot_nn(picture, weight)
    own = (raw * lax.rsqrt(jnp.sum(raw * raw, axis=-1, keepdims=True) + NORM_EPS)).astype(BF16)
    embed = raw.shape[1]
    text = pack[:, :embed].astype(BF16)
    lse = pack[:, embed : embed + 1]
    target = pack[:, embed + 1 : embed + 2].astype(jnp.int32)
    logits = dot_nt(text, own) / temp
    hit = lax.broadcasted_iota(jnp.int32, logits.shape, 1) + first == target
    dlogits = jnp.exp(logits - lse) - hit.astype(F32)
    dimage = dot_tn((dlogits / temp).astype(BF16), text)
    draw = unit_pull(raw, dimage).astype(BF16)
    return dot_nt(draw, weight), dot_tn(picture, draw)


def image_backward_kernel(
    first_ref, temp_ref, picture_ref, weight_ref, pack_ref, dpicture_ref, dweight_ref
):
    dpicture, dweight = image_backward(
        first_ref[0], temp_ref[0], picture_ref[...], weight_ref[...], pack_ref[...]
    )
    dpicture_ref[...] = dpicture
    dweight_ref[...] = dweight.astype(BF16)


def widen_kernel(own, last_ref, dkv_ref, dqo_ref, dimage_ref, dup_ref, ddown_ref, dtext_ref, small_ref, *outs):
    for index in range(4):
        outs[index][...] = last_ref[index * own : (index + 1) * own, :].astype(F32)
    for index in range(2):
        outs[4 + index][...] = dqo_ref[index * own : (index + 1) * own, :].astype(F32)
        outs[6 + index][...] = dkv_ref[index * own : (index + 1) * own, :].astype(F32)
    for out, ref in zip(outs[8:12], (dup_ref, ddown_ref, dtext_ref, dimage_ref), strict=True):
        out[...] = ref[...].astype(F32)
    small = small_ref[0:16, :].astype(F32)
    for index in range(6):
        outs[12 + index][...] = small[index]
    outs[18][...] = small[6:7, 0:1]


def full(shape):
    return pl.BlockSpec(shape, lambda i: (0,) * len(shape), pipeline_mode=pl.Buffered(1))


def fixed(shape):
    return pl.BlockSpec(shape, lambda i: (0,) * len(shape))


def rows_of(count, width):
    return pl.BlockSpec((count, width), lambda i: (i, 0))


SMEM = pl.BlockSpec(memory_space=pltpu.SMEM)


def shape_of(shape, kind):
    return jax.ShapeDtypeStruct(shape, kind)


def call(kernel, steps, ins, outs, args, scratch=(), flops=0, moved=0, ident=None):
    specs, shapes = zip(*outs, strict=True)
    remote = {} if ident is None else {"collective_id": ident, "has_side_effects": True}
    return pl.pallas_call(
        kernel,
        grid=(steps,),
        in_specs=list(ins),
        out_specs=list(specs),
        out_shape=list(shapes),
        scratch_shapes=list(scratch),
        compiler_params=pltpu.CompilerParams(
            vmem_limit_bytes=VMEM_LIMIT, dimension_semantics=("arbitrary",), **remote
        ),
        cost_estimate=pl.CostEstimate(flops=flops, bytes_accessed=moved, transcendentals=0),
    )(*args)


DEPTH = 4


def gathered(groups):
    shapes = [(len(group), *group[0].shape) for group in groups]
    outs = [
        (pl.BlockSpec(memory_space=pl.ANY), shape_of((shape[0], DEPTH, *shape[1:]), BF16)) for shape in shapes
    ]
    scratch = [pltpu.VMEM(shape, BF16) for shape in shapes]
    specs = [full(shard.shape) for group in groups for shard in group]
    return specs, outs, [*scratch, *Gather.semaphores(len(groups), DEPTH)] if groups else []


def flatten(groups):
    return [shard for group in groups for shard in group]


TOKEN_ROWS = 8
IMAGE_ROWS = 16


def square(width, index):
    return pl.BlockSpec((width, width), lambda i: (index, 0), pipeline_mode=pl.Buffered(1))


def run_prep(region, picture, wimage, shards):
    patch_count, rows, vision = region.shape
    padded = -(-patch_count // 16) * 16
    embed = wimage.shape[1]
    specs, outs, sems = gathered(shards)
    return call(
        partial(prep_kernel, len(shards), len(flatten(shards))),
        vision // 128,
        [pl.BlockSpec((patch_count, rows, 128), lambda i: (0, 0, i)), full(picture.shape), full(wimage.shape), *specs],
        [
            (pl.BlockSpec((rows, padded, 128), lambda i: (0, 0, i)), shape_of((rows, padded, vision), BF16)),
            (fixed((rows, embed)), shape_of((rows, embed), BF16)),
            *outs,
        ],
        (region, picture, wimage, *flatten(shards)),
        scratch=[pltpu.VMEM((patch_count * rows, 128), F32), *sems],
        moved=4 * rows * padded * vision,
        ident=1 if shards else None,
    )


def run_self_forward(length, dp_size, bound, tok, squares, embed, shards):
    tokens, width = tok.shape
    block = TOKEN_ROWS * length
    specs, outs, sems = gathered(shards)
    if shards:
        shape = shape_of((dp_size * embed.shape[0], embed.shape[1]), BF16)
        outs = [*outs, (pl.BlockSpec(memory_space=pl.ANY), shape)]
        sems = [DMA, DMA((dp_size,)), DMA((dp_size,)), *sems]
    return call(
        partial(self_forward_kernel, length, len(shards), len(flatten(shards))),
        tokens // block,
        [SMEM, rows_of(block, width), full((3 * width, width)), square(width, 3), full(embed.shape), *specs],
        [
            (rows_of(block, 3 * width), shape_of((tokens, 3 * width), BF16)),
            (rows_of(block, width), shape_of((tokens, width), BF16)),
            (rows_of(block, width), shape_of((tokens, width), F32)),
            (rows_of(block, 1), shape_of((tokens, 1), F32)),
            *outs,
        ],
        (bound, tok, squares, squares, embed, *flatten(shards)),
        scratch=sems,
        flops=10 * tokens * width * width,
        moved=20 * tokens * width,
        ident=2 if shards else None,
    )


def run_cross_forward(length, patch_count, region, wkv, xhat1, norms, wcq, wout, shards):
    rows, padded, vision = region.shape
    tokens, width = xhat1.shape
    images = TOKEN_ROWS
    block = images * length
    specs, outs, sems = gathered(shards)
    return call(
        partial(cross_forward_kernel, patch_count, length, len(shards), len(flatten(shards))),
        rows // images,
        [
            pl.BlockSpec((images, padded, vision), lambda i: (i, 0, 0)), full((2 * width, vision)),
            rows_of(block, width), full(norms.shape), square(width, 0), square(width, 1), *specs,
        ],
        [
            (
                pl.BlockSpec((images, padded, 2 * width), lambda i: (i, 0, 0)),
                shape_of((rows, padded, 2 * width), BF16),
            ),
            (rows_of(block, width), shape_of((tokens, width), BF16)),
            (rows_of(block, width), shape_of((tokens, width), BF16)),
            (rows_of(block, width), shape_of((tokens, width), F32)),
            (rows_of(block, 1), shape_of((tokens, 1), F32)),
            *outs,
        ],
        (region, wkv, xhat1, norms, wcq, wout, *flatten(shards)),
        scratch=sems,
        flops=4 * rows * padded * width * vision,
        moved=2 * rows * padded * (vision + 2 * width),
        ident=3 if shards else None,
    )


def run_feed_forward(
    length, bound, which, temp, xhat2, rstd2, norms, ffn, adjoint, target, image_all, wtext
):
    tokens, width = xhat2.shape
    hidden_units = ffn.shape[0] // 2
    embed = wtext.shape[1]
    block = IMAGE_ROWS * length
    captions = 2 * IMAGE_ROWS
    ff_own = hidden_units // 4
    return call(
        partial(feed_forward_kernel, length),
        tokens // block,
        [
            SMEM, SMEM, SMEM, rows_of(block, width), rows_of(block, 1), full(norms.shape),
            full((hidden_units, width)),
            pl.BlockSpec((hidden_units, width), lambda i: (1, 0), pipeline_mode=pl.Buffered(1)),
            rows_of(block, width), rows_of(captions, 1),
            full(image_all.shape), full((width, embed)),
        ],
        [
            (rows_of(block, width), shape_of((tokens, width), BF16)),
            (rows_of(captions, 1), shape_of(target.shape, F32)),
            (rows_of(captions, embed + 128), shape_of((target.shape[0], embed + 128), F32)),
            (rows_of(block, width), shape_of((tokens, width), F32)),
            (fixed((width, ff_own)), shape_of((width, ff_own), BF16)),
            (fixed((ff_own, width)), shape_of((ff_own, width), BF16)),
            (fixed((1, width)), shape_of((1, width), F32)),
            (fixed((1, width)), shape_of((1, width), F32)),
            (fixed((1, width)), shape_of((1, width), F32)),
            (fixed((1, width)), shape_of((1, width), F32)),
            (fixed((width, embed)), shape_of((width, embed), BF16)),
            (fixed((1, 1)), shape_of((1, 1), F32)),
        ],
        (
            bound, which, temp, xhat2, rstd2, norms, ffn, ffn, adjoint, target, image_all,
            wtext,
        ),
        scratch=[
            pltpu.VMEM((block, hidden_units), BF16),
            pltpu.VMEM((block, hidden_units), F32),
            pltpu.VMEM((block, width), F32),
            pltpu.VMEM((block, width), F32),
            pltpu.VMEM((captions, width), F32),
            pltpu.VMEM((width, ff_own), F32),
            pltpu.VMEM((ff_own, width), F32),
            pltpu.VMEM((width, embed), F32),
        ],
        flops=10 * tokens * width * hidden_units,
        moved=20 * tokens * width,
    )


def run_cross_backward(length, patch_count, which, region, kv, cq, ctx2, xhat1, rstd1, norms, dr2, wkv, wcq, wout):
    rows, padded, vision = region.shape
    tokens, width = cq.shape
    images = TOKEN_ROWS
    block = images * length
    own = width // 4
    stored = -(-patch_count // 8) * 8
    return call(
        partial(cross_backward_kernel, patch_count, length),
        rows // images,
        [
            SMEM,
            pl.BlockSpec((images, padded, vision), lambda i: (i, 0, 0)),
            pl.BlockSpec((images, padded, 2 * width), lambda i: (i, 0, 0)),
            rows_of(block, width), rows_of(block, width), rows_of(block, width), rows_of(block, 1), full(norms.shape),
            rows_of(block, width), full((2 * width, vision)), square(width, 1), square(width, 0),
        ],
        [
            (pl.BlockSpec(memory_space=pl.ANY), shape_of((patch_count, rows, vision), BF16)),
            (rows_of(block, width), shape_of((tokens, width), F32)),
            (fixed((2 * own, vision)), shape_of((2 * own, vision), BF16)),
            (fixed((2 * own, width)), shape_of((2 * own, width), BF16)),
            (fixed((1, width)), shape_of((1, width), F32)),
            (fixed((1, width)), shape_of((1, width), F32)),
        ],
        (which, region, kv, cq, ctx2, xhat1, rstd1, norms, dr2, wkv, wout, wcq),
        scratch=[
            pltpu.VMEM((block, width), BF16),
            pltpu.VMEM((block, width), BF16),
            pltpu.VMEM((images, padded, 2 * width), BF16),
            pltpu.VMEM((vision // 128, stored * IMAGE_ROWS, 128), F32),
            pltpu.VMEM((2, patch_count // 5, IMAGE_ROWS, vision), BF16),
            pltpu.VMEM((2, GROUP, vision), F32),
            pltpu.VMEM((GROUP, width), F32),
            pltpu.VMEM((GROUP, width), F32),
            DMA((2,)),
        ],
        flops=6 * rows * padded * width * vision,
        moved=2 * rows * padded * 2 * (vision + width),
    )


def run_self_backward(length, dp_size, bound, tok, qkv, ctx1, dr1, selves, others):
    tokens, width = tok.shape
    block = TOKEN_ROWS * length
    last = shape_of((width, width), BF16)
    extra, outs, scratch = [], [], []
    if others:
        dkv, dqo, _, pack, picture, wimage, *vectors = others
        image = shape_of(wimage.shape, BF16)
        small = shape_of((128, width), BF16)
        half = (width // 2, width)
        shapes = [shape_of(dkv.shape, BF16), shape_of(dqo.shape, BF16), small, image]
        extra = [full(dkv.shape), full(dqo.shape), SMEM, *(full(other.shape) for other in others[3:])]
        outs = [*((fixed(shape.shape), shape) for shape in shapes), (fixed(picture.shape), shape_of(picture.shape, F32))]
        scratch = [
            pltpu.VMEM((dp_size, *pack.shape), F32), pltpu.VMEM(image.shape, BF16), pltpu.VMEM(small.shape, BF16),
            DMA((dp_size,)), DMA((dp_size,)),
            *(spot for shape in (*(shape.shape for shape in shapes), half, half) for spot in Reduce.scratch(shape)),
        ]
    return call(
        partial(self_backward_kernel, length, bool(others)),
        tokens // block,
        [
            SMEM, rows_of(block, width), rows_of(block, 3 * width), rows_of(block, width), rows_of(block, width),
            full((3 * width, width)), square(width, 3), *extra,
        ],
        [(rows_of(block, width), shape_of((tokens, width), F32)), (fixed(last.shape), last), *outs],
        (bound, tok, qkv, ctx1, dr1, selves, selves, *others),
        scratch=[
            pltpu.VMEM((block, width), BF16),
            pltpu.VMEM((block, 3 * width), BF16),
            pltpu.VMEM((3, GROUP, width), F32),
            pltpu.VMEM((GROUP, width), F32),
            pltpu.VMEM(last.shape, BF16),
            *scratch,
        ],
        flops=10 * tokens * width * width,
        moved=20 * tokens * width,
        ident=4 if others else None,
    )


def run_widen(last, dkv, dqo, dimage, dup, ddown, dtext, small):
    width = last.shape[1]
    own = width // 4
    shapes = [(own, width)] * 6 + [(own, dkv.shape[1])] * 2
    shapes += [dup.shape, ddown.shape, dtext.shape, dimage.shape] + [(width,)] * 6 + [(1, 1)]
    args = (last, dkv, dqo, dimage, dup, ddown, dtext, small)
    return call(
        partial(widen_kernel, own),
        1,
        [fixed(array.shape) for array in args],
        [(fixed(shape), shape_of(shape, F32)) for shape in shapes],
        args,
        moved=20 * width * width,
    )


def body(
    dp_size,
    word_features,
    sentence_numbering,
    region_features,
    picture_global_feature,
    matched_picture,
    sharpness_array,
    incoming_adjoint,
    intra_asking_map,
    intra_lookup_map,
    intra_content_map,
    intra_attend_exit_map,
    visual_asking_map,
    visual_lookup_map,
    visual_content_map,
    visual_attend_exit_map,
    mlp_widening_factor,
    mlp_narrowing_factor,
    initial_standardize_scale,
    initial_standardize_offset,
    middle_standardize_scale,
    middle_standardize_offset,
    final_standardize_scale,
    final_standardize_offset,
    sentence_mapping_factor,
    picture_mapping_factor,
):
    rows, length = sentence_numbering.shape
    tokens, width = word_features.shape
    patch_count, vision = region_features.shape[1:]
    embed = sentence_mapping_factor.shape[1]
    hidden_units = mlp_widening_factor.shape[1] * 4
    own = width // 4
    which = lax.axis_index("mp").astype(jnp.int32).reshape(1)
    bound = (length - jnp.sum(sentence_numbering, axis=1)).astype(jnp.int32)
    target = matched_picture.reshape(-1, 1)
    norms = jnp.stack([
        initial_standardize_scale, initial_standardize_offset, middle_standardize_scale,
        middle_standardize_offset, final_standardize_scale, final_standardize_offset,
    ])

    selves = (intra_asking_map.T, intra_lookup_map.T, intra_content_map.T, intra_attend_exit_map)
    crosses = (visual_asking_map.T, visual_attend_exit_map)
    wides = (visual_lookup_map.T, visual_content_map.T)
    ffns = (mlp_widening_factor.T, mlp_narrowing_factor)
    region = jnp.transpose(region_features, (1, 0, 2))
    local = dp_size == 8 and lax.axis_size("mp") == DEPTH

    def each(*shards):
        return list(shards) if local else []

    region, image_own, *found = run_prep(region, picture_global_feature, picture_mapping_factor, each(selves))
    selves = (found[0] if local else lax.all_gather(jnp.stack(selves), "mp", axis=1)).reshape(-1, width)
    qkv, ctx1, xhat1, rstd1, *found = run_self_forward(
        length, dp_size, bound, word_features, selves, image_own, each(crosses, wides)
    )
    if local:
        crosses, wides, image_all = found
    else:
        crosses, wides = (lax.all_gather(jnp.stack(group), "mp", axis=1) for group in (crosses, wides))
        image_all = lax.all_gather(image_own, "dp", axis=0, tiled=True)
    crosses = crosses.reshape(-1, width)
    wkv = wides.reshape(-1, vision)
    kv, cq, ctx2, xhat2, rstd2, *found = run_cross_forward(
        length, patch_count, region, wkv, xhat1, norms, crosses, crosses, each(ffns)
    )
    ffns = (found[0] if local else lax.all_gather(jnp.stack(ffns), "mp", axis=1)).reshape(-1, width)
    (
        block_exit, loss, pack, dr2, dup, ddown, dgain2, dshift2, dgain3, dshift3, dtext, dtemp,
    ) = run_feed_forward(
        length, bound, which, sharpness_array, xhat2, rstd2, norms, ffns, incoming_adjoint, target, image_all,
        sentence_mapping_factor,
    )

    dp_sum = lambda grad: lax.psum(grad, "dp")
    dup, ddown, dtext = dp_sum((dup, ddown, dtext))
    dregion, dr1, dkv, dqo, dgain1, dshift1 = run_cross_backward(
        length, patch_count, which, region, kv, cq, ctx2, xhat1, rstd1, norms, dr2, wkv, crosses, crosses
    )
    vectors = (dgain1, dshift1, dgain2, dshift2, dgain3, dshift3, dtemp)
    pictures = (picture_global_feature, picture_mapping_factor)
    dtok, last, *found = run_self_backward(
        length, dp_size, bound, word_features, qkv, ctx1, dr1, selves,
        each(dkv, dqo, sharpness_array, pack, *pictures, *vectors),
    )
    if local:
        dkv, dqo, small, dimage, dpicture = found
    else:
        pack_all = lax.all_gather(pack, "dp", axis=0, tiled=True)
        first = (lax.axis_index("dp") * rows).astype(jnp.int32).reshape(1)
        dpicture, dimage = call(
            image_backward_kernel,
            1,
            [SMEM, SMEM, *(full(array.shape) for array in (*pictures, pack_all))],
            [
                (fixed((rows, vision)), shape_of((rows, vision), F32)),
                (fixed((vision, embed)), shape_of((vision, embed), BF16)),
            ],
            (first, sharpness_array, *pictures, pack_all),
        )
        lines = [*vectors[:6], jnp.broadcast_to(dtemp, (1, width)), jnp.zeros((9, width), F32)]
        small = jnp.concatenate(lines).astype(BF16)
        dkv, dqo, dimage, last, small = dp_sum((dkv, dqo, dimage, last, small))
    dq, dk, dv, dso, dcq, dco, dck, dcv, dup, ddown, dtext, dimage, *vectors = run_widen(
        last, dkv, dqo, dimage, dup, ddown, dtext, small
    )
    return (
        loss.reshape(rows, 2),
        block_exit,
        dtok,
        jnp.transpose(dregion, (1, 0, 2)),
        dpicture,
        vectors[6].reshape(1),
        dq.T,
        dk.T,
        dv.T,
        dso,
        dcq.T,
        dck.T,
        dcv.T,
        dco,
        dup,
        ddown,
        *vectors[:6],
        dtext,
        dimage,
    )


def solution(mesh):
    rows = P("dp", None)
    by_column = P(None, "mp")
    by_row = P("mp", None)
    in_specs = (
        rows, rows, P("dp", None, None), rows, rows, P(), rows,
        by_column, by_column, by_column, by_row, by_column, by_column, by_column, by_row, by_column, by_row,
        P(), P(), P(), P(), P(), P(), P(), P(),
    )
    out_specs = (
        rows, rows, rows, P("dp", None, None), rows, P(),
        by_column, by_column, by_column, by_row, by_column, by_column, by_column, by_row, by_column, by_row,
        P(), P(), P(), P(), P(), P(), P(), P(),
    )
    return jax.shard_map(
        partial(body, mesh.shape["dp"]), mesh=mesh, in_specs=in_specs, out_specs=out_specs, check_vma=False
    )
```

time: 936 us -> 364 us (0.39)
  the two profiles are of different devices: /device:TPU:0 before, /device:TPU:17 now
where the time goes in v2:
time: 364 us; the launch traced here: 358 us
  Pallas kernels  330 us (91%)
  between operations  15.1 us (4%)
  local copies, waits for them, and re-layouts  11.3 us (3%)
    pallas_call x7, Pallas kernels, call(): pl.pallas_call(kernel, grid=(steps,), in_specs=list(ins), out_specs=list(...  330 us
  transfers between devices with their start and end apart: 1, of which 0 were waited for; matrix products, arithmetic and copies ran while one was open for 0% of the time, Pallas kernels for 42%

profile of v2, /device:TPU:17, one launch (start us, length us, event | category | flops | bytes accessed | tf_op | source)
XLA Modules:
  0.0 357.6 jit_solution(7442850536096203608)
XLA Ops:
  7.2 0.0 copy-start.3
  7.2 0.0 all-reduce.3.cloned.1.call-start
  7.3 0.8 reduce_sum.9
  8.1 0.5 broadcast_subtract_fusion.refs_0_.bound_ref
  9.3 0.7 stack.21
  9.9 0.7 stack.22
  10.6 0.7 stack.23
  11.3 0.7 stack.24
  12.0 0.7 stack.25
  12.7 0.7 stack.26
  13.4 2.4 copy.53
  15.8 0.0 copy-done.3
  15.8 0.1 copy.54
  15.9 0.7 reshape.80.target_ref
  16.5 0.6 stack.27.refs_3_.norm_ref
  17.2 33.8 %shard_map.424 = (bf16[32,160,1024]{2,1,0:T(8,128)(2,1)}, bf16[32,256]{1,0:T(8,128)(2,1)}, bf16[4,4,192,768]{3,2,1,0:T(8,128)(2,1)}) custom-call(bf16[145,32,1024]{2,1,0:T(8,128)(2,1)} %bitcast.21, bf16[32,1024]{1,0:T(8,128)(2,1)} %refs_11_.1, bf16[1024,256]{1,0:T(8,128)(2,1)} %refs_12_.1, bf16[192,768]{1,0:T(8,128)(2,1)} %bitcast.23, ...), custom_call_target="tpu_custom_call" | custom-call | bytes 20971520 | tf_op jit(solution)/shard_map/pallas_call | solution.py:980
  51.0 36.6 %shard_map.425 = (bf16[1280,2304]{1,0:T(8,128)(2,1)}, bf16[1280,768]{1,0:T(8,128)(2,1)}, f32[1280,768]{1,0:T(8,128)}, f32[1280,1]{1,0:T(8,128)}, bf16[2,4,192,76...) custom-call(s32[32]{0:T(128)} %broadcast_subtract_fusion.refs_0_.bound_ref, ...), custom_call_target="tpu_custom_call" | custom-call | flops 7549747200 | bytes 19660800 | tf_op jit(solution)/shard_map/pallas_call | solution.py:980
  87.6 57.1 %shard_map.426 = (bf16[32,160,1536]{2,1,0:T(8,128)(2,1)}, bf16[1280,768]{1,0:T(8,128)(2,1)}, bf16[1280,768]{1,0:T(8,128)(2,1)}, f32[1280,768]{1,0:T(8,128)}, f32...) custom-call(bf16[32,160,1024]{2,1,0:T(8,128)(2,1)} %get-tuple-element.84.refs_0_.region_ref, ...), custom_call_target="tpu_custom_call" | custom-call | flops 16106127360 | bytes 26214400 | tf_op jit(solution)/shard_map/pallas_call | solution.py:980
  144.6 45.3 %shard_map.427 = (bf16[1280,768]{1,0:T(8,128)(2,1)}, f32[64,1]{1,0:T(8,128)}, f32[64,384]{1,0:T(8,128)}, f32[1280,768]{1,0:T(8,128)}, bf16[768,768]{1,0:T(8,128)...) custom-call(s32[32]{0:T(128)} %broadcast_subtract_fusion.refs_0_.bou, ...), custom_call_target="tpu_custom_call" | custom-call | flops 30198988800 | bytes 19660800 | tf_op jit(solution)/shard_map/pallas_call | solution.py:980
  189.9 0.0 all-reduce.3.cloned.1.call-update
  190.0 0.0 copy-start.2
  190.0 76.7 %shard_map.428 = (bf16[145,32,1024]{2,1,0:T(8,128)(2,1)}, f32[1280,768]{1,0:T(8,128)}, bf16[384,1024]{1,0:T(8,128)(2,1)}, bf16[384,768]{1,0:T(8,128)(2,1)}, f32[1,768]{1,0:T(1,128)}, /*index=5*/f32[1,768]{1,0:T(1,128)}) custom-call(s32[1]{0:T(128)} %bitcast.which_ref, bf16[32,160,1024]{2,1,0:T(8,128)(2,1)} %get-tuple-element.84.refs_0_.region_ref, ...), custom_call_target="tpu_custom_call" | custom-call | flops 24159191040 | bytes 36700160 | tf_op jit(solution)/shard_map/pallas_call | solution.py:980
  266.7 0.0 copy-done.2
  266.7 0.1 reduce
  266.8 0.1 reshape.78
  266.9 0.6 copy.56
  267.5 73.1 %shard_map.429 = (f32[1280,768]{1,0:T(8,128)}, bf16[768,768]{1,0:T(8,128)(2,1)}, bf16[384,1024]{1,0:T(8,128)(2,1)}, bf16[384,768]{1,0:T(8,128)(2,1)}, bf16[128,7...) custom-call(s32[32]{0:T(128)} %broadcast_subtract_fusion.refs_0_.bound_ref, ...), custom_call_target="tpu_custom_call" | custom-call | flops 7549747200 | bytes 19660800 | tf_op jit(solution)/shard_map/pallas_call | solution.py:980
  340.7 0.0 all-reduce.3.cloned.1.call-done
  340.7 0.0 copy-start
  340.7 7.2 %shard_map.430 = (f32[192,768]{1,0:T(8,128)}, f32[192,768]{1,0:T(8,128)}, f32[192,768]{1,0:T(8,128)}, f32[192,768]{1,0:T(8,128)}, f32[192,768]{1,0:T(8,128)}, /*...) custom-call(bf16[768,768]{1,0:T(8,128)(2,1)} %get-tuple-element.117., ...), custom_call_target="tpu_custom_call" | custom-call | bytes 11796480 | tf_op jit(solution)/shard_map/pallas_call | solution.py:980
  347.9 1.9 copy.63
  349.9 0.7 copy.64
  (3 shorter events, 0.0 us)
Async XLA Ops:
  7.2 8.6 %copy-start.3 = (s32[32,2]{0,1:T(2,128)S(1)}, s32[32,2]{0,1:T(2,128)}, u32[]{:S(2)}) copy-start(s32[32,2]{0,1:T(2,128)} %param.29) | copy-start | bytes 772
  7.2 333.5 %all-reduce.3.cloned.1.call-start = ((), (), s32[]{:S(2)}) async-start(), calls=%async_computation | async-start | bytes 5505024 | tf_op jit(solution)/shard_map/psum | solution.py:1325
  190.0 76.7 %copy-start.2 = (f32[64,1]{1,0:T(8,128)S(1)}, f32[64,1]{1,0:T(8,128)}, u32[]{:S(2)}) copy-start(f32[64,1]{1,0:T(8,128)} %get-tuple-element.94) | copy-start | bytes 772
  340.7 7.2 %copy-start = (f32[1280,768]{1,0:T(8,128)S(1)}, f32[1280,768]{1,0:T(8,128)}, u32[]{:S(2)}) copy-start(f32[1280,768]{1,0:T(8,128)} %get-tuple-element.221) | copy-start | bytes 11796484
  347.9 1.9 copy-start.1
Sparse Core Ops, SparseCore 0:
  190.1 66.8 all-reduce.2

commit v3 on v2

--- a/solution.py
+++ b/solution.py
@@ -323,7 +323,7 @@
 
 def attend_forward(query, keys, values, keep):
     probs = attend_probs(spread_heads(query), keys, keep).astype(BF16)
-    return collect_heads(dot_tn(probs, values), query.shape[0])
+    return collect_heads(dot_tn(probs, values), query.shape[0]), probs
 
 
 def split_heads(tensor):
@@ -344,14 +344,14 @@
     return jnp.concatenate(out, axis=1)
 
 
-def attend_backward(query, keys, values, keep, grad_context):
+def attend_backward(query, keys, values, keep, grad_context, kept=None):
     query_blocks = spread_heads(query)
     grad_blocks = spread_heads(grad_context)
-    probs = attend_probs(query_blocks, keys, keep)
+    probs = attend_probs(query_blocks, keys, keep) if kept is None else kept.astype(F32)
     grad_probs = dot_nt(values, grad_blocks)
     inner = jnp.sum(grad_probs * probs, axis=0, keepdims=True)
     grad_scores = (probs * (grad_probs - inner)).astype(BF16)
-    grad_values = dot_nn(probs.astype(BF16), grad_blocks)
+    grad_values = dot_nn(probs.astype(BF16) if kept is None else kept, grad_blocks)
     grad_keys = dot_nn(grad_scores, query_blocks)
     grad_query = collect_heads(dot_tn(grad_scores, keys), query.shape[0]) * 0.125
     return grad_query, grad_keys, grad_values
@@ -409,12 +409,9 @@
             def _(distance=distance):
                 gather.pull(distance)
 
-        @pl.when(step == steps - 3)
+        @pl.when(step == steps - 1)
         def _():
             gather.pair(1)
-
-        @pl.when(step == steps - 1)
-        def _():
             gather.pair(2)
             gather.pair(3)
             gather.finish()
@@ -459,8 +456,6 @@
             @pl.when(step == distance)
             def _(distance=distance):
                 gather.pull(distance)
-                if distance > 1:
-                    gather.pair(distance - 1)
 
     tok = tok_ref[...]
     for part in range(3):
@@ -494,7 +489,8 @@
 
         @pl.when(step == steps - 1)
         def _():
-            gather.pair(3)
+            for distance in range(1, 4):
+                gather.pair(distance)
             for k in range(1, dp_size):
                 embed_copy(k, (dp + dp_size - k) % dp_size, (dp + k) % dp_size).wait_recv()
                 embed_copy(k, dp, (dp + k) % dp_size).wait_send()
@@ -505,8 +501,8 @@
 def cross_forward_kernel(patch_count, length, gathers, count, *refs):
     region_ref, wkv_ref, xhat1_ref, norm_ref, wcq_ref, wout_ref = refs[:6]
     shards, refs = refs[6 : 6 + count], refs[6 + count :]
-    kv_ref, cq_ref, ctx_ref, xhat_ref, rstd_ref = refs[:5]
-    whole, refs = refs[5 : 5 + gathers], refs[5 + gathers :]
+    kv_ref, cq_ref, ctx_ref, xhat_ref, rstd_ref, probs_ref = refs[:6]
+    whole, refs = refs[6 : 6 + gathers], refs[6 + gathers :]
     images, padded, vision = region_ref.shape
     width = cq_ref.shape[1]
     step = pl.program_id(0)
@@ -523,8 +519,6 @@
             @pl.when(step == distance)
             def _(distance=distance):
                 gather.pull(distance)
-                if distance > 1:
-                    gather.pair(distance - 1)
 
     hidden1 = xhat1_ref[...] * norm_ref[0:1] + norm_ref[1:2]
     cq_ref[...] = (dot_nt(hidden1.astype(BF16), wcq_ref[...]) * 0.125).astype(BF16)
@@ -549,7 +543,9 @@
                 image = 2 * index + j
                 keys = kv_ref[image, :, lanes]
                 values = kv_ref[image, :, width + group * GROUP : width + (group + 1) * GROUP]
-                out.append(attend_forward(q[j * length : (j + 1) * length], keys, values, keep))
+                context, probs = attend_forward(q[j * length : (j + 1) * length], keys, values, keep)
+                out.append(context)
+                probs_ref[image, group] = probs
             ctx_ref[span, lanes] = jnp.concatenate(out, axis=0).astype(BF16)
         return carry
 
@@ -562,7 +558,8 @@
 
         @pl.when(step == steps - 1)
         def _():
-            gather.pair(3)
+            for distance in range(1, 4):
+                gather.pair(distance)
             gather.finish()
 
 
@@ -676,7 +673,7 @@
 
 def cross_backward_kernel(
     patch_count, length, which_ref, region_ref, kv_ref, cq_ref, ctx_ref, xhat1_ref, rstd1_ref, norm_ref,
-    dr2_ref, wkv_ref, wout_ref, wcq_ref,
+    dr2_ref, wkv_ref, wout_ref, wcq_ref, probs_ref,
     dregion_ref, dr1_ref, dkv_ref, dqo_ref, dgain_ref, dshift_ref,
     dctx_ref, dq_ref, grads_ref, flat_ref, stage_ref, kv_acc, cq_acc, out_acc, sem,
 ):
@@ -700,7 +697,6 @@
     dx = dr2.astype(BF16)
     dctx_ref[...] = dot_nt(dx, wout_ref[...]).astype(BF16)
     out_acc[...] += dot_tn(ctx_ref[:, mine], dx)
-    keep = lax.broadcasted_iota(jnp.int32, (padded, 4 * length), 0) < patch_count
 
     def pair(index, carry):
         span = pl.ds(pl.multiple_of(index * 2 * length, 16), 2 * length)
@@ -714,7 +710,7 @@
                 image = 2 * index + j
                 at = slice(j * length, (j + 1) * length)
                 dq, dk, dv = attend_backward(
-                    q[at], kv_ref[image, :, lanes], kv_ref[image, :, value_lanes], keep, d[at]
+                    q[at], kv_ref[image, :, lanes], kv_ref[image, :, value_lanes], None, d[at], probs_ref[image, group]
                 )
                 out.append(dq)
                 grads_ref[image, :, lanes] = dk.astype(BF16)
@@ -796,6 +792,7 @@
     refs = refs[5:]
     step = pl.program_id(0)
     steps = pl.num_programs(0)
+    half = steps // 2
     tokens, width = tok_ref.shape
     rows = tokens // length
     own = width // 4
@@ -859,36 +856,39 @@
         for ref in (qkv_acc, out_acc):
             ref[...] = jnp.zeros_like(ref)
 
-    dr1 = dr1_ref[...]
-    da = dr1.astype(BF16)
-    dctx_ref[...] = dot_nt(da, wout_ref[...]).astype(BF16)
-    out_acc[...] += dot_tn(ctx_ref[:, window(which, GROUP)], da)
-
-    def pair(index, carry):
-        span = pl.ds(pl.multiple_of(index * 2 * length, 16), 2 * length)
-        keeps = [row_keep(bound_ref[step * rows + 2 * index + j], length) for j in range(2)]
-        for group in range(width // GROUP):
-            q, k, v = (
-                qkv_ref[span, part * width + group * GROUP : part * width + (group + 1) * GROUP].astype(F32)
-                for part in range(3)
-            )
-            d = dctx_ref[span, group * GROUP : (group + 1) * GROUP].astype(F32)
-            outs = []
-            for j in range(2):
-                at = slice(j * length, (j + 1) * length)
-                outs.append(attend_backward(q[at], k[at].astype(BF16), v[at].astype(BF16), keeps[j], d[at]))
-            for part in range(3):
-                both = jnp.concatenate([outs[0][part], outs[1][part]], axis=0).astype(BF16)
-                grads_ref[span, part * width + group * GROUP : part * width + (group + 1) * GROUP] = both
-        return carry
-
-    lax.fori_loop(0, rows // 2, pair, 0, unroll=4)
-    tok = tok_ref[...]
-    for part in range(3):
-        mine = grads_ref[:, pl.ds(pl.multiple_of(which * 3 // 2 * 128 + part * width, 128), GROUP)]
-        qkv_acc[part] += dot_tn(mine, tok)
-
-    @pl.when(step == steps - 1)
+    @pl.when(step < half)
+    def _():
+        all_rows = pl.ds(pl.multiple_of(step * tokens, 16), tokens)
+        da = dr1_ref[...].astype(BF16)
+        dctx_ref[...] = dot_nt(da, wout_ref[...]).astype(BF16)
+        out_acc[...] += dot_tn(ctx_ref[:, window(which, GROUP)], da)
+
+        def pair(index, carry):
+            span = pl.ds(pl.multiple_of(index * 2 * length, 16), 2 * length)
+            far = pl.ds(pl.multiple_of(step * tokens + index * 2 * length, 16), 2 * length)
+            keeps = [row_keep(bound_ref[step * rows + 2 * index + j], length) for j in range(2)]
+            for group in range(width // GROUP):
+                q, k, v = (
+                    qkv_ref[span, part * width + group * GROUP : part * width + (group + 1) * GROUP].astype(F32)
+                    for part in range(3)
+                )
+                d = dctx_ref[span, group * GROUP : (group + 1) * GROUP].astype(F32)
+                outs = []
+                for j in range(2):
+                    at = slice(j * length, (j + 1) * length)
+                    outs.append(attend_backward(q[at], k[at].astype(BF16), v[at].astype(BF16), keeps[j], d[at]))
+                for part in range(3):
+                    both = jnp.concatenate([outs[0][part], outs[1][part]], axis=0).astype(BF16)
+                    grads_ref[far, part * width + group * GROUP : part * width + (group + 1) * GROUP] = both
+            return carry
+
+        lax.fori_loop(0, rows // 2, pair, 0, unroll=4)
+        tok = tok_ref[...]
+        for part in range(3):
+            mine = grads_ref[all_rows, pl.ds(pl.multiple_of(which * 3 // 2 * 128 + part * width, 128), GROUP)]
+            qkv_acc[part] += dot_tn(mine, tok)
+
+    @pl.when(step == half - 1)
     def _():
         for part in range(3):
             last[part * own : (part + 1) * own, :] = own_rows(qkv_acc[part], which, own).astype(BF16)
@@ -897,19 +897,31 @@
             for reduce in finals:
                 reduce.stage(1)
 
-    dtok_ref[...] = dr1 + dot_nn(grads_ref[...], wqkv_ref[...])
+    @pl.when(step >= half)
+    def _():
+        done = pl.ds(pl.multiple_of((step - half) * tokens, 16), tokens)
+        dtok_ref[...] = dr1_ref[...] + dot_nn(grads_ref[done, :], wqkv_ref[...])
+
+    if sums:
+
+        @pl.when(step == half)
+        def _():
+            image_sum.stage(4)
+            for reduce in finals:
+                reduce.stage(2)
 
     @pl.when(step == steps - 1)
     def _():
         if sums:
-            image_sum.stage(4)
-            for number in range(2, 6):
-                for reduce in finals:
-                    reduce.stage(number)
+            for reduce in finals:
+                reduce.stage(3)
             for reduce in (kv_sum, qo_sum, small_sum, image_sum):
                 reduce.stage(5)
             for reduce, out in zip((kv_sum, qo_sum, small_sum, image_sum), outs, strict=True):
                 out[...] = reduce.done[...]
+            for number in (4, 5):
+                for reduce in finals:
+                    reduce.stage(number)
             last_ref[: 2 * own, :] = finals[0].done[...]
             last_ref[2 * own :, :] = finals[1].done[...]
         else:
@@ -1064,6 +1076,10 @@
     )
 
 
+def probs_spec(width, length, padded):
+    return pl.BlockSpec((TOKEN_ROWS, width // GROUP, padded, 4 * length), lambda i: (i, 0, 0, 0))
+
+
 def run_cross_forward(length, patch_count, region, wkv, xhat1, norms, wcq, wout, shards):
     rows, padded, vision = region.shape
     tokens, width = xhat1.shape
@@ -1086,6 +1102,7 @@
             (rows_of(block, width), shape_of((tokens, width), BF16)),
             (rows_of(block, width), shape_of((tokens, width), F32)),
             (rows_of(block, 1), shape_of((tokens, 1), F32)),
+            (probs_spec(width, length, padded), shape_of((rows, width // GROUP, padded, 4 * length), BF16)),
             *outs,
         ],
         (region, wkv, xhat1, norms, wcq, wout, *flatten(shards)),
@@ -1148,7 +1165,7 @@
     )
 
 
-def run_cross_backward(length, patch_count, which, region, kv, cq, ctx2, xhat1, rstd1, norms, dr2, wkv, wcq, wout):
+def run_cross_backward(length, patch_count, which, region, kv, cq, ctx2, xhat1, rstd1, norms, dr2, wkv, wcq, wout, probs):
     rows, padded, vision = region.shape
     tokens, width = cq.shape
     images = TOKEN_ROWS
@@ -1164,6 +1181,7 @@
             pl.BlockSpec((images, padded, 2 * width), lambda i: (i, 0, 0)),
             rows_of(block, width), rows_of(block, width), rows_of(block, width), rows_of(block, 1), full(norms.shape),
             rows_of(block, width), full((2 * width, vision)), square(width, 1), square(width, 0),
+            probs_spec(width, length, padded),
         ],
         [
             (pl.BlockSpec(memory_space=pl.ANY), shape_of((patch_count, rows, vision), BF16)),
@@ -1173,7 +1191,7 @@
             (fixed((1, width)), shape_of((1, width), F32)),
             (fixed((1, width)), shape_of((1, width), F32)),
         ],
-        (which, region, kv, cq, ctx2, xhat1, rstd1, norms, dr2, wkv, wout, wcq),
+        (which, region, kv, cq, ctx2, xhat1, rstd1, norms, dr2, wkv, wout, wcq, probs),
         scratch=[
             pltpu.VMEM((block, width), BF16),
             pltpu.VMEM((block, width), BF16),
@@ -1193,7 +1211,12 @@
 def run_self_backward(length, dp_size, bound, tok, qkv, ctx1, dr1, selves, others):
     tokens, width = tok.shape
     block = TOKEN_ROWS * length
+    steps = tokens // block
     last = shape_of((width, width), BF16)
+
+    def early(lanes):
+        return pl.BlockSpec((block, lanes), lambda i: (jnp.minimum(i, steps - 1), 0))
+
     extra, outs, scratch = [], [], []
     if others:
         dkv, dqo, _, pack, picture, wimage, *vectors = others
@@ -1210,16 +1233,24 @@
         ]
     return call(
         partial(self_backward_kernel, length, bool(others)),
-        tokens // block,
+        2 * steps,
         [
-            SMEM, rows_of(block, width), rows_of(block, 3 * width), rows_of(block, width), rows_of(block, width),
+            SMEM, early(width), early(3 * width), early(width),
+            pl.BlockSpec((block, width), lambda i: (lax.rem(i, steps), 0)),
             full((3 * width, width)), square(width, 3), *extra,
         ],
-        [(rows_of(block, width), shape_of((tokens, width), F32)), (fixed(last.shape), last), *outs],
+        [
+            (
+                pl.BlockSpec((block, width), lambda i: (jnp.maximum(i - steps, 0), 0)),
+                shape_of((tokens, width), F32),
+            ),
+            (fixed(last.shape), last),
+            *outs,
+        ],
         (bound, tok, qkv, ctx1, dr1, selves, selves, *others),
         scratch=[
             pltpu.VMEM((block, width), BF16),
-            pltpu.VMEM((block, 3 * width), BF16),
+            pltpu.VMEM((tokens, 3 * width), BF16),
             pltpu.VMEM((3, GROUP, width), F32),
             pltpu.VMEM((GROUP, width), F32),
             pltpu.VMEM(last.shape, BF16),
@@ -1311,7 +1342,7 @@
         image_all = lax.all_gather(image_own, "dp", axis=0, tiled=True)
     crosses = crosses.reshape(-1, width)
     wkv = wides.reshape(-1, vision)
-    kv, cq, ctx2, xhat2, rstd2, *found = run_cross_forward(
+    kv, cq, ctx2, xhat2, rstd2, probs, *found = run_cross_forward(
         length, patch_count, region, wkv, xhat1, norms, crosses, crosses, each(ffns)
     )
     ffns = (found[0] if local else lax.all_gather(jnp.stack(ffns), "mp", axis=1)).reshape(-1, width)
@@ -1325,7 +1356,7 @@
     dp_sum = lambda grad: lax.psum(grad, "dp")
     dup, ddown, dtext = dp_sum((dup, ddown, dtext))
     dregion, dr1, dkv, dqo, dgain1, dshift1 = run_cross_backward(
-        length, patch_count, which, region, kv, cq, ctx2, xhat1, rstd1, norms, dr2, wkv, crosses, crosses
+        length, patch_count, which, region, kv, cq, ctx2, xhat1, rstd1, norms, dr2, wkv, crosses, crosses, probs
     )
     vectors = (dgain1, dshift1, dgain2, dshift2, dgain3, dshift3, dtemp)
     pictures = (picture_global_feature, picture_mapping_factor)

time: 364 us -> 350 us (0.962)
  the two profiles are of different devices: /device:TPU:17 before, /device:TPU:0 now
where the time goes in v3:
time: 350 us; the launch traced here: 344 us
  Pallas kernels  316 us (90%)
  between operations  15 us (4%)
  local copies, waits for them, and re-layouts  11.3 us (3%)
    pallas_call x7, Pallas kernels, call(): pl.pallas_call(kernel, grid=(steps,), in_specs=list(ins), out_specs=list(...  316 us
  transfers between devices with their start and end apart: 1, of which 0 were waited for; matrix products, arithmetic and copies ran while one was open for 0% of the time, Pallas kernels for 40%

profile of v3, /device:TPU:0, one launch (start us, length us, event | category | flops | bytes accessed | tf_op | source)
XLA Modules:
  0.0 343.7 jit_solution(6060296440953967473)
XLA Ops:
  7.2 0.0 copy-start.3
  7.2 0.0 all-reduce.3.cloned.1.call-start
  7.3 0.8 reduce_sum.9
  8.1 0.5 broadcast_subtract_fusion.refs_0_.bound_ref
  9.3 0.7 stack.21
  9.9 0.7 stack.22
  10.6 0.7 stack.23
  11.3 0.7 stack.24
  12.0 0.7 stack.25
  12.7 0.7 stack.26
  13.4 2.4 copy.53
  15.8 0.0 copy-done.3
  15.8 0.1 copy.54
  15.9 0.7 reshape.80.target_ref
  16.5 0.6 stack.27.refs_3_.norm_ref
  17.2 35.1 %shard_map.424 = (bf16[32,160,1024]{2,1,0:T(8,128)(2,1)}, bf16[32,256]{1,0:T(8,128)(2,1)}, bf16[4,4,192,768]{3,2,1,0:T(8,128)(2,1)}) custom-call(bf16[145,32,1024]{2,1,0:T(8,128)(2,1)} %bitcast.21, bf16[32,1024]{1,0:T(8,128)(2,1)} %refs_11_.1, bf16[1024,256]{1,0:T(8,128)(2,1)} %refs_12_.1, bf16[192,768]{1,0:T(8,128)(2,1)} %bitcast.23, ...), custom_call_target="tpu_custom_call" | custom-call | bytes 20971520 | tf_op jit(solution)/shard_map/pallas_call | solution.py:992
  52.3 34.9 %shard_map.425 = (bf16[1280,2304]{1,0:T(8,128)(2,1)}, bf16[1280,768]{1,0:T(8,128)(2,1)}, f32[1280,768]{1,0:T(8,128)}, f32[1280,1]{1,0:T(8,128)}, bf16[2,4,192,76...) custom-call(s32[32]{0:T(128)} %broadcast_subtract_fusion.refs_0_.bound_ref, ...), custom_call_target="tpu_custom_call" | custom-call | flops 7549747200 | bytes 19660800 | tf_op jit(solution)/shard_map/pallas_call | solution.py:992
  87.2 56.8 %shard_map.426 = (bf16[32,160,1536]{2,1,0:T(8,128)(2,1)}, bf16[1280,768]{1,0:T(8,128)(2,1)}, bf16[1280,768]{1,0:T(8,128)(2,1)}, f32[1280,768]{1,0:T(8,128)}, f32...) custom-call(bf16[32,160,1024]{2,1,0:T(8,128)(2,1)} %get-tuple-element.85.refs_0_.region_ref, ...), custom_call_target="tpu_custom_call" | custom-call | flops 16106127360 | bytes 26214400 | tf_op jit(solution)/shard_map/pallas_call | solution.py:992
  144.0 45.2 %shard_map.427 = (bf16[1280,768]{1,0:T(8,128)(2,1)}, f32[64,1]{1,0:T(8,128)}, f32[64,384]{1,0:T(8,128)}, f32[1280,768]{1,0:T(8,128)}, bf16[768,768]{1,0:T(8,128)...) custom-call(s32[32]{0:T(128)} %broadcast_subtract_fusion.refs_0_.bou, ...), custom_call_target="tpu_custom_call" | custom-call | flops 30198988800 | bytes 19660800 | tf_op jit(solution)/shard_map/pallas_call | solution.py:992
  189.2 0.0 all-reduce.3.cloned.1.call-update
  189.2 0.0 copy-start.2
  189.2 69.0 %shard_map.428 = (bf16[145,32,1024]{2,1,0:T(8,128)(2,1)}, f32[1280,768]{1,0:T(8,128)}, bf16[384,1024]{1,0:T(8,128)(2,1)}, bf16[384,768]{1,0:T(8,128)(2,1)}, f32[1,768]{1,0:T(1,128)}, /*index=5*/f32[1,768]{1,0:T(1,128)}) custom-call(s32[1]{0:T(128)} %bitcast.which_ref, bf16[32,160,1024]{2,1,0:T(8,128)(2,1)} %get-tuple-element.85.refs_0_.region_ref, ...), custom_call_target="tpu_custom_call" | custom-call | flops 24159191040 | bytes 36700160 | tf_op jit(solution)/shard_map/pallas_call | solution.py:992
  258.2 0.0 copy-done.2
  258.2 0.1 reduce
  258.3 0.1 reshape.78
  258.4 0.6 copy.56
  259.1 67.7 %shard_map.429 = (f32[1280,768]{1,0:T(8,128)}, bf16[768,768]{1,0:T(8,128)(2,1)}, bf16[384,1024]{1,0:T(8,128)(2,1)}, bf16[384,768]{1,0:T(8,128)(2,1)}, bf16[128,7...) custom-call(s32[32]{0:T(128)} %broadcast_subtract_fusion.refs_0_.bound_ref, ...), custom_call_target="tpu_custom_call" | custom-call | flops 7549747200 | bytes 19660800 | tf_op jit(solution)/shard_map/pallas_call | solution.py:992
  326.8 0.0 all-reduce.3.cloned.1.call-done
  326.8 0.0 copy-start
  326.8 7.2 %shard_map.430 = (f32[192,768]{1,0:T(8,128)}, f32[192,768]{1,0:T(8,128)}, f32[192,768]{1,0:T(8,128)}, f32[192,768]{1,0:T(8,128)}, f32[192,768]{1,0:T(8,128)}, /*...) custom-call(bf16[768,768]{1,0:T(8,128)(2,1)} %get-tuple-element.119., ...), custom_call_target="tpu_custom_call" | custom-call | bytes 11796480 | tf_op jit(solution)/shard_map/pallas_call | solution.py:992
  334.0 1.9 copy.63
  336.0 0.7 copy.64
  (3 shorter events, 0.0 us)
Async XLA Ops:
  7.2 8.6 %copy-start.3 = (s32[32,2]{0,1:T(2,128)S(1)}, s32[32,2]{0,1:T(2,128)}, u32[]{:S(2)}) copy-start(s32[32,2]{0,1:T(2,128)} %param.29) | copy-start | bytes 772
  7.2 319.6 %all-reduce.3.cloned.1.call-start = ((), (), s32[]{:S(2)}) async-start(), calls=%async_computation | async-start | bytes 5505024 | tf_op jit(solution)/shard_map/psum | solution.py:1356
  189.2 69.0 %copy-start.2 = (f32[64,1]{1,0:T(8,128)S(1)}, f32[64,1]{1,0:T(8,128)}, u32[]{:S(2)}) copy-start(f32[64,1]{1,0:T(8,128)} %get-tuple-element.95) | copy-start | bytes 772
  326.8 7.2 %copy-start = (f32[1280,768]{1,0:T(8,128)S(1)}, f32[1280,768]{1,0:T(8,128)}, u32[]{:S(2)}) copy-start(f32[1280,768]{1,0:T(8,128)} %get-tuple-element.223) | copy-start | bytes 11796484
  334.0 1.9 copy-start.1
Sparse Core Ops, SparseCore 0:
  189.3 65.2 all-reduce.2

commit v4 on v3

--- a/solution.py
+++ b/solution.py
@@ -54,8 +54,10 @@
 
 
 class Gather:
-    def __init__(self, shards, outs, refs):
+    def __init__(self, shards, outs, refs, split=1):
         count = len(outs)
+        self.units = [(array, piece) for array in range(count) for piece in range(split)]
+        self.split = split
         self.ins, self.outs, self.shards, sems = refs[:count], outs, shards, refs[count:]
         self.local, self.up, self.down, self.across, self.below, self.above, self.near, self.out, self.back = sems
         self.dp, self.z = lax.axis_index("dp"), lax.axis_index("mp")
@@ -91,10 +93,15 @@
     def inside(self, z):
         return (z >= 0) & (z < self.depth)
 
+    def tall(self, index):
+        return self.ins[self.units[index][0]].shape[1] // self.split
+
     def part(self, index, source, first, size, core=None):
-        mats = self.ins[index].shape[0] // 2
+        array, piece = self.units[index]
+        mats = self.ins[array].shape[0] // 2
         core = self.core if core is None else core
-        return self.outs[index].at[pl.ds(core * mats, mats), source, pl.ds(pl.multiple_of(first, 16), size), :]
+        first = pl.multiple_of(piece * self.tall(index) + first, 16)
+        return self.outs[array].at[pl.ds(core * mats, mats), source, pl.ds(first, size), :]
 
     def copy(self, src, dst, send, recv, to):
         return pltpu.make_async_remote_copy(
@@ -102,7 +109,7 @@
         )
 
     def span(self, index):
-        tall = self.ins[index].shape[1]
+        tall = self.tall(index)
         return self.color * (tall // 2) + self.y * (tall // 6), tall // 3
 
     def hop(self, index, source, step):
@@ -112,14 +119,16 @@
 
     def first_hop(self, index, step):
         first, size = self.span(index)
-        mats = self.ins[index].shape[0] // 2
-        src = self.ins[index].at[pl.ds(self.core * mats, mats), pl.ds(pl.multiple_of(first, 16), size), :]
+        array, piece = self.units[index]
+        mats = self.ins[array].shape[0] // 2
+        begin = pl.multiple_of(piece * self.tall(index) + first, 16)
+        src = self.ins[array].at[pl.ds(self.core * mats, mats), pl.ds(begin, size), :]
         send, recv = (self.up, self.below) if step > 0 else (self.down, self.above)
         spot = self.part(index, self.z, first, size)
         return self.copy(src, spot, send.at[index, self.z], recv.at[index, self.z], (self.dp, self.z + step))
 
     def side(self, index, source, which, inward=False):
-        tall = self.ins[index].shape[1]
+        tall = self.tall(index)
         color, y = self.color, self.y
         if inward:
             color, y = (1 - color, y) if which == 0 else (1 - color, 1 - y) if which == 1 else (color, 1 - y)
@@ -130,11 +139,14 @@
 
     def pass_on(self, index, source, inward=False):
         core = 1 - self.core if inward else self.core
-        spot = self.part(index, source, 0, self.ins[index].shape[1], core)
+        spot = self.part(index, source, 0, self.tall(index), core)
         return self.copy(spot, spot, self.out.at[index, source], self.back.at[index, source], self.twin)
 
     def keep(self, index):
-        return pltpu.make_async_copy(self.ins[index], self.outs[index].at[:, self.z], self.local.at[index])
+        array, piece = self.units[index]
+        rows = pl.ds(piece * self.tall(index), self.tall(index))
+        spot = self.outs[array].at[:, self.z, rows, :]
+        return pltpu.make_async_copy(self.ins[array].at[:, rows, :], spot, self.local.at[index])
 
     def start(self, everyone=0):
         count = 0
@@ -143,7 +155,7 @@
                 stack[index] = self.shards[count][...]
                 count += 1
         self.enter(everyone)
-        for index in range(len(self.ins)):
+        for index in range(len(self.units)):
             for step in (1, -1):
 
                 @pl.when(self.inside(self.z + step))
@@ -152,8 +164,8 @@
 
             self.keep(index).start()
 
-    def each(self, distance, what):
-        for index in range(len(self.ins)):
+    def each(self, distance, what, only=None):
+        for index in range(len(self.units)) if only is None else (only,):
             for step in (1, -1):
                 source = self.z - step * distance
 
@@ -161,7 +173,7 @@
                 def _(index=index, step=step, source=source):
                     what(index, step, source)
 
-    def pull(self, distance):
+    def pull(self, distance, only=None):
         def what(index, step, source):
             self.hop(index, source, step).wait_recv()
 
@@ -172,7 +184,7 @@
             for which in range(3):
                 self.side(index, source, which).start()
 
-        self.each(distance, what)
+        self.each(distance, what, only)
 
     def pair(self, distance):
         def what(index, step, source):
@@ -195,7 +207,7 @@
 
         for distance in range(1, self.depth):
             self.each(distance, what)
-        for index in range(len(self.ins)):
+        for index in range(len(self.units)):
             for step in (1, -1):
 
                 @pl.when(self.inside(self.z + step))
@@ -292,6 +304,9 @@
             self.back(self.core).wait_send()
 
 
+ARRIVALS = ((1, 0), (1, 1), (2, 0), (2, 1), (3, 0), (3, 1))
+
+
 def spread_heads(tensor):
     count = tensor.shape[0]
     left = lax.broadcasted_iota(jnp.int32, (count, 2 * HEAD), 1) < HEAD
@@ -403,11 +418,11 @@
 
     if gather:
 
-        for late, distance in ((6, 1), (4, 2), (2, 3)):
-
-            @pl.when(step == steps - late)
-            def _(distance=distance):
-                gather.pull(distance)
+        for place, arrival in enumerate(ARRIVALS):
+
+            @pl.when(step == place + 1)
+            def _(arrival=arrival):
+                gather.pull(*arrival)
 
         @pl.when(step == steps - 1)
         def _():
@@ -418,8 +433,8 @@
 
 
 def self_forward_kernel(length, gathers, count, *refs):
-    bound_ref, tok_ref, wqkv_ref, wout_ref, embed_ref = refs[:5]
-    shards, refs = refs[5 : 5 + count], refs[5 + count :]
+    bound_ref, tok_ref, wqk_ref, wv_ref, wout_ref, embed_ref = refs[:6]
+    shards, refs = refs[6 : 6 + count], refs[6 + count :]
     qkv_ref, ctx_ref, xhat_ref, rstd_ref = refs[:4]
     whole, refs = refs[4 : 4 + gathers], refs[4 + gathers :]
     width = tok_ref.shape[1]
@@ -455,14 +470,21 @@
 
             @pl.when(step == distance)
             def _(distance=distance):
-                gather.pull(distance)
+                gather.pull(distance, 1 if distance == 3 else None)
 
     tok = tok_ref[...]
     for part in range(3):
-        proj = dot_nt(tok, wqkv_ref[part * width : (part + 1) * width, :])
+        weight = wv_ref[...] if part == 2 else wqk_ref[part * width : (part + 1) * width, :]
+        proj = dot_nt(tok, weight)
         if part == 0:
             proj = proj * 0.125
         qkv_ref[:, part * width : (part + 1) * width] = proj.astype(BF16)
+
+    if gathers:
+
+        @pl.when(step == 2)
+        def _():
+            gather.pull(3, 0)
 
     def pair(index, carry):
         span = pl.ds(pl.multiple_of(index * 2 * length, 16), 2 * length)
@@ -507,18 +529,18 @@
     width = cq_ref.shape[1]
     step = pl.program_id(0)
     steps = pl.num_programs(0)
-    gather = Gather(shards, whole, refs) if gathers else None
+    gather = Gather(shards, whole, refs, split=2) if gathers else None
     if gathers:
 
         @pl.when(step == 0)
         def _():
             gather.start()
 
-        for distance in range(1, 4):
-
-            @pl.when(step == distance)
-            def _(distance=distance):
-                gather.pull(distance)
+        for place, arrival in enumerate(ARRIVALS[1::2]):
+
+            @pl.when(step == place + 1)
+            def _(arrival=arrival):
+                gather.pull(*arrival)
 
     hidden1 = xhat1_ref[...] * norm_ref[0:1] + norm_ref[1:2]
     cq_ref[...] = (dot_nt(hidden1.astype(BF16), wcq_ref[...]) * 0.125).astype(BF16)
@@ -531,6 +553,13 @@
         return carry
 
     lax.fori_loop(0, 2 * width // 512, chunk, 0, unroll=True)
+    if gathers:
+        for place, arrival in enumerate(ARRIVALS[::2]):
+
+            @pl.when(step == place)
+            def _(arrival=arrival):
+                gather.pull(*arrival)
+
     keep = lax.broadcasted_iota(jnp.int32, (padded, 4 * length), 0) < patch_count
 
     def pair(index, carry):
@@ -779,8 +808,8 @@
 
 
 def self_backward_kernel(length, sums, *refs):
-    bound_ref, tok_ref, qkv_ref, ctx_ref, dr1_ref, wqkv_ref, wout_ref = refs[:7]
-    refs = refs[7:]
+    bound_ref, tok_ref, qkv_ref, ctx_ref, dr1_ref, wqk_ref, wv_ref, wout_ref = refs[:8]
+    refs = refs[8:]
     if sums:
         dkv_ref, dqo_ref, temp_ref, pack_ref, picture_ref, wimage_ref = refs[:6]
         vectors, refs = refs[6:13], refs[13:]
@@ -900,7 +929,8 @@
     @pl.when(step >= half)
     def _():
         done = pl.ds(pl.multiple_of((step - half) * tokens, 16), tokens)
-        dtok_ref[...] = dr1_ref[...] + dot_nn(grads_ref[done, :], wqkv_ref[...])
+        part = dr1_ref[...] + dot_nn(grads_ref[done, : 2 * width], wqk_ref[...])
+        dtok_ref[...] = part + dot_nn(grads_ref[done, 2 * width :], wv_ref[...])
 
     if sums:
 
@@ -1006,14 +1036,14 @@
 DEPTH = 4
 
 
-def gathered(groups):
+def gathered(groups, split=1):
     shapes = [(len(group), *group[0].shape) for group in groups]
     outs = [
         (pl.BlockSpec(memory_space=pl.ANY), shape_of((shape[0], DEPTH, *shape[1:]), BF16)) for shape in shapes
     ]
     scratch = [pltpu.VMEM(shape, BF16) for shape in shapes]
     specs = [full(shard.shape) for group in groups for shard in group]
-    return specs, outs, [*scratch, *Gather.semaphores(len(groups), DEPTH)] if groups else []
+    return specs, outs, [*scratch, *Gather.semaphores(len(groups) * split, DEPTH)] if groups else []
 
 
 def flatten(groups):
@@ -1049,7 +1079,7 @@
     )
 
 
-def run_self_forward(length, dp_size, bound, tok, squares, embed, shards):
+def run_self_forward(length, dp_size, bound, tok, weights, embed, shards):
     tokens, width = tok.shape
     block = TOKEN_ROWS * length
     specs, outs, sems = gathered(shards)
@@ -1060,7 +1090,7 @@
     return call(
         partial(self_forward_kernel, length, len(shards), len(flatten(shards))),
         tokens // block,
-        [SMEM, rows_of(block, width), full((3 * width, width)), square(width, 3), full(embed.shape), *specs],
+        [SMEM, rows_of(block, width), full((2 * width, width)), square(width, 0), square(width, 1), full(embed.shape), *specs],
         [
             (rows_of(block, 3 * width), shape_of((tokens, 3 * width), BF16)),
             (rows_of(block, width), shape_of((tokens, width), BF16)),
@@ -1068,7 +1098,7 @@
             (rows_of(block, 1), shape_of((tokens, 1), F32)),
             *outs,
         ],
-        (bound, tok, squares, squares, embed, *flatten(shards)),
+        (bound, tok, weights[0], weights[1], weights[1], embed, *flatten(shards)),
         scratch=sems,
         flops=10 * tokens * width * width,
         moved=20 * tokens * width,
@@ -1085,7 +1115,7 @@
     tokens, width = xhat1.shape
     images = TOKEN_ROWS
     block = images * length
-    specs, outs, sems = gathered(shards)
+    specs, outs, sems = gathered(shards, split=2)
     return call(
         partial(cross_forward_kernel, patch_count, length, len(shards), len(flatten(shards))),
         rows // images,
@@ -1208,7 +1238,7 @@
     )
 
 
-def run_self_backward(length, dp_size, bound, tok, qkv, ctx1, dr1, selves, others):
+def run_self_backward(length, dp_size, bound, tok, qkv, ctx1, dr1, weights, others):
     tokens, width = tok.shape
     block = TOKEN_ROWS * length
     steps = tokens // block
@@ -1237,7 +1267,7 @@
         [
             SMEM, early(width), early(3 * width), early(width),
             pl.BlockSpec((block, width), lambda i: (lax.rem(i, steps), 0)),
-            full((3 * width, width)), square(width, 3), *extra,
+            full((2 * width, width)), square(width, 0), square(width, 1), *extra,
         ],
         [
             (
@@ -1247,7 +1277,7 @@
             (fixed(last.shape), last),
             *outs,
         ],
-        (bound, tok, qkv, ctx1, dr1, selves, selves, *others),
+        (bound, tok, qkv, ctx1, dr1, weights[0], weights[1], weights[1], *others),
         scratch=[
             pltpu.VMEM((block, width), BF16),
             pltpu.VMEM((tokens, 3 * width), BF16),
@@ -1320,7 +1350,7 @@
         middle_standardize_offset, final_standardize_scale, final_standardize_offset,
     ])
 
-    selves = (intra_asking_map.T, intra_lookup_map.T, intra_content_map.T, intra_attend_exit_map)
+    selves = [(intra_asking_map.T, intra_lookup_map.T), (intra_content_map.T, intra_attend_exit_map)]
     crosses = (visual_asking_map.T, visual_attend_exit_map)
     wides = (visual_lookup_map.T, visual_content_map.T)
     ffns = (mlp_widening_factor.T, mlp_narrowing_factor)
@@ -1330,8 +1360,9 @@
     def each(*shards):
         return list(shards) if local else []
 
-    region, image_own, *found = run_prep(region, picture_global_feature, picture_mapping_factor, each(selves))
-    selves = (found[0] if local else lax.all_gather(jnp.stack(selves), "mp", axis=1)).reshape(-1, width)
+    region, image_own, *found = run_prep(region, picture_global_feature, picture_mapping_factor, each(*selves))
+    selves = found if local else [lax.all_gather(jnp.stack(pair), "mp", axis=1) for pair in selves]
+    selves = [pair.reshape(-1, width) for pair in selves]
     qkv, ctx1, xhat1, rstd1, *found = run_self_forward(
         length, dp_size, bound, word_features, selves, image_own, each(crosses, wides)
     )

time: 350 us -> 344 us (0.983)
  Pallas kernels: 316 us -> 310 us
    pallas_call x7, Pallas kernels: 316 us -> 310 us  [call(): pl.pallas_call(kernel, grid=(steps,), in_specs=list(ins), out_specs=list(...]
where the time goes in v4:
time: 344 us; the launch traced here: 338 us
  Pallas kernels  310 us (90%)
  between operations  15.1 us (4%)
  local copies, waits for them, and re-layouts  11.3 us (3%)
    pallas_call x7, Pallas kernels, call(): pl.pallas_call(kernel, grid=(steps,), in_specs=list(ins), out_specs=list(...  310 us
  transfers between devices with their start and end apart: 1, of which 0 were waited for; matrix products, arithmetic and copies ran while one was open for 0% of the time, Pallas kernels for 40%

profile of v4, /device:TPU:0, one launch (start us, length us, event | category | flops | bytes accessed | tf_op | source)
XLA Modules:
  0.0 337.6 jit_solution(2515396545796517321)
XLA Ops:
  7.2 0.0 copy-start.3
  7.2 0.0 all-reduce.3.cloned.1.call-start
  7.3 0.8 reduce_sum.9
  8.1 0.5 broadcast_subtract_fusion.refs_0_.bound_ref
  9.3 0.7 stack.21
  9.9 0.7 stack.22
  10.6 0.7 stack.23
  11.3 0.7 stack.24
  12.0 0.7 stack.25
  12.7 0.7 stack.26
  13.4 2.4 copy.53
  15.8 0.0 copy-done.3
  15.8 0.1 copy.54
  15.9 0.7 reshape.84.target_ref
  16.5 0.6 stack.27.refs_3_.norm_ref
  17.2 32.6 %shard_map.424 = (bf16[32,160,1024]{2,1,0:T(8,128)(2,1)}, bf16[32,256]{1,0:T(8,128)(2,1)}, bf16[2,4,192,768]{3,2,1,0:T(8,128)(2,1)}, bf16[2,4,192,768]{3,2,1,0:T(8,128)(2,1)}) custom-call(bf16[145,32,1024]{2,1,0:T(8,128)(2,1)} %bitcast.22, bf16[32,1024]{1,0:T(8,128)(2,1)} %refs_12_.1, bf16[1024,256]{1,0:T(8,128)(2,1)} %refs_13_.1, ...), custom_call_target="tpu_custom_call" | custom-call | bytes 20971520 | tf_op jit(solution)/shard_map/pallas_call | solution.py:1022
  49.8 36.1 %shard_map.425 = (bf16[1280,2304]{1,0:T(8,128)(2,1)}, bf16[1280,768]{1,0:T(8,128)(2,1)}, f32[1280,768]{1,0:T(8,128)}, f32[1280,1]{1,0:T(8,128)}, bf16[2,4,192,76...) custom-call(s32[32]{0:T(128)} %broadcast_subtract_fusion.refs_0_.bound_ref, ...), custom_call_target="tpu_custom_call" | custom-call | flops 7549747200 | bytes 19660800 | tf_op jit(solution)/shard_map/pallas_call | solution.py:1022
  85.9 52.1 %shard_map.426 = (bf16[32,160,1536]{2,1,0:T(8,128)(2,1)}, bf16[1280,768]{1,0:T(8,128)(2,1)}, bf16[1280,768]{1,0:T(8,128)(2,1)}, f32[1280,768]{1,0:T(8,128)}, f32...) custom-call(bf16[32,160,1024]{2,1,0:T(8,128)(2,1)} %get-tuple-element.86.refs_0_.region_ref, ...), custom_call_target="tpu_custom_call" | custom-call | flops 16106127360 | bytes 26214400 | tf_op jit(solution)/shard_map/pallas_call | solution.py:1022
  138.0 45.2 %shard_map.427 = (bf16[1280,768]{1,0:T(8,128)(2,1)}, f32[64,1]{1,0:T(8,128)}, f32[64,384]{1,0:T(8,128)}, f32[1280,768]{1,0:T(8,128)}, bf16[768,768]{1,0:T(8,128)...) custom-call(s32[32]{0:T(128)} %broadcast_subtract_fusion.refs_0_.bou, ...), custom_call_target="tpu_custom_call" | custom-call | flops 30198988800 | bytes 19660800 | tf_op jit(solution)/shard_map/pallas_call | solution.py:1022
  183.2 0.0 all-reduce.3.cloned.1.call-update
  183.2 0.0 copy-start.2
  183.2 69.0 %shard_map.428 = (bf16[145,32,1024]{2,1,0:T(8,128)(2,1)}, f32[1280,768]{1,0:T(8,128)}, bf16[384,1024]{1,0:T(8,128)(2,1)}, bf16[384,768]{1,0:T(8,128)(2,1)}, f32[1,768]{1,0:T(1,128)}, /*index=5*/f32[1,768]{1,0:T(1,128)}) custom-call(s32[1]{0:T(128)} %bitcast.which_ref, bf16[32,160,1024]{2,1,0:T(8,128)(2,1)} %get-tuple-element.86.refs_0_.region_ref, ...), custom_call_target="tpu_custom_call" | custom-call | flops 24159191040 | bytes 36700160 | tf_op jit(solution)/shard_map/pallas_call | solution.py:1022
  252.2 0.0 copy-done.2
  252.3 0.1 reduce
  252.4 0.1 reshape.82
  252.5 0.6 copy.56
  253.1 67.5 %shard_map.429 = (f32[1280,768]{1,0:T(8,128)}, bf16[768,768]{1,0:T(8,128)(2,1)}, bf16[384,1024]{1,0:T(8,128)(2,1)}, bf16[384,768]{1,0:T(8,128)(2,1)}, bf16[128,7...) custom-call(s32[32]{0:T(128)} %broadcast_subtract_fusion.refs_0_.bound_ref, ...), custom_call_target="tpu_custom_call" | custom-call | flops 7549747200 | bytes 19660800 | tf_op jit(solution)/shard_map/pallas_call | solution.py:1022
  320.6 0.0 all-reduce.3.cloned.1.call-done
  320.7 7.2 %shard_map.430 = (f32[192,768]{1,0:T(8,128)}, f32[192,768]{1,0:T(8,128)}, f32[192,768]{1,0:T(8,128)}, f32[192,768]{1,0:T(8,128)}, f32[192,768]{1,0:T(8,128)}, /*...) custom-call(bf16[768,768]{1,0:T(8,128)(2,1)} %get-tuple-element.121., ...), custom_call_target="tpu_custom_call" | custom-call | bytes 11796480 | tf_op jit(solution)/shard_map/pallas_call | solution.py:1022
  327.9 1.9 copy.63
  329.8 0.0 copy-done.1
  329.8 0.7 copy.64
  (3 shorter events, 0.0 us)
Async XLA Ops:
  7.2 8.6 %copy-start.3 = (s32[32,2]{0,1:T(2,128)S(1)}, s32[32,2]{0,1:T(2,128)}, u32[]{:S(2)}) copy-start(s32[32,2]{0,1:T(2,128)} %param.29) | copy-start | bytes 772
  7.2 313.5 %all-reduce.3.cloned.1.call-start = ((), (), s32[]{:S(2)}) async-start(), calls=%async_computation | async-start | bytes 5505024 | tf_op jit(solution)/shard_map/psum | solution.py:1387
  183.2 69.0 %copy-start.2 = (f32[64,1]{1,0:T(8,128)S(1)}, f32[64,1]{1,0:T(8,128)}, u32[]{:S(2)}) copy-start(f32[64,1]{1,0:T(8,128)} %get-tuple-element.97) | copy-start | bytes 772
  320.7 7.2 %copy-start = (f32[1280,768]{1,0:T(8,128)S(1)}, f32[1280,768]{1,0:T(8,128)}, u32[]{:S(2)}) copy-start(f32[1280,768]{1,0:T(8,128)} %get-tuple-element.225) | copy-start | bytes 11796484
  327.9 1.9 copy-start.1
Sparse Core Ops, SparseCore 0:
  183.3 64.8 all-reduce.2

commit v5 on v4

--- a/solution.py
+++ b/solution.py
@@ -749,7 +749,7 @@
 
     lax.fori_loop(0, images // 2, pair, 0, unroll=4)
 
-    some = 4
+    some = images
     for index in range(images // some):
         grads = grads_ref[index * some : (index + 1) * some].reshape(some * padded, 2 * width)
         dregion = dot_nn(grads, wkv_ref[...])
@@ -1345,10 +1345,10 @@
     which = lax.axis_index("mp").astype(jnp.int32).reshape(1)
     bound = (length - jnp.sum(sentence_numbering, axis=1)).astype(jnp.int32)
     target = matched_picture.reshape(-1, 1)
-    norms = jnp.stack([
+    norms = jnp.concatenate([
         initial_standardize_scale, initial_standardize_offset, middle_standardize_scale,
         middle_standardize_offset, final_standardize_scale, final_standardize_offset,
-    ])
+    ]).reshape(6, width)
 
     selves = [(intra_asking_map.T, intra_lookup_map.T), (intra_content_map.T, intra_attend_exit_map)]
     crosses = (visual_asking_map.T, visual_attend_exit_map)

time: 344 us -> 345 us (level)
    another operation x7 -> x0, local copies, waits for them, and re-layouts: 4.78 us -> none  [body(): jnp.stack([initial_standardize_scale, initial_standardize_offset, middle_...]
    unnamed x13 -> x18, local copies, waits for them, and re-layouts: 5.7 us -> 9.16 us
  transfers between devices with their start and end apart: 1 -> 1, of which waited for: 0 -> 0; matrix products, arithmetic and copies ran while one was open for 0% -> 0% of each run, Pallas kernels for 40% -> 41%
where the time goes in v5:
time: 345 us; the launch traced here: 338 us
  Pallas kernels  310 us (90%)
  between operations  15.1 us (4%)
  local copies, waits for them, and re-layouts  11.3 us (3%)
    pallas_call x7, Pallas kernels, call(): pl.pallas_call(kernel, grid=(steps,), in_specs=list(ins), out_specs=list(...  310 us
    unnamed x18, local copies, waits for them, and re-layouts  9.16 us
  transfers between devices with their start and end apart: 1, of which 0 were waited for; matrix products, arithmetic and copies ran while one was open for 0% of the time, Pallas kernels for 41%

profile of v5, /device:TPU:0, one launch (start us, length us, event | category | flops | bytes accessed | tf_op | source)
XLA Modules:
  0.0 338.2 jit_solution(5818404958902747920)
XLA Ops:
  7.2 0.0 copy-start.3
  7.2 0.0 all-reduce.3.cloned.1.call-start
  7.3 0.8 reduce_sum.9
  8.1 0.5 broadcast_subtract_fusion.refs_0_.bound_ref
  9.3 0.7 constant_dynamic-update-slice_fusion.5
  10.0 0.7 constant_dynamic-update-slice_fusion.4
  10.7 0.7 constant_dynamic-update-slice_fusion.3
  11.3 0.7 constant_dynamic-update-slice_fusion.2
  12.0 0.7 constant_dynamic-update-slice_fusion.1
  12.7 0.7 constant_dynamic-update-slice_fusion
  13.4 0.6 reshape.82.refs_3_.norm_ref
  14.0 2.4 copy.53
  16.4 0.0 copy-done.3
  16.4 0.1 copy.54
  16.5 0.7 reshape.88.target_ref
  17.2 32.6 %shard_map.424 = (bf16[32,160,1024]{2,1,0:T(8,128)(2,1)}, bf16[32,256]{1,0:T(8,128)(2,1)}, bf16[2,4,192,768]{3,2,1,0:T(8,128)(2,1)}, bf16[2,4,192,768]{3,2,1,0:T(8,128)(2,1)}) custom-call(bf16[145,32,1024]{2,1,0:T(8,128)(2,1)} %bitcast.22, bf16[32,1024]{1,0:T(8,128)(2,1)} %refs_12_.1, bf16[1024,256]{1,0:T(8,128)(2,1)} %refs_13_.1, ...), custom_call_target="tpu_custom_call" | custom-call | bytes 20971520 | tf_op jit(solution)/shard_map/pallas_call | solution.py:1022
  49.8 36.1 %shard_map.425 = (bf16[1280,2304]{1,0:T(8,128)(2,1)}, bf16[1280,768]{1,0:T(8,128)(2,1)}, f32[1280,768]{1,0:T(8,128)}, f32[1280,1]{1,0:T(8,128)}, bf16[2,4,192,76...) custom-call(s32[32]{0:T(128)} %broadcast_subtract_fusion.refs_0_.bound_ref, ...), custom_call_target="tpu_custom_call" | custom-call | flops 7549747200 | bytes 19660800 | tf_op jit(solution)/shard_map/pallas_call | solution.py:1022
  85.9 52.1 %shard_map.426 = (bf16[32,160,1536]{2,1,0:T(8,128)(2,1)}, bf16[1280,768]{1,0:T(8,128)(2,1)}, bf16[1280,768]{1,0:T(8,128)(2,1)}, f32[1280,768]{1,0:T(8,128)}, f32...) custom-call(bf16[32,160,1024]{2,1,0:T(8,128)(2,1)} %get-tuple-element.86.refs_0_.region_ref, ...), custom_call_target="tpu_custom_call" | custom-call | flops 16106127360 | bytes 26214400 | tf_op jit(solution)/shard_map/pallas_call | solution.py:1022
  138.0 45.2 %shard_map.427 = (bf16[1280,768]{1,0:T(8,128)(2,1)}, f32[64,1]{1,0:T(8,128)}, f32[64,384]{1,0:T(8,128)}, f32[1280,768]{1,0:T(8,128)}, bf16[768,768]{1,0:T(8,128)...) custom-call(s32[32]{0:T(128)} %broadcast_subtract_fusion.refs_0_.bou, ...), custom_call_target="tpu_custom_call" | custom-call | flops 30198988800 | bytes 19660800 | tf_op jit(solution)/shard_map/pallas_call | solution.py:1022
  183.2 0.0 all-reduce.3.cloned.1.call-update
  183.2 0.0 copy-start.2
  183.2 69.6 %shard_map.428 = (bf16[145,32,1024]{2,1,0:T(8,128)(2,1)}, f32[1280,768]{1,0:T(8,128)}, bf16[384,1024]{1,0:T(8,128)(2,1)}, bf16[384,768]{1,0:T(8,128)(2,1)}, f32[1,768]{1,0:T(1,128)}, /*index=5*/f32[1,768]{1,0:T(1,128)}) custom-call(s32[1]{0:T(128)} %bitcast.which_ref, bf16[32,160,1024]{2,1,0:T(8,128)(2,1)} %get-tuple-element.86.refs_0_.region_ref, ...), custom_call_target="tpu_custom_call" | custom-call | flops 24159191040 | bytes 36700160 | tf_op jit(solution)/shard_map/pallas_call | solution.py:1022
  252.8 0.0 copy-done.2
  252.8 0.1 reduce
  252.9 0.1 reshape.86
  253.0 0.6 copy.56
  253.7 67.6 %shard_map.429 = (f32[1280,768]{1,0:T(8,128)}, bf16[768,768]{1,0:T(8,128)(2,1)}, bf16[384,1024]{1,0:T(8,128)(2,1)}, bf16[384,768]{1,0:T(8,128)(2,1)}, bf16[128,7...) custom-call(s32[32]{0:T(128)} %broadcast_subtract_fusion.refs_0_.bound_ref, ...), custom_call_target="tpu_custom_call" | custom-call | flops 7549747200 | bytes 19660800 | tf_op jit(solution)/shard_map/pallas_call | solution.py:1022
  321.2 0.0 all-reduce.3.cloned.1.call-done
  321.3 0.0 copy-start
  321.3 7.2 %shard_map.430 = (f32[192,768]{1,0:T(8,128)}, f32[192,768]{1,0:T(8,128)}, f32[192,768]{1,0:T(8,128)}, f32[192,768]{1,0:T(8,128)}, f32[192,768]{1,0:T(8,128)}, /*...) custom-call(bf16[768,768]{1,0:T(8,128)(2,1)} %get-tuple-element.121., ...), custom_call_target="tpu_custom_call" | custom-call | bytes 11796480 | tf_op jit(solution)/shard_map/pallas_call | solution.py:1022
  328.5 1.9 copy.69
  330.4 0.7 copy.70
  (4 shorter events, 0.0 us)
Async XLA Ops:
  7.2 9.2 %copy-start.3 = (s32[32,2]{0,1:T(2,128)S(1)}, s32[32,2]{0,1:T(2,128)}, u32[]{:S(2)}) copy-start(s32[32,2]{0,1:T(2,128)} %param.29) | copy-start | bytes 772
  7.2 314.1 %all-reduce.3.cloned.1.call-start = ((), (), s32[]{:S(2)}) async-start(), calls=%async_computation | async-start | bytes 5505024 | tf_op jit(solution)/shard_map/psum | solution.py:1387
  183.2 69.6 %copy-start.2 = (f32[64,1]{1,0:T(8,128)S(1)}, f32[64,1]{1,0:T(8,128)}, u32[]{:S(2)}) copy-start(f32[64,1]{1,0:T(8,128)} %get-tuple-element.97) | copy-start | bytes 772
  321.3 7.2 %copy-start = (f32[1280,768]{1,0:T(8,128)S(1)}, f32[1280,768]{1,0:T(8,128)}, u32[]{:S(2)}) copy-start(f32[1280,768]{1,0:T(8,128)} %get-tuple-element.225) | copy-start | bytes 11796484
  328.5 1.9 copy-start.1
Sparse Core Ops, SparseCore 0:
  183.3 64.9 all-reduce.2
